TPU v7x, 128 devices: a whole 4x4x4 slice. The times are simulated.
128 devices in a mesh: ctx: 16 (over x, z), head: 8 (over y, core).
Axes of the slice: x: 4, y: 4, z: 4, core: 2. Of those that a mesh axis runs over, the one named last changes fastest.
Arguments:
- tokens: bfloat16 [16384, 7168], P(('ctx', 'head')), may hold values from -6 to 6
- routes: int32 [16384, 8], P(('ctx', 'head')), may hold values from 0 to 255, all different within a row; in each aligned block of 128 rows (0 to 127, 128 to 255, ...) at most 6 rows name the same one
- route_weight: float32 [16384, 8], P(('ctx', 'head')), may hold values from 0.2 to 2
- w_gate: bfloat16 [16, 7168, 1024], P('ctx', 'head'), may hold values from -0.0625 to 0.0625
- w_up: bfloat16 [16, 7168, 1024], P('ctx', 'head'), may hold values from -0.0625 to 0.0625
- w_down: bfloat16 [16, 1024, 7168], P('ctx', None, 'head'), may hold values from -0.1875 to 0.1875
- grad_out: bfloat16 [16384, 7168], P(('ctx', 'head')), may hold values from -6 to 6
Outputs:
- moe_out: bfloat16 [16384, 7168], P(('ctx', 'head'))
- grad_tokens: bfloat16 [16384, 7168], P(('ctx', 'head'))
- grad_route: float32 [16384, 8], P(('ctx', 'head'))
- grad_gate: bfloat16 [16, 7168, 1024], P('ctx', 'head')
- grad_up: bfloat16 [16, 7168, 1024], P('ctx', 'head')
- grad_down: bfloat16 [16, 1024, 7168], P('ctx', None, 'head')
Inputs may be any that keep to these rules, and one draw needn't show every extreme that they name: `routes`: each row names 8 different experts. In each aligned block of 128 rows (the tokens of one device) no expert is named more than 6 times. Experts below 16 are the window's.
All inputs are finite; a program needn't handle non-finite values.
Results may differ from a plain program's by a relative error of at most 0.0057.
Values may be sent and summed in bfloat16 or wider, within the bound.
No kernel may reach another device: no remote copies, remote signals or barrier semaphores. Data moves between devices by JAX's collectives and lax.ppermute only.
A program may use at most 128 MiB of HBM per device.

v0:
```python
import jax
import jax.numpy as jnp
from jax import lax
from jax.sharding import PartitionSpec as P

CAP = 6


def silu_parts(gate_pre):
    sigmoid_g = jax.nn.sigmoid(gate_pre)
    return (gate_pre * sigmoid_g, sigmoid_g * (1.0 + gate_pre * (1.0 - sigmoid_g)))


def activate(summed, hidden_width):
    gate_pre = summed[:, :hidden_width]
    up_value = summed[:, hidden_width : 2 * hidden_width]
    back_grad = summed[:, 2 * hidden_width :]
    smooth, silu_slope = silu_parts(gate_pre)
    hidden = (smooth * up_value).astype(jnp.bfloat16)
    d_gate = (back_grad * up_value * silu_slope).astype(jnp.bfloat16)
    d_up = (back_grad * smooth).astype(jnp.bfloat16)
    return jnp.concatenate([hidden, d_gate, d_up], axis=1)


def on_device(tokens, routes, route_weight, w_gate, w_up, w_down, grad_out):
    experts = lax.axis_size("ctx")
    groups = lax.axis_size("head")
    tok_rows, model_width = tokens.shape
    pick_count = routes.shape[1]
    slice_width = w_gate.shape[1]
    hidden_width = w_gate.shape[2]
    slot_count = experts * CAP
    flat_routes = routes.reshape(-1)
    onehot = (flat_routes[:, None] == jnp.arange(experts, dtype=jnp.int32)[None, :]).astype(
        jnp.int32
    )
    before = jnp.sum((jnp.cumsum(onehot, axis=0) - onehot) * onehot, axis=1)
    slot_of = jnp.where(flat_routes < experts, flat_routes * CAP + before, -1)
    placed = (slot_of[:, None] == jnp.arange(slot_count, dtype=jnp.int32)[None, :]).astype(
        jnp.float32
    )
    placed_picks = placed.reshape(tok_rows, pick_count, slot_count)
    selector = jnp.sum(placed_picks, axis=1)
    weighted_sel = jnp.sum(placed_picks * route_weight[:, :, None], axis=1)
    slot_weight = jnp.sum(weighted_sel, axis=0)
    stacked = jnp.concatenate([tokens, grad_out], axis=1)
    slot_values = jnp.dot(
        selector.T.astype(jnp.bfloat16), stacked, preferred_element_type=jnp.float32
    )
    x_rows = slot_values[:, :model_width].astype(jnp.bfloat16)
    dy_rows = slot_values[:, model_width:]
    do_rows = (slot_weight[:, None] * dy_rows).astype(jnp.bfloat16)

    def to_slices(block):
        return block.reshape(experts, CAP, groups, slice_width).transpose(0, 2, 1, 3)

    def to_tokens(block):
        return (
            block.reshape(experts, groups, CAP, slice_width)
            .transpose(0, 2, 1, 3)
            .reshape(slot_count, model_width)
        )

    total_rows = experts * groups * CAP
    x_in, d_in = (
        lax.all_to_all(
            to_slices(x_rows).reshape(experts * groups, CAP, slice_width),
            ("ctx", "head"),
            split_axis=0,
            concat_axis=0,
            tiled=True,
        ),
        lax.all_to_all(
            to_slices(do_rows).reshape(experts * groups, CAP, slice_width),
            ("ctx", "head"),
            split_axis=0,
            concat_axis=0,
            tiled=True,
        ),
    )
    x_in = x_in.reshape(total_rows, slice_width)
    d_in = d_in.reshape(total_rows, slice_width)
    gate_slice = w_gate[0]
    up_slice = w_up[0]
    down_slice = w_down[0]
    w_pair = jnp.concatenate([gate_slice, up_slice], axis=1)
    forward = jnp.dot(x_in, w_pair, preferred_element_type=jnp.float32)
    backward = lax.dot_general(
        d_in, down_slice, (((1,), (1,)), ((), ())), preferred_element_type=jnp.float32
    )
    row_share = lax.psum_scatter(
        jnp.concatenate([forward, backward], axis=1), "head", scatter_dimension=0, tiled=True
    )
    packed = lax.all_gather(activate(row_share, hidden_width), "head", axis=0, tiled=True)
    hidden = packed[:, :hidden_width]
    grads_hidden = packed[:, hidden_width:]
    expert_out = jnp.dot(hidden, down_slice, preferred_element_type=jnp.float32).astype(
        jnp.bfloat16
    )
    grad_down = lax.dot_general(
        hidden, d_in, (((0,), (0,)), ((), ())), preferred_element_type=jnp.float32
    ).astype(jnp.bfloat16)
    grad_pair = lax.dot_general(
        x_in, grads_hidden, (((0,), (0,)), ((), ())), preferred_element_type=jnp.float32
    )
    grad_gate = grad_pair[:, :hidden_width].astype(jnp.bfloat16)
    grad_up = grad_pair[:, hidden_width:].astype(jnp.bfloat16)
    grad_rows = lax.dot_general(
        grads_hidden, w_pair, (((1,), (1,)), ((), ())), preferred_element_type=jnp.float32
    ).astype(jnp.bfloat16)
    back_out, back_grad = (
        lax.all_to_all(
            expert_out.reshape(experts * groups, CAP, slice_width),
            ("ctx", "head"),
            split_axis=0,
            concat_axis=0,
            tiled=True,
        ),
        lax.all_to_all(
            grad_rows.reshape(experts * groups, CAP, slice_width),
            ("ctx", "head"),
            split_axis=0,
            concat_axis=0,
            tiled=True,
        ),
    )
    out_slots = to_tokens(back_out).astype(jnp.float32)
    grad_slots = to_tokens(back_grad)
    moe_out = jnp.dot(
        weighted_sel, out_slots, precision=lax.Precision.HIGHEST, preferred_element_type=jnp.float32
    ).astype(jnp.bfloat16)
    grad_tokens = jnp.dot(
        selector.astype(jnp.bfloat16), grad_slots, preferred_element_type=jnp.float32
    ).astype(jnp.bfloat16)
    slot_inner = jnp.sum(dy_rows * out_slots, axis=1)
    grad_route = jnp.dot(
        placed, slot_inner, precision=lax.Precision.HIGHEST, preferred_element_type=jnp.float32
    ).reshape(tok_rows, pick_count)
    return (moe_out, grad_tokens, grad_route, grad_gate[None], grad_up[None], grad_down[None])


def solution(mesh):
    return jax.shard_map(
        on_device,
        mesh=mesh,
        in_specs=(
            P(("ctx", "head"), None),
            P(("ctx", "head"), None),
            P(("ctx", "head"), None),
            P("ctx", "head", None),
            P("ctx", "head", None),
            P("ctx", None, "head"),
            P(("ctx", "head"), None),
        ),
        out_specs=(
            P(("ctx", "head"), None),
            P(("ctx", "head"), None),
            P(("ctx", "head"), None),
            P("ctx", "head", None),
            P("ctx", "head", None),
            P("ctx", None, "head"),
        ),
        check_vma=False,
    )
```

profile of v0, /device:TPU:0, one launch (start us, length us, event | category | flops | bytes accessed | tf_op | source)
XLA Modules:
  0.0 299.2 jit_solution(10918729008019234311)
XLA Ops:
  7.2 0.9 copy.65
  8.3 4.5 %reduce-window.6 = s32[16,8,128]{2,1,0:T(8,128)S(1)} reduce-window(s32[16,8,128]{2,1,0:T(8,128)S(1)} %fusion.28, s32[]{:T(128)} %constant.5.clone.1), window={size=1x1x128 pad=0_0x0_0x127_0}, to_apply=%region_0.0 | reduce-window | flops 2080768 | bytes 131076 | tf_op jit(solution)/shard_map/reduce-window
  12.9 0.1 copy.67
  13.4 0.7 add_select_fusion
  14.1 0.9 select_reduce_fusion
  15.0 2.9 fusion
  17.9 2.3 copy-done.1
  20.3 0.3 multiply_convert_fusion
  20.5 0.2 copy.81
  20.8 0.2 copy.87
  20.9 2.0 copy.73
  23.0 11.6 %all-to-all-start.1 = ((bf16[128,6,896]{2,1,0:T(8,128)(2,1)}), bf16[128,6,896]{2,1,0:T(8,128)(2,1)}, u32[]{:S(2)}, u32[]{:S(2)}) async-start(bf16[128,6,896]{2,1,0:T(8,128)(2,1)} %copy.73), calls=%async_computation.1 | async-start | bytes 3670016 | tf_op jit(solution)/shard_map/all_to_all | solution.py:73
  34.6 1.9 slice.83
  36.5 0.2 copy.80
  36.7 0.2 copy.88
  36.9 2.0 copy.71
  38.9 22.9 %all-to-all-done.1 = bf16[128,6,896]{2,1,0:T(8,128)(2,1)} async-done(((bf16[128,6,896]{2,1,0:T(8,128)(2,1)}), bf16[128,6,896]{2,1,0:T(8,128)(2,1)}, u32[]{:S(2)}, u32[]{:S(2)}) %all-to-all-start.1) | async-done | bytes 1376288 | tf_op jit(solution)/shard_map/all_to_all | solution.py:73
  61.8 5.7 %all-to-all-start = ((bf16[128,6,896]{2,1,0:T(8,128)(2,1)}), bf16[128,6,896]{2,1,0:T(8,128)(2,1)}, u32[]{:S(2)}, u32[]{:S(2)}) async-start(bf16[128,6,896]{2,1,0:T(8,128)(2,1)} %copy.71), calls=%async_computation | async-start | bytes 3670016 | tf_op jit(solution)/shard_map/all_to_all | solution.py:66
  67.6 2.5 reshape.105
  70.1 3.5 %fusion.10 = f32[768,1024]{1,0:T(8,128)} fusion(bf16[768,896]{1,0:T(8,128)(2,1)S(1)} %reshape.105, bf16[1,1024,896]{2,1,0:T(8,128)(2,1)S(1)} %copy-done), kind=kOutput, calls=%fused_computation.20 | convolution fusion | flops 1409286144 | bytes 6356992 | tf_op jit(solution)/shard_map/dot_general | solution.py:88
  73.6 21.2 %all-to-all-done = bf16[128,6,896]{2,1,0:T(8,128)(2,1)} async-done(((bf16[128,6,896]{2,1,0:T(8,128)(2,1)}), bf16[128,6,896]{2,1,0:T(8,128)(2,1)}, u32[]{:S(2)}, u32[]{:S(2)}) %all-to-all-start) | async-done | bytes 1376288 | tf_op jit(solution)/shard_map/all_to_all | solution.py:66
  94.8 3.6 %reshape.102 = bf16[768,896]{1,0:T(8,128)(2,1)} reshape(bf16[128,6,896]{2,1,0:T(8,128)(2,1)} %all-to-all-done) | data formatting | bytes 2752512 | tf_op jit(solution)/shard_map/reshape | solution.py:81
  98.3 8.7 %fusion.7 = f32[768,2048]{1,0:T(8,128)} fusion(bf16[768,896]{1,0:T(8,128)(2,1)} %reshape.102, bf16[896,1024]{1,0:T(8,128)(2,1)} %bitcast.88, bf16[896,1024]{1,0:T(8,128)(2,1)} %bitcast.90), kind=kOutput, calls=%fused_computation.15 | convolution fusion | flops 2825912320 | bytes 11337728 | tf_op jit(solution)/shard_map/dot_general | solution.py:87
  107.1 7.4 %pad_maximum_fusion = f32[768,3072]{1,0:T(8,128)} fusion(f32[768,1024]{1,0:T(8,128)S(1)} %copy-done.2, f32[768,2048]{1,0:T(8,128)} %fusion.7), kind=kLoop, calls=%fused_computation | loop fusion | flops 2359296 | bytes 18874368 | tf_op jit(solution)/shard_map/concatenate | solution.py:92
  114.5 0.2 all-gather.2.cloned.1.call-start
  114.7 53.1 %reduce-scatter.2.cloned.1.call-done = f32[96,3072]{1,0:T(8,128)} async-done(((f32[768,3072]{1,0:T(8,128)}), f32[96,3072]{1,0:T(8,128)}) %reduce-scatter.2.cloned.1.call-update) | async-done | bytes 1179664 | tf_op jit(solution)/shard_map/reduce_scatter | solution.py:91
  167.8 1.5 multiply_convert_fusion.3
  169.3 0.9 pad_maximum_fusion.6
  170.2 34.1 %all-gather.2.cloned.1.call-done = bf16[768,3072]{1,0:T(8,128)(2,1)} async-done(((bf16[96,3072]{1,0:T(8,128)(2,1)}), bf16[768,3072]{1,0:T(8,128)(2,1)}) %all-gather.2.cloned.1.call-update) | async-done | bytes 4718608 | tf_op jit(solution)/shard_map/all_gather | solution.py:94
  204.3 7.5 %fusion.12 = bf16[768,896]{1,0:T(8,128)(2,1)} fusion(bf16[896,1024]{1,0:T(8,128)(2,1)} %bitcast.89, bf16[896,1024]{1,0:T(8,128)(2,1)} %bitcast.91, bf16[768,3072]{1,0:T(8,128)(2,1)} %all-gather.2.cloned.1.call-done), kind=kOutput, calls=%fused_computation.23 | convolution fusion | flops 2826600448 | bytes 8192000 | tf_op jit(solution)/shard_map/dot_general | solution.py:108
  211.8 3.5 %reshape.109 = bf16[128,6,896]{2,1,0:T(8,128)(2,1)} reshape(bf16[768,896]{1,0:T(8,128)(2,1)} %fusion.12) | data formatting | bytes 2752512 | tf_op jit(solution)/shard_map/reshape | solution.py:120
  215.2 9.1 %all-to-all-start.3 = ((bf16[128,6,896]{2,1,0:T(8,128)(2,1)}), bf16[128,6,896]{2,1,0:T(8,128)(2,1)}, u32[]{:S(2)}, u32[]{:S(2)}) async-start(bf16[128,6,896]{2,1,0:T(8,128)(2,1)} %reshape.109), calls=%async_computation.4 | async-start | bytes 3670016 | tf_op jit(solution)/shard_map/all_to_all | solution.py:119
  224.4 4.3 %fusion.15 = bf16[768,896]{1,0:T(8,128)(2,1)} fusion(bf16[1,1024,896]{2,1,0:T(8,128)(2,1)S(1)} %copy-done, bf16[768,3072]{1,0:T(8,128)(2,1)} %all-gather.2.cloned.1.call-done), kind=kOutput, calls=%fused_computation.24 | convolution fusion | flops 1409974272 | bytes 4784128 | tf_op jit(solution)/shard_map/dot_general | solution.py:97
  228.6 3.5 %reshape.106 = bf16[128,6,896]{2,1,0:T(8,128)(2,1)} reshape(bf16[768,896]{1,0:T(8,128)(2,1)} %fusion.15) | data formatting | bytes 2752512 | tf_op jit(solution)/shard_map/reshape | solution.py:113
  232.1 19.5 %all-to-all-done.3 = bf16[128,6,896]{2,1,0:T(8,128)(2,1)} async-done(((bf16[128,6,896]{2,1,0:T(8,128)(2,1)}), bf16[128,6,896]{2,1,0:T(8,128)(2,1)}, u32[]{:S(2)}, u32[]{:S(2)}) %all-to-all-start.3) | async-done | bytes 1376288 | tf_op jit(solution)/shard_map/all_to_all | solution.py:119
  251.6 5.9 %all-to-all-start.2 = ((bf16[128,6,896]{2,1,0:T(8,128)(2,1)}), bf16[128,6,896]{2,1,0:T(8,128)(2,1)}, u32[]{:S(2)}, u32[]{:S(2)}) async-start(bf16[128,6,896]{2,1,0:T(8,128)(2,1)} %reshape.106), calls=%async_computation.3 | async-start | bytes 3670016 | tf_op jit(solution)/shard_map/all_to_all | solution.py:112
  257.6 5.4 %convolution_convert_fusion.2 = bf16[896,2048]{1,0:T(8,128)(2,1)S(1)} fusion(bf16[768,896]{1,0:T(8,128)(2,1)} %reshape.102, bf16[768,3072]{1,0:T(8,128)(2,1)} %all-gather.2.cloned.1.call-done), kind=kOutput, calls=%fused_computation.8 | convolution fusion | flops 2820407296 | bytes 8192000 | tf_op jit(solution)/shard_map/dot_general | solution.py:103
  262.9 2.3 slice_bitcast_fusion
  265.2 4.5 %convert_bitcast_fusion = bf16[1,1024,896]{2,1,0:T(8,128)(2,1)} fusion(bf16[768,896]{1,0:T(8,128)(2,1)S(1)} %reshape.105, bf16[768,3072]{1,0:T(8,128)(2,1)} %all-gather.2.cloned.1.call-done), kind=kOutput, calls=%fused_computation.22 | convolution fusion | flops 1410203648 | bytes 4784128 | tf_op jit(solution)/shard_map/dot_general | solution.py:100
  269.7 1.7 copy.76
  271.4 0.2 copy.83
  271.6 1.9 convolution_convert_fusion
  273.5 11.1 %all-to-all-done.2 = bf16[128,6,896]{2,1,0:T(8,128)(2,1)} async-done(((bf16[128,6,896]{2,1,0:T(8,128)(2,1)}), bf16[128,6,896]{2,1,0:T(8,128)(2,1)}, u32[]{:S(2)}, u32[]{:S(2)}) %all-to-all-start.2) | async-done | bytes 1376288 | tf_op jit(solution)/shard_map/all_to_all | solution.py:112
  284.6 1.7 copy.75
  286.2 0.2 copy.82
  286.5 2.2 multiply_reduce_fusion
  288.7 0.8 fusion.22
  289.5 2.9 convolution_convert_fusion.1
  (19 shorter events, 0.7 us)
Async XLA Ops:
  7.2 62.9 %copy-start = (bf16[1,1024,896]{2,1,0:T(8,128)(2,1)S(1)}, bf16[1,1024,896]{2,1,0:T(8,128)(2,1)}, u32[]{:S(2)}) copy-start(bf16[1,1024,896]{2,1,0:T(8,128)(2,1)} %param.12) | copy-start | bytes 5505028
  17.9 2.3 copy-start.1
  23.0 38.9 %all-to-all-start.1 = ((bf16[128,6,896]{2,1,0:T(8,128)(2,1)}), bf16[128,6,896]{2,1,0:T(8,128)(2,1)}, u32[]{:S(2)}, u32[]{:S(2)}) async-start(bf16[128,6,896]{2,1,0:T(8,128)(2,1)} %copy.73), calls=%async_computation.1 | async-start | bytes 3670016 | tf_op jit(solution)/shard_map/all_to_all | solution.py:73
  61.8 33.0 %all-to-all-start = ((bf16[128,6,896]{2,1,0:T(8,128)(2,1)}), bf16[128,6,896]{2,1,0:T(8,128)(2,1)}, u32[]{:S(2)}, u32[]{:S(2)}) async-start(bf16[128,6,896]{2,1,0:T(8,128)(2,1)} %copy.71), calls=%async_computation | async-start | bytes 3670016 | tf_op jit(solution)/shard_map/all_to_all | solution.py:66
  67.5 100.3 %reduce-scatter.2.cloned.1.call-start = ((), (), s32[]{:S(2)}) async-start(), calls=%async_computation.5 | async-start | bytes 10616832 | tf_op jit(solution)/shard_map/reduce_scatter | solution.py:91
  98.3 8.7 %copy-start.2 = (f32[768,1024]{1,0:T(8,128)S(1)}, f32[768,1024]{1,0:T(8,128)}, u32[]{:S(2)}) copy-start(f32[768,1024]{1,0:T(8,128)} %fusion.10) | copy-start | bytes 9437188
  114.5 89.8 %all-gather.2.cloned.1.call-start = ((), (), s32[]{:S(2)}) async-start(), calls=%async_computation.6 | async-start | bytes 5308416 | tf_op jit(solution)/shard_map/all_gather | solution.py:94
  215.2 36.4 %all-to-all-start.3 = ((bf16[128,6,896]{2,1,0:T(8,128)(2,1)}), bf16[128,6,896]{2,1,0:T(8,128)(2,1)}, u32[]{:S(2)}, u32[]{:S(2)}) async-start(bf16[128,6,896]{2,1,0:T(8,128)(2,1)} %reshape.109), calls=%async_computation.4 | async-start | bytes 3670016 | tf_op jit(solution)/shard_map/all_to_all | solution.py:119
  251.6 33.0 %all-to-all-start.2 = ((bf16[128,6,896]{2,1,0:T(8,128)(2,1)}), bf16[128,6,896]{2,1,0:T(8,128)(2,1)}, u32[]{:S(2)}, u32[]{:S(2)}) async-start(bf16[128,6,896]{2,1,0:T(8,128)(2,1)} %reshape.106), calls=%async_computation.3 | async-start | bytes 3670016 | tf_op jit(solution)/shard_map/all_to_all | solution.py:112
Sparse Core Ops, SparseCore 0:
  114.6 53.1 reduce-scatter.1
  170.3 33.9 all-gather.1
where the time goes:
time: 300 us; the launch traced here: 299 us
  waiting for transfers between devices  162 us (54%)
  matrix products  42.3 us (14%)
  starting transfers between devices  32.6 us (11%)
  local copies, waits for them, and re-layouts  29.7 us (10%)
  other arithmetic  18.5 us (6%)
  between operations  14.3 us (5%)
    reduce_scatter x1, waiting for transfers between devices, on_device(): lax.psum_scatter(jnp.concatenate([forward, backward], axis=1), 'head', sc...  53.1 us
    all_gather x1, waiting for transfers between devices, on_device(): lax.all_gather(activate(row_share, hidden_width), 'head', axis=0, tiled=T...  34.1 us
    all_to_all x1, waiting for transfers between devices, on_device(): lax.all_to_all(to_slices(do_rows).reshape(experts * groups, CAP, slice_wi...  22.9 us
    all_to_all x1, waiting for transfers between devices, on_device(): lax.all_to_all(to_slices(x_rows).reshape(experts * groups, CAP, slice_wid...  21.2 us
    all_to_all x1, waiting for transfers between devices, on_device(): lax.all_to_all(grad_rows.reshape(experts * groups, CAP, slice_width), ('c...  19.5 us
    all_to_all x1, starting transfers between devices, on_device(): lax.all_to_all(to_slices(do_rows).reshape(experts * groups, CAP, slice_wi...  11.6 us
    all_to_all x1, waiting for transfers between devices, on_device(): lax.all_to_all(expert_out.reshape(experts * groups, CAP, slice_width), ('...  11.1 us
    all_to_all x1, starting transfers between devices, on_device(): lax.all_to_all(grad_rows.reshape(experts * groups, CAP, slice_width), ('c...  9.12 us
  transfers between devices with their start and end apart: 6, of which 6 were waited for; matrix products, arithmetic and copies ran while one was open for 11% of the time, Pallas kernels for 0%

commit v1 on v0

v1 whole, which is shorter than its diff:
```python
import functools

import jax
import jax.numpy as jnp
from jax import lax
from jax.experimental import pallas as pl
from jax.experimental.pallas import tpu as pltpu
from jax.sharding import Mesh, PartitionSpec as P

CAP = 6
PAD = 8
BF16 = jnp.bfloat16
F32 = jnp.float32
VMEM_LIMIT = 56 * 1024 * 1024


def dot(a, b, ca=1, cb=0):
    return lax.dot_general(a, b, (((ca,), (cb,)), ((), ())), preferred_element_type=F32)


def whole():
    return pl.BlockSpec(memory_space=pltpu.VMEM)


def smem():
    return pl.BlockSpec(memory_space=pltpu.SMEM)


def tail_slot(row, q):
    return jnp.where(row == 6, q, jnp.where(row == 7, 3 + q, -1))


def main_slot(row):
    return jnp.where(row < CAP, row, -1)


def prep_kernel(core_ref, routes_ref, weight_ref, tok_ref, go_ref, out_ref, sel_ref, wsel_ref, selt_s, scale_s):
    rows = routes_ref.shape[0]
    lanes = sel_ref.shape[2]
    half = tok_ref.shape[1] // 2

    @pl.when(pl.program_id(0) == 0)
    def _():
        lane = lax.broadcasted_iota(jnp.int32, (rows, lanes), 1)
        expert, row = lane >> 3, lane & 7
        named = jnp.zeros((rows, lanes), F32)
        weight = jnp.zeros((rows, lanes), F32)
        for k in range(routes_ref.shape[1]):
            hit = routes_ref[:, k : k + 1] == expert
            named = named + jnp.where(hit, 1.0, 0.0)
            weight = weight + jnp.where(hit, weight_ref[:, k : k + 1], 0.0)
        earlier = lax.broadcasted_iota(jnp.int32, (rows, rows), 1) < lax.broadcasted_iota(jnp.int32, (rows, rows), 0)
        before = dot(jnp.where(earlier, 1.0, 0.0).astype(BF16), named.astype(BF16))
        picked = []
        for want in [main_slot(row)] + [tail_slot(row, q) for q in range(3)]:
            picked.append(jnp.where((named > 0.5) & (before == want.astype(F32)), 1.0, 0.0))
        slot_row = lax.broadcasted_iota(jnp.int32, (lanes, 1), 0) & 7
        scales = []
        for i, one in enumerate(picked):
            sel_ref[i] = one.astype(BF16)
            selt_s[i] = one.T.astype(BF16)
            scales.append(jnp.sum((one * weight).T, axis=1, keepdims=True))
        plain = jnp.where(slot_row < CAP, 1.0, 0.0)
        scale_s[0] = plain + scales[1]
        scale_s[1] = plain + scales[2]
        scale_s[2] = scales[0] + scales[3]
        wsel = picked[0] * weight
        high = wsel.astype(BF16)
        wsel_ref[0] = high
        wsel_ref[1] = (wsel - high.astype(F32)).astype(BF16)

    own = pl.multiple_of(core_ref[0] * half, 128)
    other = pl.multiple_of((1 - core_ref[0]) * half, 128)
    tail = go_ref[:, pl.ds(other, half)]
    sources = (tok_ref[:, pl.ds(own, half)], tok_ref[:, pl.ds(other, half)], go_ref[:, pl.ds(own, half)])
    for q, source in enumerate(sources):
        rows_q = dot(selt_s[0], source) + dot(selt_s[1 + q], tail)
        out_ref[0, :, q * half : (q + 1) * half] = (scale_s[q] * rows_q).astype(BF16)


def prep(core, routes, route_weight, tokens, grad_out, quarters, experts):
    rows, width = tokens.shape
    lanes = experts * PAD
    quarter = width // quarters
    half = quarter // 2
    column = pl.BlockSpec((rows, quarter), lambda i: (0, i))
    return pl.pallas_call(
        prep_kernel,
        grid=(quarters,),
        in_specs=[smem(), whole(), whole(), column, column],
        out_specs=[
            pl.BlockSpec((1, lanes, 3 * half), lambda i: (i, 0, 0)),
            pl.BlockSpec((4, rows, lanes), lambda i: (0, 0, 0)),
            pl.BlockSpec((2, rows, lanes), lambda i: (0, 0, 0)),
        ],
        out_shape=[
            jax.ShapeDtypeStruct((quarters, lanes, 3 * half), BF16),
            jax.ShapeDtypeStruct((4, rows, lanes), BF16),
            jax.ShapeDtypeStruct((2, rows, lanes), BF16),
        ],
        scratch_shapes=[pltpu.VMEM((4, lanes, rows), BF16), pltpu.VMEM((3, lanes, 1), F32)],
        compiler_params=pltpu.CompilerParams(vmem_limit_bytes=VMEM_LIMIT),
        cost_estimate=pl.CostEstimate(flops=800_000_000, bytes_accessed=6_500_000, transcendentals=0),
        name="prep",
    )(core, routes, route_weight, tokens, grad_out)


def slot_masks(slots, lanes, transposed=False):
    shape = (lanes, slots) if transposed else (slots, lanes)
    slot_dim, lane_dim = (1, 0) if transposed else (0, 1)
    slot = lax.broadcasted_iota(jnp.int32, shape, slot_dim)
    lane = lax.broadcasted_iota(jnp.int32, shape, lane_dim)
    expert = (slot * 43) >> 8
    place = slot - expert * CAP
    row = lane & 7
    same = (lane >> 3) == expert
    wants = [main_slot(row)] + [tail_slot(row, q) for q in range(3)]
    return [jnp.where(same & (place == want), 1.0, 0.0).astype(BF16) for want in wants]


def first_kernel(at_ref, recv_ref, go_ref, gx_ref, uo_ref, ux_ref, do_ref, dx_ref, p0_ref, p1_ref, p2_ref, p3_ref, own_ref, other_ref):
    quarters, lanes, packed = recv_ref.shape
    half = packed // 3
    slots = p0_ref.shape[1]

    @pl.when(pl.program_id(0) == 0)
    def _():
        masks = slot_masks(slots, lanes)
        for j in range(quarters):
            source = lax.rem(at_ref[0] + j, quarters)
            rows = pl.ds(j * slots, slots)
            block = [recv_ref[source, :, q * half : (q + 1) * half] for q in range(3)]
            own_ref[0, rows, :] = dot(masks[0], block[0]).astype(BF16)
            other_ref[0, rows, :] = dot(masks[0], block[1]).astype(BF16)
            own_ref[1, rows, :] = dot(masks[0], block[2]).astype(BF16)
            tail = dot(masks[1], block[0]) + dot(masks[2], block[1]) + dot(masks[3], block[2])
            other_ref[1, rows, :] = tail.astype(BF16)

    gate = dot(own_ref[0], go_ref[...]) + dot(other_ref[0], gx_ref[...])
    up = dot(own_ref[0], uo_ref[...]) + dot(other_ref[0], ux_ref[...])
    back = dot(own_ref[1], do_ref[...], 1, 1) + dot(other_ref[1], dx_ref[...], 1, 1)
    for i, value in enumerate((gate, up, back)):
        p0_ref[i] = value[0:slots]
        p1_ref[i] = value[slots : 2 * slots].astype(BF16)
        p2_ref[i] = value[2 * slots : 3 * slots].astype(BF16)
        p3_ref[i] = value[3 * slots :].astype(BF16)


def first(at, recv, weights, hidden, slots):
    quarters, lanes, packed = recv.shape
    half = packed // 3
    step = 256
    up_spec = pl.BlockSpec((half, step), lambda n: (0, n))
    down_spec = pl.BlockSpec((step, half), lambda n: (n, 0))
    part = pl.BlockSpec((3, slots, step), lambda n: (0, 0, n))
    kept = pl.BlockSpec((2, quarters * slots, half), lambda n: (0, 0, 0))
    return pl.pallas_call(
        first_kernel,
        grid=(hidden // step,),
        in_specs=[smem(), whole()] + [up_spec] * 4 + [down_spec] * 2,
        out_specs=[part] * 4 + [kept] * 2,
        out_shape=[jax.ShapeDtypeStruct((3, slots, hidden), F32)]
        + [jax.ShapeDtypeStruct((3, slots, hidden), BF16)] * 3
        + [jax.ShapeDtypeStruct((2, quarters * slots, half), BF16)] * 2,
        compiler_params=pltpu.CompilerParams(vmem_limit_bytes=VMEM_LIMIT),
        cost_estimate=pl.CostEstimate(flops=6_000_000_000, bytes_accessed=20_000_000, transcendentals=0),
        name="first",
    )(at, recv, *weights)


def activate(p0, others):
    total = p0
    for one in others:
        total = total + one.astype(F32)
    gate, up, back = total[0], total[1], total[2]
    sig = jax.nn.sigmoid(gate)
    smooth = gate * sig
    slope = sig * (1.0 + gate * (1.0 - sig))
    return jnp.stack([(smooth * up).astype(BF16), (back * up * slope).astype(BF16), (back * smooth).astype(BF16)])


def second_kernel(at_ref, h0_ref, h1_ref, h2_ref, h3_ref, do_ref, dx_ref, go_ref, gx_ref, uo_ref, ux_ref, out_ref, all_s):
    quarters, lanes, packed = out_ref.shape
    half = packed // 3
    slots = h0_ref.shape[1]
    for j, h_ref in enumerate((h0_ref, h1_ref, h2_ref, h3_ref)):
        for i in range(3):
            all_s[i, j * slots : (j + 1) * slots, :] = h_ref[i]
    masks = slot_masks(slots, lanes, True)
    a_own = dot(all_s[0], do_ref[...]).astype(BF16)
    a_other = dot(all_s[0], dx_ref[...]).astype(BF16)
    b_own = (dot(all_s[1], go_ref[...], 1, 1) + dot(all_s[2], uo_ref[...], 1, 1)).astype(BF16)
    b_other = (dot(all_s[1], gx_ref[...], 1, 1) + dot(all_s[2], ux_ref[...], 1, 1)).astype(BF16)
    for j in range(quarters):
        target = lax.rem(at_ref[0] + j, quarters)
        rows = slice(j * slots, (j + 1) * slots)
        for q, value in enumerate((a_own, a_other, b_own)):
            packed_rows = dot(masks[0], value[rows]) + dot(masks[1 + q], b_other[rows])
            out_ref[target, :, q * half : (q + 1) * half] = packed_rows.astype(BF16)


def second(at, parts, weights, lanes):
    quarters = len(parts)
    _, slots, hidden = parts[0].shape
    half = weights[0].shape[1]
    return pl.pallas_call(
        second_kernel,
        in_specs=[smem()] + [whole()] * 10,
        out_specs=whole(),
        out_shape=jax.ShapeDtypeStruct((quarters, lanes, 3 * half), BF16),
        scratch_shapes=[pltpu.VMEM((3, quarters * slots, hidden), BF16)],
        compiler_params=pltpu.CompilerParams(vmem_limit_bytes=VMEM_LIMIT),
        cost_estimate=pl.CostEstimate(flops=5_000_000_000, bytes_accessed=16_000_000, transcendentals=0),
        name="second",
    )(at, *parts, *weights)


def last_kernel(core_ref, routes_ref, sel_ref, wsel_ref, recv_ref, go_ref, moe_ref, gt_ref, gr_ref, inner_s):
    step = pl.program_id(0)
    half = go_ref.shape[1] // 2
    own = pl.ds(pl.multiple_of(core_ref[0] * half, 128), half)
    other = pl.ds(pl.multiple_of((1 - core_ref[0]) * half, 128), half)
    block = [recv_ref[0, :, q * half : (q + 1) * half] for q in range(3)]
    moe_ref[:, own] = (dot(wsel_ref[0], block[0]) + dot(wsel_ref[1], block[0])).astype(BF16)
    moe_ref[:, other] = (dot(wsel_ref[0], block[1]) + dot(wsel_ref[1], block[1])).astype(BF16)
    gt_ref[:, own] = dot(sel_ref[0], block[2]).astype(BF16)
    gt_ref[:, other] = (dot(sel_ref[1], block[0]) + dot(sel_ref[2], block[1]) + dot(sel_ref[3], block[2])).astype(BF16)
    inner = dot(go_ref[:, own], block[0], 1, 1) + dot(go_ref[:, other], block[1], 1, 1)

    @pl.when(step == 0)
    def _():
        inner_s[...] = inner

    @pl.when(step > 0)
    def _():
        inner_s[...] += inner

    @pl.when(step == pl.num_programs(0) - 1)
    def _():
        rows, picks = routes_ref.shape
        lanes = sel_ref.shape[2]
        expert = lax.broadcasted_iota(jnp.int32, (rows, lanes), 1) >> 3
        column = lax.broadcasted_iota(jnp.int32, (rows, picks), 1)
        held = sel_ref[0].astype(F32) * inner_s[...]
        out = jnp.zeros((rows, picks), F32)
        for k in range(picks):
            mine = jnp.sum(jnp.where(routes_ref[:, k : k + 1] == expert, held, 0.0), axis=1, keepdims=True)
            out = out + jnp.where(column == k, mine, 0.0)
        gr_ref[...] = out


def last(core, routes, sel, wsel, recv, grad_out):
    rows, width = grad_out.shape
    quarters, lanes, packed = recv.shape
    column = pl.BlockSpec((rows, width // quarters), lambda i: (0, i))
    return pl.pallas_call(
        last_kernel,
        grid=(quarters,),
        in_specs=[smem(), whole(), whole(), whole(), pl.BlockSpec((1, lanes, packed), lambda i: (i, 0, 0)), column],
        out_specs=[column, column, pl.BlockSpec(routes.shape, lambda i: (0, 0))],
        out_shape=[
            jax.ShapeDtypeStruct((rows, width), BF16),
            jax.ShapeDtypeStruct((rows, width), BF16),
            jax.ShapeDtypeStruct(routes.shape, F32),
        ],
        scratch_shapes=[pltpu.VMEM((rows, lanes), F32)],
        compiler_params=pltpu.CompilerParams(vmem_limit_bytes=VMEM_LIMIT),
        cost_estimate=pl.CostEstimate(flops=1_500_000_000, bytes_accessed=8_500_000, transcendentals=0),
        name="last",
    )(core, routes, sel, wsel, recv, grad_out)


def on_device(tokens, routes, route_weight, w_gate, w_up, w_down, grad_out):
    quarters = lax.axis_size("y")
    experts = lax.axis_size("x") * lax.axis_size("z")
    slots = experts * CAP
    lanes = experts * PAD
    hidden = w_gate.shape[2]
    everyone = ("y", "x", "z")
    core = lax.axis_index("k").astype(jnp.int32).reshape(1)
    at = lax.axis_index("y").astype(jnp.int32).reshape(1)

    def to_partner(value):
        return lax.ppermute(value, "k", [(0, 1), (1, 0)])

    def along(value, shift):
        return lax.ppermute(value, "y", [(i, (i + shift) % quarters) for i in range(quarters)])

    def exchange(value):
        flat = value.reshape(quarters * experts, PAD, value.shape[2])
        return lax.all_to_all(flat, everyone, 0, 0, tiled=True).reshape(value.shape)

    gate_own, up_own, down_own = w_gate[0], w_up[0], w_down[0]
    gate_other, up_other, down_other = to_partner(gate_own), to_partner(up_own), to_partner(down_own)

    sent, sel, wsel = prep(core, routes, route_weight, tokens, grad_out, quarters, experts)
    recv = exchange(sent)
    p0, p1, p2, p3, rows_own, rows_other = first(
        at, recv, (gate_own, gate_other, up_own, up_other, down_own, down_other), hidden, slots
    )
    others = [along(p2, 2), along(p1, 1), along(p3, 3)]
    rows_partner = to_partner(rows_other)
    mine = activate(p0, others)
    parts = [mine, along(mine, 3), along(mine, 2), along(mine, 1)]
    back = exchange(second(at, parts, (down_own, down_other, gate_own, gate_other, up_own, up_other), lanes))

    parts_partner = [to_partner(one) for one in parts]
    x_all = jnp.concatenate([rows_own[0], rows_partner[0]], axis=0)
    d_all = jnp.concatenate([rows_own[1], rows_partner[1]], axis=0)
    h_all, dg_all, du_all = (jnp.concatenate([one[i] for one in parts + parts_partner], axis=0) for i in range(3))
    grad_gate = dot(x_all, dg_all, 0, 0).astype(BF16)
    grad_up = dot(x_all, du_all, 0, 0).astype(BF16)
    grad_down = dot(h_all, d_all, 0, 0).astype(BF16)

    moe_out, grad_tokens, grad_route = last(core, routes, sel, wsel, back, grad_out)
    return (moe_out, grad_tokens, grad_route, grad_gate[None], grad_up[None], grad_down[None])


def solution(mesh):
    ctx, head = mesh.shape["ctx"], mesh.shape["head"]
    side = int(round(ctx**0.5))
    fine = Mesh(mesh.devices.reshape(side, ctx // side, head // 2, 2), ("x", "z", "y", "k"))
    e, d, both = ("x", "z"), ("y", "k"), ("x", "z", "y", "k")
    rows = P(both, None)
    up, down = P(e, d, None), P(e, None, d)
    return jax.shard_map(
        on_device,
        mesh=fine,
        in_specs=(rows, rows, rows, up, up, down, rows),
        out_specs=(rows, rows, rows, up, up, down),
        check_vma=False,
    )
```

time: 300 us -> 199 us (0.66)
  waiting for transfers between devices: 162 us -> 97.6 us
  Pallas kernels: 0 us -> 38 us
  matrix products: 42.3 us -> 10.4 us
  other arithmetic: 18.5 us -> 3.83 us
  between operations: 14.3 us -> 0.75 us
  local copies, waits for them, and re-layouts: 29.7 us -> 18.9 us
  starting transfers between devices: 32.6 us -> 29.1 us
    ppermute x0 -> x14, waiting for transfers between devices: none -> 55.1 us  [the longest x6 46.3 us: along(): lax.ppermute(value, 'y', [(i, (i + shift) % quarters) for i in range(quar...]
    reduce_scatter x1 -> x0, waiting for transfers between devices: 53.1 us -> none  [on_device(): lax.psum_scatter(jnp.concatenate([forward, backward], axis=1), 'head', sc...]
    pallas_call x0 -> x4, Pallas kernels: none -> 38 us  [the longest x1 12.9 us: second(): pl.pallas_call(second_kernel, in_specs=[smem()] + [whole()] * 10, out_spe...]
    all_gather x1 -> x0, waiting for transfers between devices: 34.1 us -> none  [on_device(): lax.all_gather(activate(row_share, hidden_width), 'head', axis=0, tiled=T...]
    all_to_all x4 -> x2, waiting for transfers between devices: 74.6 us -> 42.5 us  [exchange(): return lax.all_to_all(flat, everyone, 0, 0, tiled=True).reshape(value.shape)]
    dot_general x10 -> x3, matrix products: 42.3 us -> 10.4 us  [dot(): lax.dot_general(a, b, (((ca,), (cb,)), ((), ())), preferred_element_type=...]
    reshape x9 -> x0, local copies, waits for them, and re-layouts: 19 us -> none  [the longest x1 3.56 us: on_device(): x_in = x_in.reshape(total_rows, slice_width)]
    unnamed x11 -> x31, local copies, waits for them, and re-layouts: 4.19 us -> 15.6 us
  transfers between devices with their start and end apart: 6 -> 16, of which waited for: 6 -> 10; matrix products, arithmetic and copies ran while one was open for 11% -> 11% of each run, Pallas kernels for 0% -> 6%
where the time goes in v1:
time: 199 us
  waiting for transfers between devices  97.6 us (49%)
  Pallas kernels  38 us (19%)
  starting transfers between devices  29.1 us (15%)
  local copies, waits for them, and re-layouts  18.9 us (9%)
  matrix products  10.4 us (5%)
  other arithmetic  3.83 us (2%)
    ppermute x6, waiting for transfers between devices, along(): lax.ppermute(value, 'y', [(i, (i + shift) % quarters) for i in range(quar...  46.3 us
    all_to_all x2, waiting for transfers between devices, exchange(): return lax.all_to_all(flat, everyone, 0, 0, tiled=True).reshape(value.shape)  42.5 us
    all_to_all x2, starting transfers between devices, exchange(): return lax.all_to_all(flat, everyone, 0, 0, tiled=True).reshape(value.shape)  22 us
    unnamed x31, local copies, waits for them, and re-layouts  15.6 us
    pallas_call x1, Pallas kernels, second(): pl.pallas_call(second_kernel, in_specs=[smem()] + [whole()] * 10, out_spe...  12.9 us
    pallas_call x1, Pallas kernels, first(): pl.pallas_call(first_kernel, grid=(hidden // step,), in_specs=[smem(), wh...  12 us
    dot_general x3, matrix products, dot(): lax.dot_general(a, b, (((ca,), (cb,)), ((), ())), preferred_element_type=...  10.4 us
    ppermute x8, waiting for transfers between devices, to_partner(): return lax.ppermute(value, 'k', [(0, 1), (1, 0)])  8.78 us
  transfers between devices with their start and end apart: 16, of which 10 were waited for; matrix products, arithmetic and copies ran while one was open for 11% of the time, Pallas kernels for 6%

profile of v1, /device:TPU:0, one launch (start us, length us, event | category | flops | bytes accessed | tf_op | source)
XLA Modules:
  0.0 198.5 jit_solution(10173839774952402094)
XLA Ops:
  0.6 1.4 copy.15.routes_ref
  2.1 1.4 copy.14.weight_ref
  3.5 6.0 %prep.1 = (bf16[4,128,2688]{2,1,0:T(8,128)(2,1)}, bf16[4,128,128]{2,1,0:T(8,128)(2,1)}, bf16[2,128,128]{2,1,0:T(8,128)(2,1)}) custom-call(s32[1]{0:T(128)} %bitcast.core_ref, s32[128,8]{1,0:T(8,128)} %copy.15.routes_ref, f32[128,8]{1,0:T(8,128)} %copy.14.weight_ref, bf16[128,7168]{1,0:T(8,128)(2,1)} %tok_ref.1, bf16[128,7168]{1,0:T(8,128)(2,1)} %go_ref.3), custom_call_target="tpu_custom_call" | custom-call | flops 800000000 | bytes 6500000 | tf_op jit(solution)/shard_map/prep/pallas_call | solution.py:87
  9.5 11.5 %all-to-all-start = ((bf16[64,8,2688]{2,1,0:T(8,128)(2,1)}), bf16[64,8,2688]{2,1,0:T(8,128)(2,1)S(1)}, u32[]{:S(2)}, u32[]{:S(2)}) async-start(bf16[64,8,2688]{2,1,0:T(8,128)(2,1)} %bitcast.161), calls=%async_computation | async-start | bytes 5505024 | tf_op jit(solution)/shard_map/all_to_all | solution.py:291
  21.1 0.5 collective-permute-start.1
  21.7 3.5 %collective-permute-done.gx_ref = bf16[896,1024]{1,0:T(8,128)(2,1)} collective-permute-done((bf16[896,1024]{1,0:T(8,128)(2,1)}, bf16[896,1024]{1,0:T(8,128)(2,1)}, u32[]{:S(2)}, u32[]{:S(2)}) %collective-permute-start) | collective-permute-done | bytes 1835040 | tf_op jit(solution)/shard_map/ppermute | solution.py:284
  25.2 2.6 %collective-permute-done.1.ux_ref = bf16[896,1024]{1,0:T(8,128)(2,1)} collective-permute-done((bf16[896,1024]{1,0:T(8,128)(2,1)}, bf16[896,1024]{1,0:T(8,128)(2,1)}, u32[]{:S(2)}, u32[]{:S(2)}) %collective-permute-start.1) | collective-permute-done | bytes 1835040 | tf_op jit(solution)/shard_map/ppermute | solution.py:284
  27.8 2.6 %collective-permute-done.2.dx_ref = bf16[1024,896]{1,0:T(8,128)(2,1)} collective-permute-done((bf16[1024,896]{1,0:T(8,128)(2,1)}, bf16[1024,896]{1,0:T(8,128)(2,1)}, u32[]{:S(2)}, u32[]{:S(2)}) %collective-permute-start.2) | collective-permute-done | bytes 1835040 | tf_op jit(solution)/shard_map/ppermute | solution.py:284
  30.4 27.0 %all-to-all-done = bf16[64,8,2688]{2,1,0:T(8,128)(2,1)S(1)} async-done(((bf16[64,8,2688]{2,1,0:T(8,128)(2,1)}), bf16[64,8,2688]{2,1,0:T(8,128)(2,1)S(1)}, u32[]{:S(2)}, u32[]{:S(2)}) %all-to-all-start) | async-done | bytes 2752544 | tf_op jit(solution)/shard_map/all_to_all | solution.py:291
  57.4 1.5 copy-done.1
  58.9 12.0 %first.1 = (f32[3,96,1024]{2,1,0:T(8,128)}, bf16[3,96,1024]{2,1,0:T(8,128)(2,1)}, bf16[3,96,1024]{2,1,0:T(8,128)(2,1)}, bf16[3,96,1024]{2,1,0:T(8,128)(2,1)}, bf...) custom-call(s32[1]{0:T(128)} %bitcast.1.at_ref, bf16[4,128,2688]{2,1,0:T(8,128)(2,1)} %bitcast.160, ...), custom_call_target="tpu_custom_call" | custom-call | flops 6000000000 | bytes 20000000 | tf_op jit(solution)/shard_map/first/pallas_call | solution.py:157
  71.0 1.4 collective-permute-start.5
  72.3 0.7 collective-permute-start.4
  73.1 0.9 collective-permute-start.3
  73.9 13.6 %collective-permute-done.5 = bf16[3,96,1024]{2,1,0:T(8,128)(2,1)S(1)} collective-permute-done((bf16[3,96,1024]{2,1,0:T(8,128)(2,1)}, bf16[3,96,1024]{2,1,0:T(8,128)(2,1)S(1)}, u32[]{:S(2)}, u32[]{:S(2)}) %collective-permute-start.5) | collective-permute-done | bytes 589856 | tf_op jit(solution)/shard_map/ppermute | solution.py:287
  87.5 11.4 %collective-permute-done.4 = bf16[3,96,1024]{2,1,0:T(8,128)(2,1)S(1)} collective-permute-done((bf16[3,96,1024]{2,1,0:T(8,128)(2,1)}, bf16[3,96,1024]{2,1,0:T(8,128)(2,1)S(1)}, u32[]{:S(2)}, u32[]{:S(2)}) %collective-permute-start.4) | collective-permute-done | bytes 589856 | tf_op jit(solution)/shard_map/ppermute | solution.py:287
  99.0 1.6 convert_add_fusion
  100.6 0.2 multiply_convert_fusion.2
  100.8 0.9 pad_maximum_fusion.3.h0_ref
  101.8 0.3 collective-permute-start.6
  102.0 0.6 collective-permute-start.7
  102.6 1.4 collective-permute-start.8
  104.0 1.0 slice_bitcast_fusion.2
  105.0 0.5 collective-permute-start.10
  105.5 1.1 fusion.14
  106.6 11.7 %collective-permute-done.6.h1_ref = bf16[3,96,1024]{2,1,0:T(8,128)(2,1)S(1)} collective-permute-done((bf16[3,96,1024]{2,1,0:T(8,128)(2,1)}, bf16[3,96,1024]{2,1,0:T(8,128)(2,1)S(1)}, u32[]{:S(2)}, u32[]{:S(2)}) %collective-permute-start.6) | collective-permute-done | bytes 589856 | tf_op jit(solution)/shard_map/ppermute | solution.py:287
  118.2 1.8 collective-permute-done.7.h2_ref
  120.0 7.8 %collective-permute-done.8.h3_ref = bf16[3,96,1024]{2,1,0:T(8,128)(2,1)S(1)} collective-permute-done((bf16[3,96,1024]{2,1,0:T(8,128)(2,1)}, bf16[3,96,1024]{2,1,0:T(8,128)(2,1)S(1)}, u32[]{:S(2)}, u32[]{:S(2)}) %collective-permute-start.8) | collective-permute-done | bytes 589856 | tf_op jit(solution)/shard_map/ppermute | solution.py:287
  127.9 0.8 copy-done.4
  128.7 12.9 %second.1 = bf16[4,128,2688]{2,1,0:T(8,128)(2,1)} custom-call(s32[1]{0:T(128)} %bitcast.1.at_ref, bf16[3,96,1024]{2,1,0:T(8,128)(2,1)} %pad_maximum_fusion.3.h0_ref, bf16[3,96,1024]{2,1,0:T(8,128)(2,1)} %copy-done.8, bf16[3,96,1024]{2,1,0:T(8,128)(2,1)} %copy-done.6, bf16[3,96,1024]{2,1,0:T(8,128)(2,1)} %copy-done.4, bf16[1024,896]{1,0:T(8,128)(2,1)} %bitcast.170, ...), custom_call_target="tpu_custom_call" | custom-call | flops 5000000000 | bytes 16000000 | tf_op jit(solution)/shard_map/second/pallas_call | solution.py:206
  141.6 10.5 %all-to-all-start.1 = ((bf16[64,8,2688]{2,1,0:T(8,128)(2,1)}), bf16[64,8,2688]{2,1,0:T(8,128)(2,1)S(1)}, u32[]{:S(2)}, u32[]{:S(2)}) async-start(bf16[64,8,2688]{2,1,0:T(8,128)(2,1)} %bitcast.159), calls=%async_computation.1 | async-start | bytes 5505024 | tf_op jit(solution)/shard_map/all_to_all | solution.py:291
  152.2 0.5 collective-permute-start.12
  152.8 1.9 fusion.22
  154.8 0.8 fusion.21
  155.6 0.8 fusion.20
  156.4 1.9 fusion.19
  158.3 1.5 slice_bitcast_fusion
  159.9 0.3 copy-done.9
  160.2 0.8 fusion.18
  161.0 0.8 fusion.17
  161.7 0.8 fusion.16
  162.5 4.4 %convert_bitcast_fusion.2 = bf16[1,896,1024]{2,1,0:T(8,128)(2,1)} fusion(bf16[768,1024]{1,0:T(8,128)(2,1)} %get-tuple-element.48, bf16[384,896]{1,0:T(8,128)(2,1)S(1)} %get-tuple-element.39, bf16[384,896]{1,0:T(8,128)(2,1)S(1)} %copy-done.3), kind=kOutput, calls=%fused_computation.2 | convolution fusion | flops 1412956160 | bytes 4784128 | tf_op jit(solution)/shard_map/dot_general | solution.py:18
  166.9 2.9 %convert_bitcast_fusion.1 = bf16[1,896,1024]{2,1,0:T(8,128)(2,1)} fusion(bf16[768,1024]{1,0:T(8,128)(2,1)S(1)} %copy-done.10, bf16[384,896]{1,0:T(8,128)(2,1)S(1)} %get-tuple-element.39, bf16[384,896]{1,0:T(8,128)(2,1)S(1)} %copy-done.3), kind=kOutput, calls=%fused_computation.1 | convolution fusion | flops 1412956160 | bytes 4784128 | tf_op jit(solution)/shard_map/dot_general | solution.py:18
  169.8 3.1 %convert_bitcast_fusion = bf16[1,1024,896]{2,1,0:T(8,128)(2,1)} fusion(bf16[768,1024]{1,0:T(8,128)(2,1)S(1)} %get-tuple-element.46, bf16[384,896]{1,0:T(8,128)(2,1)S(1)} %get-tuple-element.38, bf16[384,896]{1,0:T(8,128)(2,1)S(1)} %get-tuple-element.36), kind=kOutput, calls=%fused_computation | convolution fusion | flops 1412956160 | bytes 4784128 | tf_op jit(solution)/shard_map/dot_general | solution.py:18
  172.9 15.5 %all-to-all-done.1 = bf16[64,8,2688]{2,1,0:T(8,128)(2,1)S(1)} async-done(((bf16[64,8,2688]{2,1,0:T(8,128)(2,1)}), bf16[64,8,2688]{2,1,0:T(8,128)(2,1)S(1)}, u32[]{:S(2)}, u32[]{:S(2)}) %all-to-all-start.1) | async-done | bytes 2752544 | tf_op jit(solution)/shard_map/all_to_all | solution.py:291
  188.4 1.5 copy-done
  189.9 7.1 %last.1 = (bf16[128,7168]{1,0:T(8,128)(2,1)}, bf16[128,7168]{1,0:T(8,128)(2,1)}, f32[128,8]{1,0:T(8,128)}) custom-call(s32[1]{0:T(128)} %bitcast.core_ref, s32[128,8]{1,0:T(8,128)} %copy.15.routes_ref, bf16[4,128,128]{2,1,0:T(8,128)(2,1)} %get-tuple-element.18.sel_ref, bf16[2,128,128]{2,1,0:T(8,128)(2,1)} %get-tuple-element.19.wsel_ref, ...), custom_call_target="tpu_custom_call" | custom-call | flops 1500000000 | bytes 8500000 | tf_op jit(solution)/shard_map/last/pallas_call | solution.py:256
  197.0 1.5 copy.16
  (29 shorter events, 0.4 us)
Async XLA Ops:
  9.5 47.9 %all-to-all-start = ((bf16[64,8,2688]{2,1,0:T(8,128)(2,1)}), bf16[64,8,2688]{2,1,0:T(8,128)(2,1)S(1)}, u32[]{:S(2)}, u32[]{:S(2)}) async-start(bf16[64,8,2688]{2,1,0:T(8,128)(2,1)} %bitcast.161), calls=%async_computation | async-start | bytes 5505024 | tf_op jit(solution)/shard_map/all_to_all | solution.py:291
  21.0 4.2 %collective-permute-start = (bf16[896,1024]{1,0:T(8,128)(2,1)}, bf16[896,1024]{1,0:T(8,128)(2,1)}, u32[]{:S(2)}, u32[]{:S(2)}) collective-permute-start(bf16[896,1024]{1,0:T(8,128)(2,1)} %bitcast.162), channel_id=1, source_target_pairs={{0,1},{1,0},{2,3},{3,2},{4,5},{5,4},{6,7},{7,6},{8,9},{9,8},{10,11... | collective-permute-start | bytes 5505032 | tf_op jit(solution)/shard_map/ppermute | solution.py:284
  21.1 6.7 %collective-permute-start.1 = (bf16[896,1024]{1,0:T(8,128)(2,1)}, bf16[896,1024]{1,0:T(8,128)(2,1)}, u32[]{:S(2)}, u32[]{:S(2)}) collective-permute-start(bf16[896,1024]{1,0:T(8,128)(2,1)} %bitcast.165), channel_id=1, source_target_pairs={{0,1},{1,0},{2,3},{3,2},{4,5},{5,4},{6,7},{7,6},{8,9},{9,8},{10,11... | collective-permute-start | bytes 5505032 | tf_op jit(solution)/shard_map/ppermute | solution.py:284
  21.6 8.9 %collective-permute-start.2 = (bf16[1024,896]{1,0:T(8,128)(2,1)}, bf16[1024,896]{1,0:T(8,128)(2,1)}, u32[]{:S(2)}, u32[]{:S(2)}) collective-permute-start(bf16[1024,896]{1,0:T(8,128)(2,1)} %bitcast.168), channel_id=1, source_target_pairs={{0,1},{1,0},{2,3},{3,2},{4,5},{5,4},{6,7},{7,6},{8,9},{9,8},{10,11... | collective-permute-start | bytes 5505032 | tf_op jit(solution)/shard_map/ppermute | solution.py:284
  57.4 1.5 copy-start.1
  71.0 16.5 %collective-permute-start.5 = (bf16[3,96,1024]{2,1,0:T(8,128)(2,1)}, bf16[3,96,1024]{2,1,0:T(8,128)(2,1)S(1)}, u32[]{:S(2)}, u32[]{:S(2)}) collective-permute-start(bf16[3,96,1024]{2,1,0:T(8,128)(2,1)} %get-tuple-element.24), channel_id=1, source_target_pairs={{0,6},{2,0},{4,2},{6,4},{1,7},{3,1},{5,3},{7,5},{8,14},{10,8},{12,... | collective-permute-start | bytes 1769480 | tf_op jit(solution)/shard_map/ppermute | solution.py:287
  72.3 26.6 %collective-permute-start.4 = (bf16[3,96,1024]{2,1,0:T(8,128)(2,1)}, bf16[3,96,1024]{2,1,0:T(8,128)(2,1)S(1)}, u32[]{:S(2)}, u32[]{:S(2)}) collective-permute-start(bf16[3,96,1024]{2,1,0:T(8,128)(2,1)} %get-tuple-element.23), channel_id=1, source_target_pairs={{0,2},{2,4},{4,6},{6,0},{1,3},{3,5},{5,7},{7,1},{8,10},{10,12},{12... | collective-permute-start | bytes 1769480 | tf_op jit(solution)/shard_map/ppermute | solution.py:287
  73.1 25.9 %collective-permute-start.3 = (bf16[3,96,1024]{2,1,0:T(8,128)(2,1)}, bf16[3,96,1024]{2,1,0:T(8,128)(2,1)S(1)}, u32[]{:S(2)}, u32[]{:S(2)}) collective-permute-start(bf16[3,96,1024]{2,1,0:T(8,128)(2,1)} %get-tuple-element.22), channel_id=1, source_target_pairs={{0,4},{2,6},{4,0},{6,2},{1,5},{3,7},{5,1},{7,3},{8,12},{10,14},{12... | collective-permute-start | bytes 1769480 | tf_op jit(solution)/shard_map/ppermute | solution.py:287
  100.6 3.4 %copy-start.2 = (bf16[2,384,896]{2,1,0:T(8,128)(2,1)S(1)}, bf16[2,384,896]{2,1,0:T(8,128)(2,1)}, u32[]{:S(2)}) copy-start(bf16[2,384,896]{2,1,0:T(8,128)(2,1)} %get-tuple-element.28) | copy-start | bytes 4128772
  101.8 16.5 %collective-permute-start.6 = (bf16[3,96,1024]{2,1,0:T(8,128)(2,1)}, bf16[3,96,1024]{2,1,0:T(8,128)(2,1)S(1)}, u32[]{:S(2)}, u32[]{:S(2)}) collective-permute-start(bf16[3,96,1024]{2,1,0:T(8,128)(2,1)} %pad_maximum_fusion.3.h0_ref), channel_id=1, source_target_pairs={{0,6},{2,0},{4,2},{6,4},{1,7},{3,1},{5,3},{7,5},{8,14},{10,8},{12,... | collective-permute-start | bytes 1769480 | tf_op jit(solution)/shard_map/ppermute | solution.py:287
  102.0 18.0 %collective-permute-start.7 = (bf16[3,96,1024]{2,1,0:T(8,128)(2,1)}, bf16[3,96,1024]{2,1,0:T(8,128)(2,1)S(1)}, u32[]{:S(2)}, u32[]{:S(2)}) collective-permute-start(bf16[3,96,1024]{2,1,0:T(8,128)(2,1)} %pad_maximum_fusion.3.h0_ref), channel_id=1, source_target_pairs={{0,4},{2,6},{4,0},{6,2},{1,5},{3,7},{5,1},{7,3},{8,12},{10,14},{12... | collective-permute-start | bytes 1769480 | tf_op jit(solution)/shard_map/ppermute | solution.py:287
  102.6 25.2 %collective-permute-start.8 = (bf16[3,96,1024]{2,1,0:T(8,128)(2,1)}, bf16[3,96,1024]{2,1,0:T(8,128)(2,1)S(1)}, u32[]{:S(2)}, u32[]{:S(2)}) collective-permute-start(bf16[3,96,1024]{2,1,0:T(8,128)(2,1)} %pad_maximum_fusion.3.h0_ref), channel_id=1, source_target_pairs={{0,2},{2,4},{4,6},{6,0},{1,3},{3,5},{5,7},{7,1},{8,10},{10,12},{12... | collective-permute-start | bytes 1769480 | tf_op jit(solution)/shard_map/ppermute | solution.py:287
  104.0 54.3 %collective-permute-start.9 = (bf16[2,384,896]{2,1,0:T(8,128)(2,1)}, bf16[2,384,896]{2,1,0:T(8,128)(2,1)}, u32[]{:S(2)}, u32[]{:S(2)}) collective-permute-start(bf16[2,384,896]{2,1,0:T(8,128)(2,1)} %get-tuple-element.29), channel_id=1, source_target_pairs={{0,1},{1,0},{2,3},{3,2},{4,5},{5,4},{6,7},{7,6},{8,9},{9,8},{10,11... | collective-permute-start | bytes 4128776 | tf_op jit(solution)/shard_map/ppermute | solution.py:284
  105.0 51.4 %collective-permute-start.10 = (bf16[3,96,1024]{2,1,0:T(8,128)(2,1)}, bf16[3,96,1024]{2,1,0:T(8,128)(2,1)}, u32[]{:S(2)}, u32[]{:S(2)}) collective-permute-start(bf16[3,96,1024]{2,1,0:T(8,128)(2,1)} %pad_maximum_fusion.3.h0_ref), channel_id=1, source_target_pairs={{0,1},{1,0},{2,3},{3,2},{4,5},{5,4},{6,7},{7,6},{8,9},{9,8},{10,11... | collective-permute-start | bytes 1769480 | tf_op jit(solution)/shard_map/ppermute | solution.py:284
  118.2 9.6 %copy-start.8 = (bf16[3,96,1024]{2,1,0:T(8,128)(2,1)}, bf16[3,96,1024]{2,1,0:T(8,128)(2,1)S(1)}, u32[]{:S(2)}) copy-start(bf16[3,96,1024]{2,1,0:T(8,128)(2,1)S(1)} %collective-permute-done.6.h1_ref) | copy-start | bytes 1769476
  120.0 7.8 %copy-start.6 = (bf16[3,96,1024]{2,1,0:T(8,128)(2,1)}, bf16[3,96,1024]{2,1,0:T(8,128)(2,1)S(1)}, u32[]{:S(2)}) copy-start(bf16[3,96,1024]{2,1,0:T(8,128)(2,1)S(1)} %collective-permute-done.7.h2_ref) | copy-start | bytes 1769476
  127.9 0.8 copy-start.4
  141.6 46.8 %all-to-all-start.1 = ((bf16[64,8,2688]{2,1,0:T(8,128)(2,1)}), bf16[64,8,2688]{2,1,0:T(8,128)(2,1)S(1)}, u32[]{:S(2)}, u32[]{:S(2)}) async-start(bf16[64,8,2688]{2,1,0:T(8,128)(2,1)} %bitcast.159), calls=%async_computation.1 | async-start | bytes 5505024 | tf_op jit(solution)/shard_map/all_to_all | solution.py:291
  152.1 2.6 %copy-start.7 = (bf16[3,96,1024]{2,1,0:T(8,128)(2,1)S(1)}, bf16[3,96,1024]{2,1,0:T(8,128)(2,1)}, u32[]{:S(2)}) copy-start(bf16[3,96,1024]{2,1,0:T(8,128)(2,1)} %copy-done.6) | copy-start | bytes 1769476
  152.1 3.5 %copy-start.5 = (bf16[3,96,1024]{2,1,0:T(8,128)(2,1)S(1)}, bf16[3,96,1024]{2,1,0:T(8,128)(2,1)}, u32[]{:S(2)}) copy-start(bf16[3,96,1024]{2,1,0:T(8,128)(2,1)} %copy-done.4) | copy-start | bytes 1769476
  152.1 7.7 %collective-permute-start.11 = (bf16[3,96,1024]{2,1,0:T(8,128)(2,1)}, bf16[3,96,1024]{2,1,0:T(8,128)(2,1)S(1)}, u32[]{:S(2)}, u32[]{:S(2)}) collective-permute-start(bf16[3,96,1024]{2,1,0:T(8,128)(2,1)} %copy-done.8), channel_id=1, source_target_pairs={{0,1},{1,0},{2,3},{3,2},{4,5},{5,4},{6,7},{7,6},{8,9},{9,8},{10,11... | collective-permute-start | bytes 1769480 | tf_op jit(solution)/shard_map/ppermute | solution.py:284
  152.2 8.7 %collective-permute-start.12 = (bf16[3,96,1024]{2,1,0:T(8,128)(2,1)}, bf16[3,96,1024]{2,1,0:T(8,128)(2,1)S(1)}, u32[]{:S(2)}, u32[]{:S(2)}) collective-permute-start(bf16[3,96,1024]{2,1,0:T(8,128)(2,1)} %copy-done.6), channel_id=1, source_target_pairs={{0,1},{1,0},{2,3},{3,2},{4,5},{5,4},{6,7},{7,6},{8,9},{9,8},{10,11... | collective-permute-start | bytes 1769480 | tf_op jit(solution)/shard_map/ppermute | solution.py:284
  152.7 9.0 %collective-permute-start.13 = (bf16[3,96,1024]{2,1,0:T(8,128)(2,1)}, bf16[3,96,1024]{2,1,0:T(8,128)(2,1)S(1)}, u32[]{:S(2)}, u32[]{:S(2)}) collective-permute-start(bf16[3,96,1024]{2,1,0:T(8,128)(2,1)} %copy-done.4), channel_id=1, source_target_pairs={{0,1},{1,0},{2,3},{3,2},{4,5},{5,4},{6,7},{7,6},{8,9},{9,8},{10,11... | collective-permute-start | bytes 1769480 | tf_op jit(solution)/shard_map/ppermute | solution.py:284
  158.3 1.8 copy-start.9
  160.2 2.4 %copy-start.3 = (bf16[384,896]{1,0:T(8,128)(2,1)S(1)}, bf16[384,896]{1,0:T(8,128)(2,1)}, u32[]{:S(2)}) copy-start(bf16[384,896]{1,0:T(8,128)(2,1)} %get-tuple-element.37) | copy-start | bytes 2064388
  162.5 4.4 %copy-start.10 = (bf16[768,1024]{1,0:T(8,128)(2,1)S(1)}, bf16[768,1024]{1,0:T(8,128)(2,1)}, u32[]{:S(2)}) copy-start(bf16[768,1024]{1,0:T(8,128)(2,1)} %get-tuple-element.47) | copy-start | bytes 4718596
  188.4 1.5 copy-start

commit v2 on v1

v2 whole, which is shorter than its diff:
```python
import functools

import jax
import jax.numpy as jnp
from jax import lax
from jax.experimental import pallas as pl
from jax.experimental.pallas import tpu as pltpu
from jax.sharding import Mesh, PartitionSpec as P

CAP = 6
PAD = 8
BF16 = jnp.bfloat16
F32 = jnp.float32
VMEM_LIMIT = 32 * 1024 * 1024
SMALL_LIMIT = 32 * 1024 * 1024
BIG_LIMIT = 60 * 1024 * 1024


def dot(a, b, ca=1, cb=0):
    return lax.dot_general(a, b, (((ca,), (cb,)), ((), ())), preferred_element_type=F32)


def whole():
    return pl.BlockSpec(memory_space=pltpu.VMEM)


def hbm():
    return pl.BlockSpec(memory_space=pltpu.HBM)


def start(pairs, sems):
    copies = [pltpu.make_async_copy(src, dst, sems.at[i]) for i, (src, dst) in enumerate(pairs)]
    for one in copies:
        one.start()
    return copies


def smem():
    return pl.BlockSpec(memory_space=pltpu.SMEM)


def tail_slot(row, q):
    return jnp.where(row == 6, q, jnp.where(row == 7, 3 + q, -1))


def main_slot(row):
    return jnp.where(row < CAP, row, -1)


def prep_kernel(core_ref, routes_ref, weight_ref, tok_ref, go_ref, out_ref, sel_ref, wsel_ref, scale_s):
    picks, rows = routes_ref.shape
    lanes = sel_ref.shape[1]
    half = tok_ref.shape[1] // 2

    @pl.when(pl.program_id(0) == 0)
    def _():
        slot = lax.broadcasted_iota(jnp.int32, (lanes, rows), 0)
        expert, row = slot >> 3, slot & 7
        named = jnp.zeros((lanes, rows), F32)
        weight = jnp.zeros((lanes, rows), F32)
        for k in range(picks):
            hit = routes_ref[k : k + 1, :] == expert
            named = named + jnp.where(hit, 1.0, 0.0)
            weight = weight + jnp.where(hit, weight_ref[k : k + 1, :], 0.0)
        earlier = lax.broadcasted_iota(jnp.int32, (rows, rows), 0) < lax.broadcasted_iota(jnp.int32, (rows, rows), 1)
        before = dot(named.astype(BF16), jnp.where(earlier, 1.0, 0.0).astype(BF16))
        picked, scales = [], []
        for i, want in enumerate([main_slot(row)] + [tail_slot(row, q) for q in range(3)]):
            one = jnp.where((named > 0.5) & (before == want.astype(F32)), 1.0, 0.0)
            sel_ref[i] = one.astype(BF16)
            picked.append(one)
            scales.append(jnp.sum(one * weight, axis=1, keepdims=True))
        plain = jnp.where((lax.broadcasted_iota(jnp.int32, (lanes, 1), 0) & 7) < CAP, 1.0, 0.0)
        scale_s[0] = plain + scales[1]
        scale_s[1] = plain + scales[2]
        scale_s[2] = scales[0] + scales[3]
        wsel = picked[0] * weight
        high = wsel.astype(BF16)
        wsel_ref[0] = high
        wsel_ref[1] = (wsel - high.astype(F32)).astype(BF16)

    own = pl.multiple_of(core_ref[0] * half, 128)
    other = pl.multiple_of((1 - core_ref[0]) * half, 128)
    tail = go_ref[:, pl.ds(other, half)]
    sources = (tok_ref[:, pl.ds(own, half)], tok_ref[:, pl.ds(other, half)], go_ref[:, pl.ds(own, half)])
    for q, source in enumerate(sources):
        rows_q = dot(sel_ref[0], source) + dot(sel_ref[1 + q], tail)
        out_ref[0, :, q * half : (q + 1) * half] = (scale_s[q] * rows_q).astype(BF16)


def prep(core, routes, route_weight, tokens, grad_out, quarters, experts):
    rows, width = tokens.shape
    lanes = experts * PAD
    quarter = width // quarters
    half = quarter // 2
    column = pl.BlockSpec((rows, quarter), lambda i: (0, i))
    return pl.pallas_call(
        prep_kernel,
        grid=(quarters,),
        in_specs=[smem(), whole(), whole(), column, column],
        out_specs=[
            pl.BlockSpec((1, lanes, 3 * half), lambda i: (i, 0, 0)),
            pl.BlockSpec((4, lanes, rows), lambda i: (0, 0, 0)),
            pl.BlockSpec((2, lanes, rows), lambda i: (0, 0, 0)),
        ],
        out_shape=[
            jax.ShapeDtypeStruct((quarters, lanes, 3 * half), BF16),
            jax.ShapeDtypeStruct((4, lanes, rows), BF16),
            jax.ShapeDtypeStruct((2, lanes, rows), BF16),
        ],
        scratch_shapes=[pltpu.VMEM((3, lanes, 1), F32)],
        compiler_params=pltpu.CompilerParams(vmem_limit_bytes=BIG_LIMIT),
        cost_estimate=pl.CostEstimate(flops=800_000_000, bytes_accessed=6_500_000, transcendentals=0),
        name="prep",
    )(core, routes, route_weight, tokens, grad_out)


def slot_masks(slots, lanes, transposed=False):
    shape = (lanes, slots) if transposed else (slots, lanes)
    slot_dim, lane_dim = (1, 0) if transposed else (0, 1)
    slot = lax.broadcasted_iota(jnp.int32, shape, slot_dim)
    lane = lax.broadcasted_iota(jnp.int32, shape, lane_dim)
    expert = (slot * 171) >> 10
    place = slot - expert * CAP
    row = lane & 7
    same = (lane >> 3) == expert
    wants = [main_slot(row)] + [tail_slot(row, q) for q in range(3)]
    return [jnp.where(same & (place == want), 1.0, 0.0).astype(BF16) for want in wants]


def pair_of(ref, p, columns):
    return jnp.concatenate([ref[2 * p, :, columns], ref[2 * p + 1, :, columns]], axis=0)


def share_out(at_ref, total_s, outs):
    quarters = len(outs)
    slots = outs[0].shape[0]
    for j, out in enumerate(outs):
        rows = pl.ds(pl.multiple_of(lax.rem(at_ref[0] + j, quarters) * slots, 32), slots)
        out[...] = total_s[rows, :].astype(out.dtype)


def gate_kernel(at_ref, recv_any, wo_ref, wx_ref, p0_ref, p1_ref, p2_ref, p3_ref, own_ref, other_ref, kept_any, total_s, recv_s, sems):
    quarters, lanes, _ = recv_any.shape
    half = wo_ref.shape[0]
    slots = p0_ref.shape[0]
    pairs = quarters // 2
    copies = start([(recv_any.at[pl.ds(2 * p, 2), :, pl.ds(0, 2 * half)], recv_s.at[p]) for p in range(pairs)], sems)
    main = slot_masks(2 * slots, 2 * lanes)[0]
    for p in range(pairs):
        rows = slice(2 * p * slots, 2 * (p + 1) * slots)
        copies[p].wait()
        block = jnp.concatenate([recv_s[p, 0], recv_s[p, 1]], axis=0)
        own_ref[rows, :] = dot(main, block[:, :half]).astype(BF16)
        other_ref[rows, :] = dot(main, block[:, half:]).astype(BF16)
    total_s[...] = dot(own_ref[...], wo_ref[...]) + dot(other_ref[...], wx_ref[...])
    share_out(at_ref, total_s, (p0_ref, p1_ref, p2_ref, p3_ref))


def up_kernel(at_ref, own_ref, other_ref, wo_ref, wx_ref, p0_ref, p1_ref, p2_ref, p3_ref, total_s):
    total_s[...] = dot(own_ref[...], wo_ref[...]) + dot(other_ref[...], wx_ref[...])
    share_out(at_ref, total_s, (p0_ref, p1_ref, p2_ref, p3_ref))


def back_kernel(at_ref, recv_ref, wo_ref, wx_ref, p0_ref, p1_ref, p2_ref, p3_ref, own_ref, other_ref, total_s):
    quarters, lanes, _ = recv_ref.shape
    half = wo_ref.shape[1]
    slots = p0_ref.shape[0]
    masks = slot_masks(2 * slots, 2 * lanes)
    for p in range(quarters // 2):
        rows = slice(2 * p * slots, 2 * (p + 1) * slots)
        blocks = [pair_of(recv_ref, p, slice(q * half, (q + 1) * half)) for q in range(3)]
        own_ref[rows, :] = dot(masks[0], blocks[2]).astype(BF16)
        other_ref[rows, :] = sum(dot(masks[1 + q], blocks[q]) for q in range(3)).astype(BF16)
    total_s[...] = dot(own_ref[...], wo_ref[...], 1, 1) + dot(other_ref[...], wx_ref[...], 1, 1)
    share_out(at_ref, total_s, (p0_ref, p1_ref, p2_ref, p3_ref))


def projection(kernel, name, at, rows, weights, over, slots, quarters):
    half, hidden = weights[0].shape[over], weights[0].shape[1 - over]
    outs = [jax.ShapeDtypeStruct((slots, hidden), F32 if j == 0 else BF16) for j in range(quarters)]
    scratch = [pltpu.VMEM((quarters * slots, hidden), F32)]
    if len(rows) == 1:
        outs = outs + [jax.ShapeDtypeStruct((quarters * slots, half), BF16)] * 2
    in_specs = [smem()] + [whole()] * (len(rows) + 2)
    out_specs = [whole()] * len(outs)
    aliases = {}
    if kernel is gate_kernel:
        anywhere = pl.BlockSpec(memory_space=pl.ANY)
        in_specs[1] = anywhere
        outs.append(jax.ShapeDtypeStruct(rows[0].shape, BF16))
        out_specs.append(anywhere)
        aliases = {1: len(outs) - 1}
        scratch += [
            pltpu.VMEM((quarters // 2, 2, rows[0].shape[1], 2 * half), BF16),
            pltpu.SemaphoreType.DMA((quarters // 2,)),
        ]
    return pl.pallas_call(
        kernel,
        in_specs=in_specs,
        out_specs=out_specs,
        out_shape=outs,
        scratch_shapes=scratch,
        input_output_aliases=aliases,
        compiler_params=pltpu.CompilerParams(vmem_limit_bytes=VMEM_LIMIT),
        cost_estimate=pl.CostEstimate(flops=3_000_000_000, bytes_accessed=8_000_000, transcendentals=0),
        name=name,
    )(at, *rows, *weights)


def gather_parts(at_ref, parts, all_s):
    quarters = len(parts)
    slots = parts[0].shape[0]
    for j, part in enumerate(parts):
        rows = pl.ds(pl.multiple_of(lax.rem(at_ref[0] + j, quarters) * slots, 32), slots)
        all_s[rows, :] = part[...]


def out_kernel(at_ref, h0, h1, h2, h3, wo_ref, wx_ref, out_ref, all_ref):
    quarters, lanes, width = out_ref.shape
    half = width // 2
    slots = h0.shape[0]
    gather_parts(at_ref, (h0, h1, h2, h3), all_ref)
    main = slot_masks(2 * slots, 2 * lanes, True)[0]
    for q, w_ref in enumerate((wo_ref, wx_ref)):
        value = dot(all_ref[...], w_ref[...]).astype(BF16)
        for p in range(quarters // 2):
            rows = dot(main, value[2 * p * slots : 2 * (p + 1) * slots]).astype(BF16)
            out_ref[2 * p, :, q * half : (q + 1) * half] = rows[:lanes]
            out_ref[2 * p + 1, :, q * half : (q + 1) * half] = rows[lanes:]


def out_rows(at, parts, weights, lanes):
    quarters = len(parts)
    slots, hidden = parts[0].shape
    half = weights[0].shape[1]
    return pl.pallas_call(
        out_kernel,
        in_specs=[smem()] + [whole()] * (quarters + 2),
        out_specs=[whole()] * 2,
        out_shape=[
            jax.ShapeDtypeStruct((quarters, lanes, 2 * half), BF16),
            jax.ShapeDtypeStruct((quarters * slots, hidden), BF16),
        ],
        compiler_params=pltpu.CompilerParams(vmem_limit_bytes=VMEM_LIMIT),
        cost_estimate=pl.CostEstimate(flops=2_000_000_000, bytes_accessed=7_500_000, transcendentals=0),
        name="out_rows",
    )(at, *parts, *weights)


def grad_kernel(at_ref, g0, g1, g2, g3, main_ref, go_ref, gx_ref, uo_ref, ux_ref, out_ref, keep_hbm, all_s, sem):
    quarters, lanes, packed = out_ref.shape
    half = packed // 3
    slots = g0.shape[0]
    hidden = all_s.shape[1] // 2
    gather_parts(at_ref, (g0, g1, g2, g3), all_s)
    keep = pltpu.make_async_copy(all_s, keep_hbm, sem)
    keep.start()
    masks = slot_masks(2 * slots, 2 * lanes, True)
    dg, du = all_s[:, :hidden], all_s[:, hidden:]
    own = (dot(dg, go_ref[...], 1, 1) + dot(du, uo_ref[...], 1, 1)).astype(BF16)
    other = (dot(dg, gx_ref[...], 1, 1) + dot(du, ux_ref[...], 1, 1)).astype(BF16)
    for p in range(quarters // 2):
        rows = slice(2 * p * slots, 2 * (p + 1) * slots)
        for q in range(3):
            columns = slice(q * half, (q + 1) * half)
            value = dot(masks[1 + q], other[rows])
            if q == 2:
                value = value + dot(masks[0], own[rows])
            else:
                mine = jnp.concatenate([main_ref[2 * p, :, columns], main_ref[2 * p + 1, :, columns]], axis=0)
                value = value + mine.astype(F32)
            value = value.astype(BF16)
            out_ref[2 * p, :, columns] = value[:lanes]
            out_ref[2 * p + 1, :, columns] = value[lanes:]
    keep.wait()


def grad_rows(at, parts, main, weights):
    quarters, lanes, width = main.shape
    slots, both = parts[0].shape
    packed = width // 2 * 3
    return pl.pallas_call(
        grad_kernel,
        in_specs=[smem()] + [whole()] * (quarters + 5),
        out_specs=[whole(), hbm()],
        out_shape=[
            jax.ShapeDtypeStruct((quarters, lanes, packed), BF16),
            jax.ShapeDtypeStruct((quarters * slots, both), BF16),
        ],
        scratch_shapes=[
            pltpu.VMEM((quarters * slots, both), BF16),
            pltpu.SemaphoreType.DMA,
        ],
        compiler_params=pltpu.CompilerParams(vmem_limit_bytes=SMALL_LIMIT),
        cost_estimate=pl.CostEstimate(flops=3_500_000_000, bytes_accessed=14_000_000, transcendentals=0),
        name="grad_rows",
    )(at, *parts, main, *weights)


def weight_kernel(am_ref, ap_ref, bm_ref, bp_ref, out_ref):
    out_ref[...] = (dot(am_ref[...], bm_ref[...], 0, 0) + dot(ap_ref[...], bp_ref[...], 0, 0)).astype(BF16)


def weight_grad(a_mine, a_partner, b_mine, b_partner, step, at=0, columns=None):
    slots, rows = a_mine.shape
    columns = columns or b_mine.shape[1]
    a_spec = pl.BlockSpec((slots, rows), lambda n: (0, 0))
    b_spec = pl.BlockSpec((slots, step), lambda n: (0, n + at))
    return pl.pallas_call(
        weight_kernel,
        grid=(columns // step,),
        in_specs=[a_spec, a_spec, b_spec, b_spec],
        out_specs=pl.BlockSpec((rows, step), lambda n: (0, n)),
        out_shape=jax.ShapeDtypeStruct((rows, columns), BF16),
        compiler_params=pltpu.CompilerParams(vmem_limit_bytes=VMEM_LIMIT),
        cost_estimate=pl.CostEstimate(flops=1_500_000_000, bytes_accessed=5_000_000, transcendentals=0),
        name="weight_grad",
    )(a_mine, a_partner, b_mine, b_partner)


def last_kernel(core_ref, routes_ref, sel_ref, wsel_ref, recv_ref, go_ref, moe_ref, gt_ref, gr_ref, inner_s):
    step = pl.program_id(0)
    half = go_ref.shape[1] // 2
    own = pl.ds(pl.multiple_of(core_ref[0] * half, 128), half)
    other = pl.ds(pl.multiple_of((1 - core_ref[0]) * half, 128), half)
    block = [recv_ref[0, :, q * half : (q + 1) * half] for q in range(3)]
    moe_ref[:, own] = (dot(wsel_ref[0], block[0], 0, 0) + dot(wsel_ref[1], block[0], 0, 0)).astype(BF16)
    moe_ref[:, other] = (dot(wsel_ref[0], block[1], 0, 0) + dot(wsel_ref[1], block[1], 0, 0)).astype(BF16)
    gt_ref[:, own] = dot(sel_ref[0], block[2], 0, 0).astype(BF16)
    gt_ref[:, other] = sum(dot(sel_ref[1 + q], block[q], 0, 0) for q in range(3)).astype(BF16)
    inner = dot(block[0], go_ref[:, own], 1, 1) + dot(block[1], go_ref[:, other], 1, 1)

    @pl.when(step == 0)
    def _():
        inner_s[...] = inner

    @pl.when(step > 0)
    def _():
        inner_s[...] += inner

    @pl.when(step == pl.num_programs(0) - 1)
    def _():
        picks, rows = routes_ref.shape
        lanes = sel_ref.shape[1]
        expert = lax.broadcasted_iota(jnp.int32, (lanes, rows), 0) >> 3
        held = sel_ref[0].astype(F32) * inner_s[...]
        for k in range(picks):
            mine = jnp.where(routes_ref[k : k + 1, :] == expert, held, 0.0)
            gr_ref[k : k + 1, :] = jnp.sum(mine, axis=0, keepdims=True)


def last(core, routes, sel, wsel, recv, grad_out):
    rows, width = grad_out.shape
    quarters, lanes, packed = recv.shape
    column = pl.BlockSpec((rows, width // quarters), lambda i: (0, i))
    return pl.pallas_call(
        last_kernel,
        grid=(quarters,),
        in_specs=[smem(), whole(), whole(), whole(), pl.BlockSpec((1, lanes, packed), lambda i: (i, 0, 0)), column],
        out_specs=[column, column, pl.BlockSpec(routes.shape, lambda i: (0, 0))],
        out_shape=[
            jax.ShapeDtypeStruct((rows, width), BF16),
            jax.ShapeDtypeStruct((rows, width), BF16),
            jax.ShapeDtypeStruct(routes.shape, F32),
        ],
        scratch_shapes=[pltpu.VMEM((lanes, rows), F32)],
        compiler_params=pltpu.CompilerParams(vmem_limit_bytes=BIG_LIMIT),
        cost_estimate=pl.CostEstimate(flops=1_500_000_000, bytes_accessed=8_500_000, transcendentals=0),
        name="last",
    )(core, routes, sel, wsel, recv, grad_out)


def on_device(tokens, routes, route_weight, w_gate, w_up, w_down, grad_out):
    quarters = lax.axis_size("y")
    experts = lax.axis_size("x") * lax.axis_size("z")
    slots = experts * CAP
    lanes = experts * PAD
    hidden = w_gate.shape[2]
    everyone = ("y", "x", "z")
    half = w_gate.shape[1]
    core = lax.axis_index("k").astype(jnp.int32).reshape(1)
    at = lax.axis_index("y").astype(jnp.int32).reshape(1)

    def to_partner(value):
        return lax.ppermute(value, "k", [(0, 1), (1, 0)])

    def along(value, shift):
        return lax.ppermute(value, "y", [(i, (i + shift) % quarters) for i in range(quarters)])

    def exchange(value):
        flat = value.reshape(quarters * experts, PAD, value.shape[2])
        return lax.all_to_all(flat, everyone, 0, 0, tiled=True).reshape(value.shape)

    def add_over_y(shares):
        total = shares[0]
        for j in (2, 1, 3):
            total = total + along(shares[j], j).astype(F32)
        return total

    def from_y(value):
        return [value] + [along(value, quarters - j) for j in range(1, quarters)]

    gate_own, up_own, down_own = w_gate[0], w_up[0], w_down[0]
    gate_other, up_other, down_other = to_partner(gate_own), to_partner(up_own), to_partner(down_own)
    routes, route_weight = routes.T, route_weight.T

    sent, sel, wsel = prep(core, routes, route_weight, tokens, grad_out, quarters, experts)
    recv = exchange(sent)
    down = (down_own, down_other)
    *shares, x_own, x_other, recv = projection(gate_kernel, "gate", at, (recv,), (gate_own, gate_other), 0, slots, quarters)
    gate = add_over_y(shares)
    shares = projection(up_kernel, "up", at, (x_own, x_other), (up_own, up_other), 0, slots, quarters)
    up = add_over_y(shares)
    *shares, d_own, d_other = projection(back_kernel, "back", at, (recv,), down, 1, slots, quarters)
    back = add_over_y(shares)

    sig = jax.nn.sigmoid(gate)
    smooth = gate * sig
    slope = up * (sig * (1.0 + gate * (1.0 - sig)))
    mine, smooth, slope = lax.optimization_barrier(((smooth * up).astype(BF16), smooth, slope))
    h_parts = from_y(mine)
    back, h_parts = lax.optimization_barrier((back, h_parts))
    g_parts = from_y(jnp.concatenate([(back * slope).astype(BF16), (back * smooth).astype(BF16)], axis=1))
    main, h_mine = out_rows(at, h_parts, down, lanes)
    packed, g_mine = grad_rows(at, g_parts, main, (gate_own, gate_other, up_own, up_other))
    x_other, d_other, h_mine, g_mine = lax.optimization_barrier((x_other, d_other, h_mine, g_mine))
    returned = exchange(packed)

    x_partner, d_partner, h_partner = to_partner(x_other), to_partner(d_other), to_partner(h_mine)
    g_partner = to_partner(g_mine)
    step = hidden // 4
    grad_down = weight_grad(h_mine, h_partner, d_own, d_partner, half)
    grad_gate = weight_grad(x_own, x_partner, g_mine, g_partner, step, 0, hidden)
    grad_up = weight_grad(x_own, x_partner, g_mine, g_partner, step, 4, hidden)
    returned, grad_gate, grad_up, grad_down = lax.optimization_barrier((returned, grad_gate, grad_up, grad_down))

    moe_out, grad_tokens, grad_route = last(core, routes, sel, wsel, returned, grad_out)
    return (moe_out, grad_tokens, grad_route.T, grad_gate[None], grad_up[None], grad_down[None])


def solution(mesh):
    ctx, head = mesh.shape["ctx"], mesh.shape["head"]
    side = int(round(ctx**0.5))
    fine = Mesh(mesh.devices.reshape(side, ctx // side, head // 2, 2), ("x", "z", "y", "k"))
    e, d, both = ("x", "z"), ("y", "k"), ("x", "z", "y", "k")
    rows = P(both, None)
    up, down = P(e, d, None), P(e, None, d)
    return jax.shard_map(
        on_device,
        mesh=fine,
        in_specs=(rows, rows, rows, up, up, down, rows),
        out_specs=(rows, rows, rows, up, up, down),
        check_vma=False,
    )
```

time: 199 us -> 177 us (0.89)
  waiting for transfers between devices: 97.6 us -> 80 us
  starting transfers between devices: 29.1 us -> 45 us
  local copies, waits for them, and re-layouts: 18.9 us -> 4.17 us
  matrix products: 10.4 us -> 0 us
  Pallas kernels: 38 us -> 45.9 us
  other arithmetic: 3.83 us -> 0.54 us
    ppermute x6 -> x15, waiting for transfers between devices: 46.3 us -> 21.4 us  [along(): lax.ppermute(value, 'y', [(i, (i + shift) % quarters) for i in range(quar...]
    ppermute x6 -> x15, starting transfers between devices: 5.23 us -> 20 us  [along(): lax.ppermute(value, 'y', [(i, (i + shift) % quarters) for i in range(quar...]
    unnamed x31 -> x18, local copies, waits for them, and re-layouts: 15.6 us -> 4.17 us
    dot_general x3 -> x0, matrix products: 10.4 us -> none  [dot(): lax.dot_general(a, b, (((ca,), (cb,)), ((), ())), preferred_element_type=...]
    pallas_call x2 -> x8, Pallas kernels: 24.9 us -> 34 us  [the longest x3 12.2 us: projection(): pl.pallas_call(kernel, in_specs=in_specs, out_specs=out_specs, out_shape=...]
    all_to_all x2, waiting for transfers between devices: 42.5 us -> 50.5 us  [exchange(): return lax.all_to_all(flat, everyone, 0, 0, tiled=True).reshape(value.shape)]
    squeeze x2 -> x0, local copies, waits for them, and re-layouts: 2.49 us -> none  [on_device(): d_all = jnp.concatenate([rows_own[1], rows_partner[1]], axis=0)]
    ppermute x8 -> x7, waiting for transfers between devices: 8.78 us -> 8.17 us  [to_partner(): return lax.ppermute(value, 'k', [(0, 1), (1, 0)])]
  transfers between devices with their start and end apart: 16 -> 24, of which waited for: 10 -> 13; matrix products, arithmetic and copies ran while one was open for 11% -> 0% of each run, Pallas kernels for 6% -> 15%
where the time goes in v2:
time: 177 us
  waiting for transfers between devices  80 us (45%)
  Pallas kernels  45.9 us (26%)
  starting transfers between devices  45 us (25%)
  local copies, waits for them, and re-layouts  4.17 us (2%)
    all_to_all x2, waiting for transfers between devices, exchange(): return lax.all_to_all(flat, everyone, 0, 0, tiled=True).reshape(value.shape)  50.5 us
    all_to_all x2, starting transfers between devices, exchange(): return lax.all_to_all(flat, everyone, 0, 0, tiled=True).reshape(value.shape)  23.3 us
    ppermute x15, waiting for transfers between devices, along(): lax.ppermute(value, 'y', [(i, (i + shift) % quarters) for i in range(quar...  21.4 us
    ppermute x15, starting transfers between devices, along(): lax.ppermute(value, 'y', [(i, (i + shift) % quarters) for i in range(quar...  20 us
    pallas_call x3, Pallas kernels, projection(): pl.pallas_call(kernel, in_specs=in_specs, out_specs=out_specs, out_shape=...  12.2 us
    pallas_call x3, Pallas kernels, weight_grad(): pl.pallas_call(weight_kernel, grid=(columns // step,), in_specs=[a_spec,...  11 us
    ppermute x7, waiting for transfers between devices, to_partner(): return lax.ppermute(value, 'k', [(0, 1), (1, 0)])  8.17 us
    pallas_call x1, Pallas kernels, grad_rows(): pl.pallas_call(grad_kernel, in_specs=[smem()] + [whole()] * (quarters + 5...  6.85 us
  transfers between devices with their start and end apart: 24, of which 13 were waited for; matrix products, arithmetic and copies ran while one was open for 0% of the time, Pallas kernels for 15%

profile of v2, /device:TPU:0, one launch (start us, length us, event | category | flops | bytes accessed | tf_op | source)
XLA Modules:
  0.0 176.7 jit_solution(2908756669090247279)
XLA Ops:
  0.6 5.5 %prep.1 = (bf16[4,128,2688]{2,1,0:T(8,128)(2,1)}, bf16[4,128,128]{2,1,0:T(8,128)(2,1)}, bf16[2,128,128]{2,1,0:T(8,128)(2,1)}) custom-call(s32[1]{0:T(128)} %bitcast.core_ref, s32[8,128]{1,0:T(8,128)} %bitcast.30, f32[8,128]{1,0:T(8,128)} %bitcast.29, bf16[128,7168]{1,0:T(8,128)(2,1)} %tok_ref.1, bf16[128,7168]{1,0:T(8,128)(2,1)} %go_ref.3), custom_call_target="tpu_custom_call" | custom-call | flops 800000000 | bytes 6500000 | tf_op jit(solution)/shard_map/prep/pallas_call | solution.py:97
  6.1 11.5 %all-to-all-start = ((bf16[64,8,2688]{2,1,0:T(8,128)(2,1)}), bf16[64,8,2688]{2,1,0:T(8,128)(2,1)S(1)}, u32[]{:S(2)}, u32[]{:S(2)}) async-start(bf16[64,8,2688]{2,1,0:T(8,128)(2,1)} %bitcast.26), calls=%async_computation | async-start | bytes 5505024 | tf_op jit(solution)/shard_map/all_to_all | solution.py:393
  17.6 0.1 collective-permute-start
  17.7 0.5 collective-permute-start.8
  18.2 0.1 collective-permute-start.1
  18.3 3.5 %collective-permute-done.wx_ref.gx_ref = bf16[896,1024]{1,0:T(8,128)(2,1)} collective-permute-done((bf16[896,1024]{1,0:T(8,128)(2,1)}, bf16[896,1024]{1,0:T(8,128)(2,1)}, u32[]{:S(2)}, u32[]{:S(2)}) %collective-permute-start) | collective-permute-done | bytes 1835040 | tf_op jit(solution)/shard_map/ppermute | solution.py:386
  21.8 32.2 %all-to-all-done = bf16[64,8,2688]{2,1,0:T(8,128)(2,1)S(1)} async-done(((bf16[64,8,2688]{2,1,0:T(8,128)(2,1)}), bf16[64,8,2688]{2,1,0:T(8,128)(2,1)S(1)}, u32[]{:S(2)}, u32[]{:S(2)}) %all-to-all-start) | async-done | bytes 2752544 | tf_op jit(solution)/shard_map/all_to_all | solution.py:393
  54.0 1.5 copy-done.2
  55.5 4.3 %gate.1 = (f32[96,1024]{1,0:T(8,128)S(1)}, bf16[96,1024]{1,0:T(8,128)(2,1)S(1)}, bf16[96,1024]{1,0:T(8,128)(2,1)S(1)}, bf16[96,1024]{1,0:T(8,128)(2,1)S(1)}, bf1...) custom-call(s32[1]{0:T(128)} %bitcast.3.at_ref, ...), custom_call_target="tpu_custom_call", output_to_operand_aliasing={{6}: (1, {})} | custom-call | flops 3000000000 | bytes 8000000 | tf_op jit(solution)/shard_map/gate/pallas_call | solution.py:198
  59.9 0.9 collective-permute-start.5
  60.9 1.3 collective-permute-start.6
  62.1 2.0 %collective-permute-start.7 = (bf16[96,1024]{1,0:T(8,128)(2,1)S(1)}, bf16[96,1024]{1,0:T(8,128)(2,1)S(1)}, u32[]{:S(2)}, u32[]{:S(2)}) collective-permute-start(bf16[96,1024]{1,0:T(8,128)(2,1)S(1)} %get-tuple-element.60), channel_id=1, source_target_pairs={{0,6},{2,0},{4,2},{6,4},{1,7},{3,1},{5,3},{7,5},{8,14},{10,8},{12,... | collective-permute-start | bytes 589832 | tf_op jit(solution)/shard_map/ppermute | solution.py:389
  64.1 3.6 %up.1 = (f32[96,1024]{1,0:T(8,128)S(1)}, bf16[96,1024]{1,0:T(8,128)(2,1)S(1)}, bf16[96,1024]{1,0:T(8,128)(2,1)S(1)}, bf16[96,1024]{1,0:T(8,128)(2,1)S(1)}) custom-call(s32[1]{0:T(128)} %bitcast.3.at_ref, bf16[384,896]{1,0:T(8,128)(2,1)S(1)} %get-tuple-element.61.own_ref.am_ref, bf16[384,896]{1,0:T(8,128)(2,1)S(1)} %get-tuple-element.80.other_ref, ...), custom_call_target="tpu_custom_call" | custom-call | flops 3000000000 | bytes 8000000 | tf_op jit(solution)/shard_map/up/pallas_call | solution.py:198
  67.7 1.5 collective-permute-start.9
  69.3 3.2 %collective-permute-start.11 = (bf16[96,1024]{1,0:T(8,128)(2,1)S(1)}, bf16[96,1024]{1,0:T(8,128)(2,1)S(1)}, u32[]{:S(2)}, u32[]{:S(2)}) collective-permute-start(bf16[96,1024]{1,0:T(8,128)(2,1)S(1)} %get-tuple-element.66), channel_id=1, source_target_pairs={{0,6},{2,0},{4,2},{6,4},{1,7},{3,1},{5,3},{7,5},{8,14},{10,8},{12,... | collective-permute-start | bytes 589832 | tf_op jit(solution)/shard_map/ppermute | solution.py:389
  72.5 4.3 %back.1 = (f32[96,1024]{1,0:T(8,128)S(1)}, bf16[96,1024]{1,0:T(8,128)(2,1)S(1)}, bf16[96,1024]{1,0:T(8,128)(2,1)S(1)}, bf16[96,1024]{1,0:T(8,128)(2,1)S(1)}, bf1...) custom-call(s32[1]{0:T(128)} %bitcast.3.at_ref, bf16[4,128,2688]{2,1,0:T(8,128)(2,1)S(1)} %get-tuple-element.52.recv_ref, ...), custom_call_target="tpu_custom_call" | custom-call | flops 3000000000 | bytes 8000000 | tf_op jit(solution)/shard_map/back/pallas_call | solution.py:198
  76.8 0.9 collective-permute-start.2
  77.8 3.2 %collective-permute-start.4 = (bf16[96,1024]{1,0:T(8,128)(2,1)S(1)}, bf16[96,1024]{1,0:T(8,128)(2,1)S(1)}, u32[]{:S(2)}, u32[]{:S(2)}) collective-permute-start(bf16[96,1024]{1,0:T(8,128)(2,1)S(1)} %get-tuple-element.56), channel_id=1, source_target_pairs={{0,6},{2,0},{4,2},{6,4},{1,7},{3,1},{5,3},{7,5},{8,14},{10,8},{12,... | collective-permute-start | bytes 589832 | tf_op jit(solution)/shard_map/ppermute | solution.py:389
  81.0 0.7 collective-permute-done.10
  81.8 0.3 multiply_convert_fusion.2
  82.1 1.7 collective-permute-start.14
  83.8 1.0 collective-permute-start.13
  84.8 1.4 collective-permute-done.2
  86.3 0.3 collective-permute-start.12
  86.6 3.3 %collective-permute-done.3 = bf16[96,1024]{1,0:T(8,128)(2,1)S(1)} collective-permute-done((bf16[96,1024]{1,0:T(8,128)(2,1)S(1)}, bf16[96,1024]{1,0:T(8,128)(2,1)S(1)}, u32[]{:S(2)}, u32[]{:S(2)}) %collective-permute-start.3) | collective-permute-done | bytes 196640 | tf_op jit(solution)/shard_map/ppermute | solution.py:389
  89.9 0.3 collective-permute-done.4
  90.2 0.1 convert_add_fusion.2
  90.3 2.9 %collective-permute-done.14.h3 = bf16[96,1024]{1,0:T(8,128)(2,1)S(1)} collective-permute-done((bf16[96,1024]{1,0:T(8,128)(2,1)S(1)}, bf16[96,1024]{1,0:T(8,128)(2,1)S(1)}, u32[]{:S(2)}, u32[]{:S(2)}) %collective-permute-start.14) | collective-permute-done | bytes 196640 | tf_op jit(solution)/shard_map/ppermute | solution.py:389
  93.1 2.2 %collective-permute-done.13.h2 = bf16[96,1024]{1,0:T(8,128)(2,1)S(1)} collective-permute-done((bf16[96,1024]{1,0:T(8,128)(2,1)S(1)}, bf16[96,1024]{1,0:T(8,128)(2,1)S(1)}, u32[]{:S(2)}, u32[]{:S(2)}) %collective-permute-start.13) | collective-permute-done | bytes 196640 | tf_op jit(solution)/shard_map/ppermute | solution.py:389
  95.4 0.5 collective-permute-start.17
  95.9 2.4 %collective-permute-start.16 = (bf16[96,2048]{1,0:T(8,128)(2,1)S(1)}, bf16[96,2048]{1,0:T(8,128)(2,1)S(1)}, u32[]{:S(2)}, u32[]{:S(2)}) collective-permute-start(bf16[96,2048]{1,0:T(8,128)(2,1)S(1)} %pad_maximum_fusion.g0), channel_id=1, source_target_pairs={{0,4},{2,6},{4,0},{6,2},{1,5},{3,7},{5,1},{7,3},{8,12},{10,14},{12... | collective-permute-start | bytes 1179656 | tf_op jit(solution)/shard_map/ppermute | solution.py:389
  98.3 0.9 collective-permute-start.15
  99.3 3.9 %out_rows.1 = (bf16[4,128,1792]{2,1,0:T(8,128)(2,1)S(1)}, bf16[384,1024]{1,0:T(8,128)(2,1)S(1)}) custom-call(s32[1]{0:T(128)} %bitcast.3.at_ref, bf16[96,1024]{1,0:T(8,128)(2,1)S(1)} %get-tuple-element.71.h0, bf16[96,1024]{1,0:T(8,128)(2,1)S(1)} %collective-permute-done.12.h1, bf16[96,1024]{1,0:T(8,128)(2,1)S(1)} %collective-permute-done.13.h2, ...), custom_call_target="tpu_custom_call" | custom-call | flops 2000000000 | bytes 7500000 | tf_op jit(solution)/shard_map/out_rows/pallas_call | solution.py:237
  103.2 3.4 %collective-permute-done.17.g3 = bf16[96,2048]{1,0:T(8,128)(2,1)S(1)} collective-permute-done((bf16[96,2048]{1,0:T(8,128)(2,1)S(1)}, bf16[96,2048]{1,0:T(8,128)(2,1)S(1)}, u32[]{:S(2)}, u32[]{:S(2)}) %collective-permute-start.17) | collective-permute-done | bytes 393248 | tf_op jit(solution)/shard_map/ppermute | solution.py:389
  106.6 7.2 %collective-permute-done.16.g2 = bf16[96,2048]{1,0:T(8,128)(2,1)S(1)} collective-permute-done((bf16[96,2048]{1,0:T(8,128)(2,1)S(1)}, bf16[96,2048]{1,0:T(8,128)(2,1)S(1)}, u32[]{:S(2)}, u32[]{:S(2)}) %collective-permute-start.16) | collective-permute-done | bytes 393248 | tf_op jit(solution)/shard_map/ppermute | solution.py:389
  113.8 6.9 %grad_rows.1 = (bf16[4,128,2688]{2,1,0:T(8,128)(2,1)S(1)}, bf16[384,2048]{1,0:T(8,128)(2,1)S(1)}) custom-call(s32[1]{0:T(128)} %bitcast.3.at_ref, bf16[96,2048]{1,0:T(8,128)(2,1)S(1)} %pad_maximum_fusion.g0, bf16[96,2048]{1,0:T(8,128)(2,1)S(1)} %collective-permute-done.15.g1, bf16[96,2048]{1,0:T(8,128)(2,1)S(1)} %collective-permute-done.16.g2, ...), custom_call_target="tpu_custom_call" | custom-call | flops 3500000000 | bytes 14000000 | tf_op jit(solution)/shard_map/grad_rows/pallas_call | solution.py:283
  120.7 1.5 copy-done
  122.2 11.8 %all-to-all-start.1 = ((bf16[64,8,2688]{2,1,0:T(8,128)(2,1)}), bf16[64,8,2688]{2,1,0:T(8,128)(2,1)}, u32[]{:S(2)}, u32[]{:S(2)}) async-start(bf16[64,8,2688]{2,1,0:T(8,128)(2,1)} %bitcast.15), calls=%async_computation.1 | async-start | bytes 5505024 | tf_op jit(solution)/shard_map/all_to_all | solution.py:393
  134.1 0.5 collective-permute-start.20
  134.6 0.1 collective-permute-start.21
  134.7 0.4 collective-permute-start.18
  135.1 4.6 %collective-permute-done.21.bp_ref = bf16[384,896]{1,0:T(8,128)(2,1)S(1)} collective-permute-done((bf16[384,896]{1,0:T(8,128)(2,1)}, bf16[384,896]{1,0:T(8,128)(2,1)S(1)}, u32[]{:S(2)}, u32[]{:S(2)}) %collective-permute-start.21) | collective-permute-done | bytes 688160 | tf_op jit(solution)/shard_map/ppermute | solution.py:386
  139.7 1.1 copy-done.8
  140.8 3.5 %weight_grad.5 = bf16[1024,896]{1,0:T(8,128)(2,1)} custom-call(bf16[384,1024]{1,0:T(8,128)(2,1)S(1)} %get-tuple-element.82.am_ref, bf16[384,1024]{1,0:T(8,128)(2,1)S(1)} %collective-permute-done.20.ap_ref, bf16[384,896]{1,0:T(8,128)(2,1)S(1)} %copy-done.8, bf16[384,896]{1,0:T(8,128)(2,1)S(1)} %collective-permute-done.21.bp_ref), custom_call_target="tpu_custom_call" | custom-call | flops 1500000000 | bytes 5000000 | tf_op jit(solution)/shard_map/weight_grad/pallas_call | solution.py:310
  144.3 3.8 %weight_grad.4 = bf16[896,1024]{1,0:T(8,128)(2,1)} custom-call(bf16[384,896]{1,0:T(8,128)(2,1)S(1)} %get-tuple-element.61.own_ref.am_ref, bf16[384,896]{1,0:T(8,128)(2,1)S(1)} %collective-permute-done.18.ap_ref, bf16[384,2048]{1,0:T(8,128)(2,1)S(1)} %get-tuple-element.81.bm_ref, bf16[384,2048]{1,0:T(8,128)(2,1)S(1)} %collective-permute-done.19.bp_ref), custom_call_target="tpu_custom_call" | custom-call | flops 1500000000 | bytes 5000000 | tf_op jit(solution)/shard_map/weight_grad/pallas_call | solution.py:310
  148.1 3.7 %weight_grad.3 = bf16[896,1024]{1,0:T(8,128)(2,1)} custom-call(bf16[384,896]{1,0:T(8,128)(2,1)S(1)} %get-tuple-element.61.own_ref.am_ref, bf16[384,896]{1,0:T(8,128)(2,1)S(1)} %collective-permute-done.18.ap_ref, bf16[384,2048]{1,0:T(8,128)(2,1)S(1)} %get-tuple-element.81.bm_ref, bf16[384,2048]{1,0:T(8,128)(2,1)S(1)} %collective-permute-done.19.bp_ref), custom_call_target="tpu_custom_call" | custom-call | flops 1500000000 | bytes 5000000 | tf_op jit(solution)/shard_map/weight_grad/pallas_call | solution.py:310
  151.8 18.3 %all-to-all-done.1 = bf16[64,8,2688]{2,1,0:T(8,128)(2,1)} async-done(((bf16[64,8,2688]{2,1,0:T(8,128)(2,1)}), bf16[64,8,2688]{2,1,0:T(8,128)(2,1)}, u32[]{:S(2)}, u32[]{:S(2)}) %all-to-all-start.1) | async-done | bytes 2752544 | tf_op jit(solution)/shard_map/all_to_all | solution.py:393
  170.1 6.5 %last.1 = (bf16[128,7168]{1,0:T(8,128)(2,1)}, bf16[128,7168]{1,0:T(8,128)(2,1)}, f32[8,128]{1,0:T(8,128)}) custom-call(s32[1]{0:T(128)} %bitcast.core_ref, s32[8,128]{1,0:T(8,128)} %bitcast.31, bf16[4,128,128]{2,1,0:T(8,128)(2,1)} %get-tuple-element.49.sel_ref, bf16[2,128,128]{2,1,0:T(8,128)(2,1)} %get-tuple-element.50.wsel_ref, ...), custom_call_target="tpu_custom_call" | custom-call | flops 1500000000 | bytes 8500000 | tf_op jit(solution)/shard_map/last/pallas_call | solution.py:357
  (32 shorter events, 0.4 us)
Async XLA Ops:
  6.1 47.9 %all-to-all-start = ((bf16[64,8,2688]{2,1,0:T(8,128)(2,1)}), bf16[64,8,2688]{2,1,0:T(8,128)(2,1)S(1)}, u32[]{:S(2)}, u32[]{:S(2)}) async-start(bf16[64,8,2688]{2,1,0:T(8,128)(2,1)} %bitcast.26), calls=%async_computation | async-start | bytes 5505024 | tf_op jit(solution)/shard_map/all_to_all | solution.py:393
  17.6 4.2 %collective-permute-start = (bf16[896,1024]{1,0:T(8,128)(2,1)}, bf16[896,1024]{1,0:T(8,128)(2,1)}, u32[]{:S(2)}, u32[]{:S(2)}) collective-permute-start(bf16[896,1024]{1,0:T(8,128)(2,1)} %bitcast.20), channel_id=1, source_target_pairs={{0,1},{1,0},{2,3},{3,2},{4,5},{5,4},{6,7},{7,6},{8,9},{9,8},{10,11... | collective-permute-start | bytes 5505032 | tf_op jit(solution)/shard_map/ppermute | solution.py:386
  17.7 46.4 %collective-permute-start.8 = (bf16[896,1024]{1,0:T(8,128)(2,1)}, bf16[896,1024]{1,0:T(8,128)(2,1)}, u32[]{:S(2)}, u32[]{:S(2)}) collective-permute-start(bf16[896,1024]{1,0:T(8,128)(2,1)} %bitcast.23), channel_id=1, source_target_pairs={{0,1},{1,0},{2,3},{3,2},{4,5},{5,4},{6,7},{7,6},{8,9},{9,8},{10,11... | collective-permute-start | bytes 5505032 | tf_op jit(solution)/shard_map/ppermute | solution.py:386
  18.2 51.0 %collective-permute-start.1 = (bf16[1024,896]{1,0:T(8,128)(2,1)}, bf16[1024,896]{1,0:T(8,128)(2,1)}, u32[]{:S(2)}, u32[]{:S(2)}) collective-permute-start(bf16[1024,896]{1,0:T(8,128)(2,1)} %bitcast.17), channel_id=1, source_target_pairs={{0,1},{1,0},{2,3},{3,2},{4,5},{5,4},{6,7},{7,6},{8,9},{9,8},{10,11... | collective-permute-start | bytes 5505032 | tf_op jit(solution)/shard_map/ppermute | solution.py:386
  54.0 1.5 copy-start.2
  55.5 8.6 %copy-start.4 = (bf16[1,896,1024]{2,1,0:T(8,128)(2,1)S(1)}, bf16[1,896,1024]{2,1,0:T(8,128)(2,1)}, u32[]{:S(2)}) copy-start(bf16[1,896,1024]{2,1,0:T(8,128)(2,1)} %param.11) | copy-start | bytes 5505028
  59.9 7.8 %copy-start.5 = (bf16[384,896]{1,0:T(8,128)(2,1)}, bf16[384,896]{1,0:T(8,128)(2,1)S(1)}, u32[]{:S(2)}) copy-start(bf16[384,896]{1,0:T(8,128)(2,1)S(1)} %get-tuple-element.80.other_ref) | copy-start | bytes 2064388
  59.9 9.3 %collective-permute-start.5 = (bf16[96,1024]{1,0:T(8,128)(2,1)S(1)}, bf16[96,1024]{1,0:T(8,128)(2,1)S(1)}, u32[]{:S(2)}, u32[]{:S(2)}) collective-permute-start(bf16[96,1024]{1,0:T(8,128)(2,1)S(1)} %get-tuple-element.58), channel_id=1, source_target_pairs={{0,4},{2,6},{4,0},{6,2},{1,5},{3,7},{5,1},{7,3},{8,12},{10,14},{12... | collective-permute-start | bytes 589832 | tf_op jit(solution)/shard_map/ppermute | solution.py:389
  60.9 16.0 %collective-permute-start.6 = (bf16[96,1024]{1,0:T(8,128)(2,1)S(1)}, bf16[96,1024]{1,0:T(8,128)(2,1)S(1)}, u32[]{:S(2)}, u32[]{:S(2)}) collective-permute-start(bf16[96,1024]{1,0:T(8,128)(2,1)S(1)} %get-tuple-element.59), channel_id=1, source_target_pairs={{0,2},{2,4},{4,6},{6,0},{1,3},{3,5},{5,7},{7,1},{8,10},{10,12},{12... | collective-permute-start | bytes 589832 | tf_op jit(solution)/shard_map/ppermute | solution.py:389
  62.1 15.7 %collective-permute-start.7 = (bf16[96,1024]{1,0:T(8,128)(2,1)S(1)}, bf16[96,1024]{1,0:T(8,128)(2,1)S(1)}, u32[]{:S(2)}, u32[]{:S(2)}) collective-permute-start(bf16[96,1024]{1,0:T(8,128)(2,1)S(1)} %get-tuple-element.60), channel_id=1, source_target_pairs={{0,6},{2,0},{4,2},{6,4},{1,7},{3,1},{5,3},{7,5},{8,14},{10,8},{12,... | collective-permute-start | bytes 589832 | tf_op jit(solution)/shard_map/ppermute | solution.py:389
  64.1 8.4 %copy-start.1 = (bf16[1,1024,896]{2,1,0:T(8,128)(2,1)S(1)}, bf16[1,1024,896]{2,1,0:T(8,128)(2,1)}, u32[]{:S(2)}) copy-start(bf16[1,1024,896]{2,1,0:T(8,128)(2,1)} %param.12) | copy-start | bytes 5505028
  67.7 10.1 %collective-permute-start.9 = (bf16[96,1024]{1,0:T(8,128)(2,1)S(1)}, bf16[96,1024]{1,0:T(8,128)(2,1)S(1)}, u32[]{:S(2)}, u32[]{:S(2)}) collective-permute-start(bf16[96,1024]{1,0:T(8,128)(2,1)S(1)} %get-tuple-element.64), channel_id=1, source_target_pairs={{0,4},{2,6},{4,0},{6,2},{1,5},{3,7},{5,1},{7,3},{8,12},{10,14},{12... | collective-permute-start | bytes 589832 | tf_op jit(solution)/shard_map/ppermute | solution.py:389
  69.2 12.5 %collective-permute-start.10 = (bf16[96,1024]{1,0:T(8,128)(2,1)S(1)}, bf16[96,1024]{1,0:T(8,128)(2,1)S(1)}, u32[]{:S(2)}, u32[]{:S(2)}) collective-permute-start(bf16[96,1024]{1,0:T(8,128)(2,1)S(1)} %get-tuple-element.65), channel_id=1, source_target_pairs={{0,2},{2,4},{4,6},{6,0},{1,3},{3,5},{5,7},{7,1},{8,10},{10,12},{12... | collective-permute-start | bytes 589832 | tf_op jit(solution)/shard_map/ppermute | solution.py:389
  69.3 12.5 %collective-permute-start.11 = (bf16[96,1024]{1,0:T(8,128)(2,1)S(1)}, bf16[96,1024]{1,0:T(8,128)(2,1)S(1)}, u32[]{:S(2)}, u32[]{:S(2)}) collective-permute-start(bf16[96,1024]{1,0:T(8,128)(2,1)S(1)} %get-tuple-element.66), channel_id=1, source_target_pairs={{0,6},{2,0},{4,2},{6,4},{1,7},{3,1},{5,3},{7,5},{8,14},{10,8},{12,... | collective-permute-start | bytes 589832 | tf_op jit(solution)/shard_map/ppermute | solution.py:389
  76.8 13.5 %copy-start.6 = (bf16[384,896]{1,0:T(8,128)(2,1)}, bf16[384,896]{1,0:T(8,128)(2,1)S(1)}, u32[]{:S(2)}) copy-start(bf16[384,896]{1,0:T(8,128)(2,1)S(1)} %get-tuple-element.84) | copy-start | bytes 2064388
  76.8 13.5 %copy-start.7 = (bf16[384,896]{1,0:T(8,128)(2,1)}, bf16[384,896]{1,0:T(8,128)(2,1)S(1)}, u32[]{:S(2)}) copy-start(bf16[384,896]{1,0:T(8,128)(2,1)S(1)} %get-tuple-element.83.bm_ref) | copy-start | bytes 2064388
  76.8 9.4 %collective-permute-start.2 = (bf16[96,1024]{1,0:T(8,128)(2,1)S(1)}, bf16[96,1024]{1,0:T(8,128)(2,1)S(1)}, u32[]{:S(2)}, u32[]{:S(2)}) collective-permute-start(bf16[96,1024]{1,0:T(8,128)(2,1)S(1)} %get-tuple-element.54), channel_id=1, source_target_pairs={{0,4},{2,6},{4,0},{6,2},{1,5},{3,7},{5,1},{7,3},{8,12},{10,14},{12... | collective-permute-start | bytes 589832 | tf_op jit(solution)/shard_map/ppermute | solution.py:389
  77.8 12.1 %collective-permute-start.3 = (bf16[96,1024]{1,0:T(8,128)(2,1)S(1)}, bf16[96,1024]{1,0:T(8,128)(2,1)S(1)}, u32[]{:S(2)}, u32[]{:S(2)}) collective-permute-start(bf16[96,1024]{1,0:T(8,128)(2,1)S(1)} %get-tuple-element.55), channel_id=1, source_target_pairs={{0,2},{2,4},{4,6},{6,0},{1,3},{3,5},{5,7},{7,1},{8,10},{10,12},{12... | collective-permute-start | bytes 589832 | tf_op jit(solution)/shard_map/ppermute | solution.py:389
  77.8 12.3 %collective-permute-start.4 = (bf16[96,1024]{1,0:T(8,128)(2,1)S(1)}, bf16[96,1024]{1,0:T(8,128)(2,1)S(1)}, u32[]{:S(2)}, u32[]{:S(2)}) collective-permute-start(bf16[96,1024]{1,0:T(8,128)(2,1)S(1)} %get-tuple-element.56), channel_id=1, source_target_pairs={{0,6},{2,0},{4,2},{6,4},{1,7},{3,1},{5,3},{7,5},{8,14},{10,8},{12,... | collective-permute-start | bytes 589832 | tf_op jit(solution)/shard_map/ppermute | solution.py:389
  82.1 11.0 %collective-permute-start.14 = (bf16[96,1024]{1,0:T(8,128)(2,1)S(1)}, bf16[96,1024]{1,0:T(8,128)(2,1)S(1)}, u32[]{:S(2)}, u32[]{:S(2)}) collective-permute-start(bf16[96,1024]{1,0:T(8,128)(2,1)S(1)} %get-tuple-element.71.h0), channel_id=1, source_target_pairs={{0,2},{2,4},{4,6},{6,0},{1,3},{3,5},{5,7},{7,1},{8,10},{10,12},{12... | collective-permute-start | bytes 589832 | tf_op jit(solution)/shard_map/ppermute | solution.py:389
  83.8 11.5 %collective-permute-start.13 = (bf16[96,1024]{1,0:T(8,128)(2,1)S(1)}, bf16[96,1024]{1,0:T(8,128)(2,1)S(1)}, u32[]{:S(2)}, u32[]{:S(2)}) collective-permute-start(bf16[96,1024]{1,0:T(8,128)(2,1)S(1)} %get-tuple-element.71.h0), channel_id=1, source_target_pairs={{0,4},{2,6},{4,0},{6,2},{1,5},{3,7},{5,1},{7,3},{8,12},{10,14},{12... | collective-permute-start | bytes 589832 | tf_op jit(solution)/shard_map/ppermute | solution.py:389
  86.3 9.0 %collective-permute-start.12 = (bf16[96,1024]{1,0:T(8,128)(2,1)S(1)}, bf16[96,1024]{1,0:T(8,128)(2,1)S(1)}, u32[]{:S(2)}, u32[]{:S(2)}) collective-permute-start(bf16[96,1024]{1,0:T(8,128)(2,1)S(1)} %get-tuple-element.71.h0), channel_id=1, source_target_pairs={{0,6},{2,0},{4,2},{6,4},{1,7},{3,1},{5,3},{7,5},{8,14},{10,8},{12,... | collective-permute-start | bytes 589832 | tf_op jit(solution)/shard_map/ppermute | solution.py:389
  95.4 18.4 %copy-start.3 = (bf16[1,896,1024]{2,1,0:T(8,128)(2,1)S(1)}, bf16[1,896,1024]{2,1,0:T(8,128)(2,1)}, u32[]{:S(2)}) copy-start(bf16[1,896,1024]{2,1,0:T(8,128)(2,1)} %param.10) | copy-start | bytes 5505028
  95.4 11.2 %collective-permute-start.17 = (bf16[96,2048]{1,0:T(8,128)(2,1)S(1)}, bf16[96,2048]{1,0:T(8,128)(2,1)S(1)}, u32[]{:S(2)}, u32[]{:S(2)}) collective-permute-start(bf16[96,2048]{1,0:T(8,128)(2,1)S(1)} %pad_maximum_fusion.g0), channel_id=1, source_target_pairs={{0,2},{2,4},{4,6},{6,0},{1,3},{3,5},{5,7},{7,1},{8,10},{10,12},{12... | collective-permute-start | bytes 1179656 | tf_op jit(solution)/shard_map/ppermute | solution.py:389
  95.9 17.9 %collective-permute-start.16 = (bf16[96,2048]{1,0:T(8,128)(2,1)S(1)}, bf16[96,2048]{1,0:T(8,128)(2,1)S(1)}, u32[]{:S(2)}, u32[]{:S(2)}) collective-permute-start(bf16[96,2048]{1,0:T(8,128)(2,1)S(1)} %pad_maximum_fusion.g0), channel_id=1, source_target_pairs={{0,4},{2,6},{4,0},{6,2},{1,5},{3,7},{5,1},{7,3},{8,12},{10,14},{12... | collective-permute-start | bytes 1179656 | tf_op jit(solution)/shard_map/ppermute | solution.py:389
  98.3 15.5 %collective-permute-start.15 = (bf16[96,2048]{1,0:T(8,128)(2,1)S(1)}, bf16[96,2048]{1,0:T(8,128)(2,1)S(1)}, u32[]{:S(2)}, u32[]{:S(2)}) collective-permute-start(bf16[96,2048]{1,0:T(8,128)(2,1)S(1)} %pad_maximum_fusion.g0), channel_id=1, source_target_pairs={{0,6},{2,0},{4,2},{6,4},{1,7},{3,1},{5,3},{7,5},{8,14},{10,8},{12,... | collective-permute-start | bytes 1179656 | tf_op jit(solution)/shard_map/ppermute | solution.py:389
  120.7 1.5 copy-start
  122.2 47.9 %all-to-all-start.1 = ((bf16[64,8,2688]{2,1,0:T(8,128)(2,1)}), bf16[64,8,2688]{2,1,0:T(8,128)(2,1)}, u32[]{:S(2)}, u32[]{:S(2)}) async-start(bf16[64,8,2688]{2,1,0:T(8,128)(2,1)} %bitcast.15), calls=%async_computation.1 | async-start | bytes 5505024 | tf_op jit(solution)/shard_map/all_to_all | solution.py:393
  134.0 10.3 %collective-permute-start.19 = (bf16[384,2048]{1,0:T(8,128)(2,1)S(1)}, bf16[384,2048]{1,0:T(8,128)(2,1)S(1)}, u32[]{:S(2)}, u32[]{:S(2)}) collective-permute-start(bf16[384,2048]{1,0:T(8,128)(2,1)S(1)} %get-tuple-element.81.bm_ref), channel_id=1, source_target_pairs={{0,1},{1,0},{2,3},{3,2},{4,5},{5,4},{6,7},{7,6},{8,9},{9,8},{10,11... | collective-permute-start | bytes 4718600 | tf_op jit(solution)/shard_map/ppermute | solution.py:386
  134.1 5.6 %collective-permute-start.20 = (bf16[384,1024]{1,0:T(8,128)(2,1)S(1)}, bf16[384,1024]{1,0:T(8,128)(2,1)S(1)}, u32[]{:S(2)}, u32[]{:S(2)}) collective-permute-start(bf16[384,1024]{1,0:T(8,128)(2,1)S(1)} %get-tuple-element.82.am_ref), channel_id=1, source_target_pairs={{0,1},{1,0},{2,3},{3,2},{4,5},{5,4},{6,7},{7,6},{8,9},{9,8},{10,11... | collective-permute-start | bytes 2359304 | tf_op jit(solution)/shard_map/ppermute | solution.py:386
  134.6 5.1 %collective-permute-start.21 = (bf16[384,896]{1,0:T(8,128)(2,1)}, bf16[384,896]{1,0:T(8,128)(2,1)S(1)}, u32[]{:S(2)}, u32[]{:S(2)}) collective-permute-start(bf16[384,896]{1,0:T(8,128)(2,1)} %copy-done.6), channel_id=1, source_target_pairs={{0,1},{1,0},{2,3},{3,2},{4,5},{5,4},{6,7},{7,6},{8,9},{9,8},{10,11... | collective-permute-start | bytes 2064392 | tf_op jit(solution)/shard_map/ppermute | solution.py:386
  134.7 9.7 %collective-permute-start.18 = (bf16[384,896]{1,0:T(8,128)(2,1)}, bf16[384,896]{1,0:T(8,128)(2,1)S(1)}, u32[]{:S(2)}, u32[]{:S(2)}) collective-permute-start(bf16[384,896]{1,0:T(8,128)(2,1)} %copy-done.5), channel_id=1, source_target_pairs={{0,1},{1,0},{2,3},{3,2},{4,5},{5,4},{6,7},{7,6},{8,9},{9,8},{10,11... | collective-permute-start | bytes 2064392 | tf_op jit(solution)/shard_map/ppermute | solution.py:386
  139.7 1.1 copy-start.8

commit v3 on v2

--- a/solution.py
+++ b/solution.py
@@ -83,8 +83,9 @@
     other = pl.multiple_of((1 - core_ref[0]) * half, 128)
     tail = go_ref[:, pl.ds(other, half)]
     sources = (tok_ref[:, pl.ds(own, half)], tok_ref[:, pl.ds(other, half)], go_ref[:, pl.ds(own, half)])
+    tails = dot(sel_ref[1:].reshape(3 * sel_ref.shape[1], sel_ref.shape[2]), tail)
     for q, source in enumerate(sources):
-        rows_q = dot(sel_ref[0], source) + dot(sel_ref[1 + q], tail)
+        rows_q = dot(sel_ref[0], source) + tails[q * sel_ref.shape[1] : (q + 1) * sel_ref.shape[1]]
         out_ref[0, :, q * half : (q + 1) * half] = (scale_s[q] * rows_q).astype(BF16)
 
 
@@ -248,23 +249,48 @@
     )(at, *parts, *weights)
 
 
-def grad_kernel(at_ref, g0, g1, g2, g3, main_ref, go_ref, gx_ref, uo_ref, ux_ref, out_ref, keep_hbm, all_s, sem):
+def half_grad_kernel(at_ref, g0, g1, g2, g3, wo_ref, wx_ref, own_ref, other_ref, keep_hbm, all_s, sem):
+    gather_parts(at_ref, (g0, g1, g2, g3), all_s)
+    keep = pltpu.make_async_copy(all_s, keep_hbm, sem)
+    keep.start()
+    own_ref[...] = dot(all_s[...], wo_ref[...], 1, 1)
+    other_ref[...] = dot(all_s[...], wx_ref[...], 1, 1)
+    keep.wait()
+
+
+def half_grad(at, parts, weights):
+    quarters = len(parts)
+    slots, hidden = parts[0].shape
+    value = jax.ShapeDtypeStruct((quarters * slots, weights[0].shape[0]), F32)
+    return pl.pallas_call(
+        half_grad_kernel,
+        in_specs=[smem()] + [whole()] * (quarters + 2),
+        out_specs=[whole(), whole(), hbm()],
+        out_shape=[value, value, jax.ShapeDtypeStruct((quarters * slots, hidden), BF16)],
+        scratch_shapes=[pltpu.VMEM((quarters * slots, hidden), BF16), pltpu.SemaphoreType.DMA],
+        compiler_params=pltpu.CompilerParams(vmem_limit_bytes=SMALL_LIMIT),
+        cost_estimate=pl.CostEstimate(flops=1_500_000_000, bytes_accessed=8_000_000, transcendentals=0),
+        name="half_grad",
+    )(at, *parts, *weights)
+
+
+def grad_kernel(at_ref, g0, g1, g2, g3, main_ref, half_own_ref, half_other_ref, wo_ref, wx_ref, out_ref, keep_hbm, all_s, sem):
     quarters, lanes, packed = out_ref.shape
     half = packed // 3
     slots = g0.shape[0]
-    hidden = all_s.shape[1] // 2
     gather_parts(at_ref, (g0, g1, g2, g3), all_s)
     keep = pltpu.make_async_copy(all_s, keep_hbm, sem)
     keep.start()
     masks = slot_masks(2 * slots, 2 * lanes, True)
-    dg, du = all_s[:, :hidden], all_s[:, hidden:]
-    own = (dot(dg, go_ref[...], 1, 1) + dot(du, uo_ref[...], 1, 1)).astype(BF16)
-    other = (dot(dg, gx_ref[...], 1, 1) + dot(du, ux_ref[...], 1, 1)).astype(BF16)
+    tail_masks = jnp.concatenate(masks[1:], axis=0)
+    other = (half_other_ref[...] + dot(all_s[...], wx_ref[...], 1, 1)).astype(BF16)
+    own = (half_own_ref[...] + dot(all_s[...], wo_ref[...], 1, 1)).astype(BF16)
     for p in range(quarters // 2):
         rows = slice(2 * p * slots, 2 * (p + 1) * slots)
+        tails = dot(tail_masks, other[rows])
         for q in range(3):
             columns = slice(q * half, (q + 1) * half)
-            value = dot(masks[1 + q], other[rows])
+            value = tails[2 * q * lanes : 2 * (q + 1) * lanes]
             if q == 2:
                 value = value + dot(masks[0], own[rows])
             else:
@@ -276,26 +302,22 @@
     keep.wait()
 
 
-def grad_rows(at, parts, main, weights):
+def grad_rows(at, parts, main, halves, weights):
     quarters, lanes, width = main.shape
-    slots, both = parts[0].shape
-    packed = width // 2 * 3
+    slots, hidden = parts[0].shape
     return pl.pallas_call(
         grad_kernel,
         in_specs=[smem()] + [whole()] * (quarters + 5),
         out_specs=[whole(), hbm()],
         out_shape=[
-            jax.ShapeDtypeStruct((quarters, lanes, packed), BF16),
-            jax.ShapeDtypeStruct((quarters * slots, both), BF16),
+            jax.ShapeDtypeStruct((quarters, lanes, width // 2 * 3), BF16),
+            jax.ShapeDtypeStruct((quarters * slots, hidden), BF16),
         ],
-        scratch_shapes=[
-            pltpu.VMEM((quarters * slots, both), BF16),
-            pltpu.SemaphoreType.DMA,
-        ],
+        scratch_shapes=[pltpu.VMEM((quarters * slots, hidden), BF16), pltpu.SemaphoreType.DMA],
         compiler_params=pltpu.CompilerParams(vmem_limit_bytes=SMALL_LIMIT),
-        cost_estimate=pl.CostEstimate(flops=3_500_000_000, bytes_accessed=14_000_000, transcendentals=0),
+        cost_estimate=pl.CostEstimate(flops=2_500_000_000, bytes_accessed=14_000_000, transcendentals=0),
         name="grad_rows",
-    )(at, *parts, main, *weights)
+    )(at, *parts, main, *halves, *weights)
 
 
 def weight_kernel(am_ref, ap_ref, bm_ref, bp_ref, out_ref):
@@ -319,16 +341,27 @@
     )(a_mine, a_partner, b_mine, b_partner)
 
 
-def last_kernel(core_ref, routes_ref, sel_ref, wsel_ref, recv_ref, go_ref, moe_ref, gt_ref, gr_ref, inner_s):
+def last_kernel(core_ref, routes_ref, sel_ref, wsel_ref, recv_ref, go_ref, moe_ref, gt_ref, gr_ref, inner_s, lhs_s):
     step = pl.program_id(0)
     half = go_ref.shape[1] // 2
     own = pl.ds(pl.multiple_of(core_ref[0] * half, 128), half)
     other = pl.ds(pl.multiple_of((1 - core_ref[0]) * half, 128), half)
     block = [recv_ref[0, :, q * half : (q + 1) * half] for q in range(3)]
-    moe_ref[:, own] = (dot(wsel_ref[0], block[0], 0, 0) + dot(wsel_ref[1], block[0], 0, 0)).astype(BF16)
-    moe_ref[:, other] = (dot(wsel_ref[0], block[1], 0, 0) + dot(wsel_ref[1], block[1], 0, 0)).astype(BF16)
-    gt_ref[:, own] = dot(sel_ref[0], block[2], 0, 0).astype(BF16)
-    gt_ref[:, other] = sum(dot(sel_ref[1 + q], block[q], 0, 0) for q in range(3)).astype(BF16)
+    rows = go_ref.shape[0]
+
+    @pl.when(step == 0)
+    def _():
+        for q in range(2):
+            for i, one in enumerate((wsel_ref[0], wsel_ref[1], sel_ref[1 + q])):
+                lhs_s[q, i * rows : (i + 1) * rows, :] = one.astype(F32).T.astype(BF16)
+        for i in (0, 3):
+            lhs_s[2, i // 3 * rows : (i // 3 + 1) * rows, :] = sel_ref[i].astype(F32).T.astype(BF16)
+
+    first, second, third = dot(lhs_s[0], block[0]), dot(lhs_s[1], block[1]), dot(lhs_s[2, : 2 * rows, :], block[2])
+    moe_ref[:, own] = (first[:rows] + first[rows : 2 * rows]).astype(BF16)
+    moe_ref[:, other] = (second[:rows] + second[rows : 2 * rows]).astype(BF16)
+    gt_ref[:, own] = third[:rows].astype(BF16)
+    gt_ref[:, other] = (first[2 * rows :] + second[2 * rows :] + third[rows:]).astype(BF16)
     inner = dot(block[0], go_ref[:, own], 1, 1) + dot(block[1], go_ref[:, other], 1, 1)
 
     @pl.when(step == 0)
@@ -364,7 +397,7 @@
             jax.ShapeDtypeStruct((rows, width), BF16),
             jax.ShapeDtypeStruct(routes.shape, F32),
         ],
-        scratch_shapes=[pltpu.VMEM((lanes, rows), F32)],
+        scratch_shapes=[pltpu.VMEM((lanes, rows), F32), pltpu.VMEM((3, 3 * rows, lanes), BF16)],
         compiler_params=pltpu.CompilerParams(vmem_limit_bytes=BIG_LIMIT),
         cost_estimate=pl.CostEstimate(flops=1_500_000_000, bytes_accessed=8_500_000, transcendentals=0),
         name="last",
@@ -421,18 +454,21 @@
     mine, smooth, slope = lax.optimization_barrier(((smooth * up).astype(BF16), smooth, slope))
     h_parts = from_y(mine)
     back, h_parts = lax.optimization_barrier((back, h_parts))
-    g_parts = from_y(jnp.concatenate([(back * slope).astype(BF16), (back * smooth).astype(BF16)], axis=1))
+    dg_parts = from_y((back * slope).astype(BF16))
     main, h_mine = out_rows(at, h_parts, down, lanes)
-    packed, g_mine = grad_rows(at, g_parts, main, (gate_own, gate_other, up_own, up_other))
-    x_other, d_other, h_mine, g_mine = lax.optimization_barrier((x_other, d_other, h_mine, g_mine))
+    du, main = lax.optimization_barrier(((back * smooth).astype(BF16), main))
+    du_parts = from_y(du)
+    *halves, dg_mine = half_grad(at, dg_parts, (gate_own, gate_other))
+    packed, du_mine = grad_rows(at, du_parts, main, halves, (up_own, up_other))
+    x_other, d_other, h_mine, dg_mine, du_mine = lax.optimization_barrier((x_other, d_other, h_mine, dg_mine, du_mine))
     returned = exchange(packed)
 
     x_partner, d_partner, h_partner = to_partner(x_other), to_partner(d_other), to_partner(h_mine)
-    g_partner = to_partner(g_mine)
+    dg_partner, du_partner = to_partner(dg_mine), to_partner(du_mine)
     step = hidden // 4
     grad_down = weight_grad(h_mine, h_partner, d_own, d_partner, half)
-    grad_gate = weight_grad(x_own, x_partner, g_mine, g_partner, step, 0, hidden)
-    grad_up = weight_grad(x_own, x_partner, g_mine, g_partner, step, 4, hidden)
+    grad_gate = weight_grad(x_own, x_partner, dg_mine, dg_partner, step)
+    grad_up = weight_grad(x_own, x_partner, du_mine, du_partner, step)
     returned, grad_gate, grad_up, grad_down = lax.optimization_barrier((returned, grad_gate, grad_up, grad_down))
 
     moe_out, grad_tokens, grad_route = last(core, routes, sel, wsel, returned, grad_out)

time: 177 us -> 173 us (0.977)
  waiting for transfers between devices: 80 us -> 71.2 us
  starting transfers between devices: 45 us -> 48.8 us
  Pallas kernels: 45.9 us -> 48.7 us
    ppermute x15 -> x18, waiting for transfers between devices: 21.4 us -> 13.1 us  [along(): lax.ppermute(value, 'y', [(i, (i + shift) % quarters) for i in range(quar...]
    ppermute x15 -> x18, starting transfers between devices: 20 us -> 25.1 us  [along(): lax.ppermute(value, 'y', [(i, (i + shift) % quarters) for i in range(quar...]
    pallas_call x0 -> x1, Pallas kernels: none -> 3.45 us  [half_grad(): pl.pallas_call(half_grad_kernel, in_specs=[smem()] + [whole()] * (quarter...]
    ppermute x7 -> x8, waiting for transfers between devices: 8.17 us -> 6.67 us  [to_partner(): return lax.ppermute(value, 'k', [(0, 1), (1, 0)])]
  transfers between devices with their start and end apart: 24 -> 28, of which waited for: 13 -> 11; matrix products, arithmetic and copies ran while one was open for 0% -> 0% of each run, Pallas kernels for 15% -> 18%
where the time goes in v3:
time: 173 us
  waiting for transfers between devices  71.2 us (41%)
  starting transfers between devices  48.8 us (28%)
  Pallas kernels  48.7 us (28%)
  local copies, waits for them, and re-layouts  2.64 us (2%)
    all_to_all x2, waiting for transfers between devices, exchange(): return lax.all_to_all(flat, everyone, 0, 0, tiled=True).reshape(value.shape)  51.4 us
    ppermute x18, starting transfers between devices, along(): lax.ppermute(value, 'y', [(i, (i + shift) % quarters) for i in range(quar...  25.1 us
    all_to_all x2, starting transfers between devices, exchange(): return lax.all_to_all(flat, everyone, 0, 0, tiled=True).reshape(value.shape)  21.8 us
    ppermute x18, waiting for transfers between devices, along(): lax.ppermute(value, 'y', [(i, (i + shift) % quarters) for i in range(quar...  13.1 us
    pallas_call x3, Pallas kernels, projection(): pl.pallas_call(kernel, in_specs=in_specs, out_specs=out_specs, out_shape=...  12.2 us
    pallas_call x3, Pallas kernels, weight_grad(): pl.pallas_call(weight_kernel, grid=(columns // step,), in_specs=[a_spec,...  11 us
    ppermute x8, waiting for transfers between devices, to_partner(): return lax.ppermute(value, 'k', [(0, 1), (1, 0)])  6.67 us
    pallas_call x1, Pallas kernels, last(): pl.pallas_call(last_kernel, grid=(quarters,), in_specs=[smem(), whole(),...  6.52 us
  transfers between devices with their start and end apart: 28, of which 11 were waited for; matrix products, arithmetic and copies ran while one was open for 0% of the time, Pallas kernels for 18%

profile of v3, /device:TPU:0, one launch (start us, length us, event | category | flops | bytes accessed | tf_op | source)
XLA Modules:
  0.0 172.8 jit_solution(2777233191386074409)
XLA Ops:
  0.6 5.5 %prep.1 = (bf16[4,128,2688]{2,1,0:T(8,128)(2,1)}, bf16[4,128,128]{2,1,0:T(8,128)(2,1)}, bf16[2,128,128]{2,1,0:T(8,128)(2,1)}) custom-call(s32[1]{0:T(128)} %bitcast.core_ref, s32[8,128]{1,0:T(8,128)} %bitcast.27, f32[8,128]{1,0:T(8,128)} %bitcast.26, bf16[128,7168]{1,0:T(8,128)(2,1)} %tok_ref.1, bf16[128,7168]{1,0:T(8,128)(2,1)} %go_ref.3), custom_call_target="tpu_custom_call" | custom-call | flops 800000000 | bytes 6500000 | tf_op jit(solution)/shard_map/prep/pallas_call | solution.py:98
  6.1 11.5 %all-to-all-start = ((bf16[64,8,2688]{2,1,0:T(8,128)(2,1)}), bf16[64,8,2688]{2,1,0:T(8,128)(2,1)S(1)}, u32[]{:S(2)}, u32[]{:S(2)}) async-start(bf16[64,8,2688]{2,1,0:T(8,128)(2,1)} %bitcast.25), calls=%async_computation | async-start | bytes 5505024 | tf_op jit(solution)/shard_map/all_to_all | solution.py:426
  17.7 0.5 collective-permute-start.8
  18.2 0.1 collective-permute-start.1
  18.3 3.5 %collective-permute-done.wx_ref = bf16[896,1024]{1,0:T(8,128)(2,1)} collective-permute-done((bf16[896,1024]{1,0:T(8,128)(2,1)}, bf16[896,1024]{1,0:T(8,128)(2,1)}, u32[]{:S(2)}, u32[]{:S(2)}) %collective-permute-start) | collective-permute-done | bytes 1835040 | tf_op jit(solution)/shard_map/ppermute | solution.py:419
  21.8 32.2 %all-to-all-done = bf16[64,8,2688]{2,1,0:T(8,128)(2,1)S(1)} async-done(((bf16[64,8,2688]{2,1,0:T(8,128)(2,1)}), bf16[64,8,2688]{2,1,0:T(8,128)(2,1)S(1)}, u32[]{:S(2)}, u32[]{:S(2)}) %all-to-all-start) | async-done | bytes 2752544 | tf_op jit(solution)/shard_map/all_to_all | solution.py:426
  54.0 1.5 copy-done.1
  55.5 4.3 %gate.1 = (f32[96,1024]{1,0:T(8,128)S(1)}, bf16[96,1024]{1,0:T(8,128)(2,1)S(1)}, bf16[96,1024]{1,0:T(8,128)(2,1)S(1)}, bf16[96,1024]{1,0:T(8,128)(2,1)S(1)}, bf1...) custom-call(s32[1]{0:T(128)} %bitcast.3.at_ref, ...), custom_call_target="tpu_custom_call", output_to_operand_aliasing={{6}: (1, {})} | custom-call | flops 3000000000 | bytes 8000000 | tf_op jit(solution)/shard_map/gate/pallas_call | solution.py:199
  59.9 0.9 collective-permute-start.5
  60.8 1.3 collective-permute-start.6
  62.1 1.9 %collective-permute-start.7 = (bf16[96,1024]{1,0:T(8,128)(2,1)S(1)}, bf16[96,1024]{1,0:T(8,128)(2,1)S(1)}, u32[]{:S(2)}, u32[]{:S(2)}) collective-permute-start(bf16[96,1024]{1,0:T(8,128)(2,1)S(1)} %get-tuple-element.66), channel_id=1, source_target_pairs={{0,6},{2,0},{4,2},{6,4},{1,7},{3,1},{5,3},{7,5},{8,14},{10,8},{12,... | collective-permute-start | bytes 589832 | tf_op jit(solution)/shard_map/ppermute | solution.py:422
  64.0 3.6 %up.1 = (f32[96,1024]{1,0:T(8,128)S(1)}, bf16[96,1024]{1,0:T(8,128)(2,1)S(1)}, bf16[96,1024]{1,0:T(8,128)(2,1)S(1)}, bf16[96,1024]{1,0:T(8,128)(2,1)S(1)}) custom-call(s32[1]{0:T(128)} %bitcast.3.at_ref, bf16[384,896]{1,0:T(8,128)(2,1)S(1)} %get-tuple-element.67.own_ref.am_ref, bf16[384,896]{1,0:T(8,128)(2,1)S(1)} %get-tuple-element.91.other_ref, ...), custom_call_target="tpu_custom_call" | custom-call | flops 3000000000 | bytes 8000000 | tf_op jit(solution)/shard_map/up/pallas_call | solution.py:199
  67.6 1.6 collective-permute-start.9
  69.2 3.2 %collective-permute-start.11 = (bf16[96,1024]{1,0:T(8,128)(2,1)S(1)}, bf16[96,1024]{1,0:T(8,128)(2,1)S(1)}, u32[]{:S(2)}, u32[]{:S(2)}) collective-permute-start(bf16[96,1024]{1,0:T(8,128)(2,1)S(1)} %get-tuple-element.72), channel_id=1, source_target_pairs={{0,6},{2,0},{4,2},{6,4},{1,7},{3,1},{5,3},{7,5},{8,14},{10,8},{12,... | collective-permute-start | bytes 589832 | tf_op jit(solution)/shard_map/ppermute | solution.py:422
  72.4 4.3 %back.1 = (f32[96,1024]{1,0:T(8,128)S(1)}, bf16[96,1024]{1,0:T(8,128)(2,1)S(1)}, bf16[96,1024]{1,0:T(8,128)(2,1)S(1)}, bf16[96,1024]{1,0:T(8,128)(2,1)S(1)}, bf1...) custom-call(s32[1]{0:T(128)} %bitcast.3.at_ref, bf16[4,128,2688]{2,1,0:T(8,128)(2,1)S(1)} %get-tuple-element.58.recv_ref, ...), custom_call_target="tpu_custom_call" | custom-call | flops 3000000000 | bytes 8000000 | tf_op jit(solution)/shard_map/back/pallas_call | solution.py:199
  76.8 0.9 collective-permute-start.2
  77.7 0.1 collective-permute-start.3
  77.8 3.1 %collective-permute-start.4 = (bf16[96,1024]{1,0:T(8,128)(2,1)S(1)}, bf16[96,1024]{1,0:T(8,128)(2,1)S(1)}, u32[]{:S(2)}, u32[]{:S(2)}) collective-permute-start(bf16[96,1024]{1,0:T(8,128)(2,1)S(1)} %get-tuple-element.62), channel_id=1, source_target_pairs={{0,6},{2,0},{4,2},{6,4},{1,7},{3,1},{5,3},{7,5},{8,14},{10,8},{12,... | collective-permute-start | bytes 589832 | tf_op jit(solution)/shard_map/ppermute | solution.py:422
  81.0 0.7 collective-permute-done.10
  81.7 0.3 multiply_convert_fusion.2
  82.0 1.7 collective-permute-start.14
  83.7 1.0 collective-permute-start.13
  84.8 1.5 collective-permute-done.2
  86.2 0.3 collective-permute-start.12
  86.5 3.4 %collective-permute-done.3 = bf16[96,1024]{1,0:T(8,128)(2,1)S(1)} collective-permute-done((bf16[96,1024]{1,0:T(8,128)(2,1)S(1)}, bf16[96,1024]{1,0:T(8,128)(2,1)S(1)}, u32[]{:S(2)}, u32[]{:S(2)}) %collective-permute-start.3) | collective-permute-done | bytes 196640 | tf_op jit(solution)/shard_map/ppermute | solution.py:422
  89.9 0.2 collective-permute-done.4
  90.2 2.9 %collective-permute-done.14.h3 = bf16[96,1024]{1,0:T(8,128)(2,1)S(1)} collective-permute-done((bf16[96,1024]{1,0:T(8,128)(2,1)S(1)}, bf16[96,1024]{1,0:T(8,128)(2,1)S(1)}, u32[]{:S(2)}, u32[]{:S(2)}) %collective-permute-start.14) | collective-permute-done | bytes 196640 | tf_op jit(solution)/shard_map/ppermute | solution.py:422
  93.1 2.2 %collective-permute-done.13.h2 = bf16[96,1024]{1,0:T(8,128)(2,1)S(1)} collective-permute-done((bf16[96,1024]{1,0:T(8,128)(2,1)S(1)}, bf16[96,1024]{1,0:T(8,128)(2,1)S(1)}, u32[]{:S(2)}, u32[]{:S(2)}) %collective-permute-start.13) | collective-permute-done | bytes 196640 | tf_op jit(solution)/shard_map/ppermute | solution.py:422
  95.3 0.5 collective-permute-start.20
  95.9 2.4 %collective-permute-start.19 = (bf16[96,1024]{1,0:T(8,128)(2,1)S(1)}, bf16[96,1024]{1,0:T(8,128)(2,1)S(1)}, u32[]{:S(2)}, u32[]{:S(2)}) collective-permute-start(bf16[96,1024]{1,0:T(8,128)(2,1)S(1)} %get-tuple-element.107.g0), channel_id=1, source_target_pairs={{0,4},{2,6},{4,0},{6,2},{1,5},{3,7},{5,1},{7,3},{8,12},{10,14},{12... | collective-permute-start | bytes 589832 | tf_op jit(solution)/shard_map/ppermute | solution.py:422
  98.3 0.9 collective-permute-start.18
  99.2 3.9 %out_rows.1 = (bf16[4,128,1792]{2,1,0:T(8,128)(2,1)S(1)}, bf16[384,1024]{1,0:T(8,128)(2,1)S(1)}) custom-call(s32[1]{0:T(128)} %bitcast.3.at_ref, bf16[96,1024]{1,0:T(8,128)(2,1)S(1)} %get-tuple-element.76.h0, bf16[96,1024]{1,0:T(8,128)(2,1)S(1)} %collective-permute-done.12.h1, bf16[96,1024]{1,0:T(8,128)(2,1)S(1)} %collective-permute-done.13.h2, ...), custom_call_target="tpu_custom_call" | custom-call | flops 2000000000 | bytes 7500000 | tf_op jit(solution)/shard_map/out_rows/pallas_call | solution.py:238
  103.1 1.2 collective-permute-start.17
  104.2 1.4 collective-permute-start.16
  105.6 2.5 %collective-permute-start.15 = (bf16[96,1024]{1,0:T(8,128)(2,1)S(1)}, bf16[96,1024]{1,0:T(8,128)(2,1)S(1)}, u32[]{:S(2)}, u32[]{:S(2)}) collective-permute-start(bf16[96,1024]{1,0:T(8,128)(2,1)S(1)} %get-tuple-element.81.g0), channel_id=1, source_target_pairs={{0,6},{2,0},{4,2},{6,4},{1,7},{3,1},{5,3},{7,5},{8,14},{10,8},{12,... | collective-permute-start | bytes 589832 | tf_op jit(solution)/shard_map/ppermute | solution.py:422
  108.2 3.4 %half_grad.1 = (f32[384,896]{1,0:T(8,128)S(1)}, f32[384,896]{1,0:T(8,128)S(1)}, bf16[384,1024]{1,0:T(8,128)(2,1)S(1)}) custom-call(s32[1]{0:T(128)} %bitcast.3.at_ref, bf16[96,1024]{1,0:T(8,128)(2,1)S(1)} %get-tuple-element.107.g0, bf16[96,1024]{1,0:T(8,128)(2,1)S(1)} %collective-permute-done.18.g1, bf16[96,1024]{1,0:T(8,128)(2,1)S(1)} %collective-permute-done.19.g2, ...), custom_call_target="tpu_custom_call" | custom-call | flops 1500000000 | bytes 8000000 | tf_op jit(solution)/shard_map/half_grad/pallas_call | solution.py:265
  111.6 2.3 %collective-permute-done.17.g3 = bf16[96,1024]{1,0:T(8,128)(2,1)S(1)} collective-permute-done((bf16[96,1024]{1,0:T(8,128)(2,1)S(1)}, bf16[96,1024]{1,0:T(8,128)(2,1)S(1)}, u32[]{:S(2)}, u32[]{:S(2)}) %collective-permute-start.17) | collective-permute-done | bytes 196640 | tf_op jit(solution)/shard_map/ppermute | solution.py:422
  113.9 6.2 %grad_rows.1 = (bf16[4,128,2688]{2,1,0:T(8,128)(2,1)}, bf16[384,1024]{1,0:T(8,128)(2,1)S(1)}) custom-call(s32[1]{0:T(128)} %bitcast.3.at_ref, bf16[96,1024]{1,0:T(8,128)(2,1)S(1)} %get-tuple-element.81.g0, bf16[96,1024]{1,0:T(8,128)(2,1)S(1)} %collective-permute-done.15.g1, bf16[96,1024]{1,0:T(8,128)(2,1)S(1)} %collective-permute-done.16.g2, ...), custom_call_target="tpu_custom_call" | custom-call | flops 2500000000 | bytes 14000000 | tf_op jit(solution)/shard_map/grad_rows/pallas_call | solution.py:308
  120.1 10.3 %all-to-all-start.1 = ((bf16[64,8,2688]{2,1,0:T(8,128)(2,1)}), bf16[64,8,2688]{2,1,0:T(8,128)(2,1)}, u32[]{:S(2)}, u32[]{:S(2)}) async-start(bf16[64,8,2688]{2,1,0:T(8,128)(2,1)} %bitcast.9), calls=%async_computation.1 | async-start | bytes 5505024 | tf_op jit(solution)/shard_map/all_to_all | solution.py:426
  130.5 0.5 collective-permute-start.21
  131.1 0.4 collective-permute-start.24
  131.7 3.1 %collective-permute-done.21.ap_ref = bf16[384,896]{1,0:T(8,128)(2,1)S(1)} collective-permute-done((bf16[384,896]{1,0:T(8,128)(2,1)S(1)}, bf16[384,896]{1,0:T(8,128)(2,1)S(1)}, u32[]{:S(2)}, u32[]{:S(2)}) %collective-permute-start.21) | collective-permute-done | bytes 688160 | tf_op jit(solution)/shard_map/ppermute | solution.py:419
  134.8 1.1 copy-done.6
  135.9 3.7 %weight_grad.3 = bf16[896,1024]{1,0:T(8,128)(2,1)} custom-call(bf16[384,896]{1,0:T(8,128)(2,1)S(1)} %copy-done.6, bf16[384,896]{1,0:T(8,128)(2,1)S(1)} %collective-permute-done.21.ap_ref, bf16[384,1024]{1,0:T(8,128)(2,1)S(1)} %get-tuple-element.92.bm_ref, bf16[384,1024]{1,0:T(8,128)(2,1)S(1)} %collective-permute-done.22.bp_ref), custom_call_target="tpu_custom_call" | custom-call | flops 1500000000 | bytes 5000000 | tf_op jit(solution)/shard_map/weight_grad/pallas_call | solution.py:332
  139.6 3.8 %weight_grad.4 = bf16[896,1024]{1,0:T(8,128)(2,1)} custom-call(bf16[384,896]{1,0:T(8,128)(2,1)S(1)} %copy-done.6, bf16[384,896]{1,0:T(8,128)(2,1)S(1)} %collective-permute-done.21.ap_ref, bf16[384,1024]{1,0:T(8,128)(2,1)S(1)} %get-tuple-element.93.bm_ref, bf16[384,1024]{1,0:T(8,128)(2,1)S(1)} %collective-permute-done.23.bp_ref), custom_call_target="tpu_custom_call" | custom-call | flops 1500000000 | bytes 5000000 | tf_op jit(solution)/shard_map/weight_grad/pallas_call | solution.py:332
  143.4 3.5 %weight_grad.5 = bf16[1024,896]{1,0:T(8,128)(2,1)} custom-call(bf16[384,1024]{1,0:T(8,128)(2,1)S(1)} %get-tuple-element.94.am_ref, bf16[384,1024]{1,0:T(8,128)(2,1)S(1)} %collective-permute-done.24.ap_ref, bf16[384,896]{1,0:T(8,128)(2,1)S(1)} %copy-done.8, bf16[384,896]{1,0:T(8,128)(2,1)S(1)} %collective-permute-done.25.bp_ref), custom_call_target="tpu_custom_call" | custom-call | flops 1500000000 | bytes 5000000 | tf_op jit(solution)/shard_map/weight_grad/pallas_call | solution.py:332
  146.9 19.2 %all-to-all-done.1 = bf16[64,8,2688]{2,1,0:T(8,128)(2,1)} async-done(((bf16[64,8,2688]{2,1,0:T(8,128)(2,1)}), bf16[64,8,2688]{2,1,0:T(8,128)(2,1)}, u32[]{:S(2)}, u32[]{:S(2)}) %all-to-all-start.1) | async-done | bytes 2752544 | tf_op jit(solution)/shard_map/all_to_all | solution.py:426
  166.1 6.5 %last.1 = (bf16[128,7168]{1,0:T(8,128)(2,1)}, bf16[128,7168]{1,0:T(8,128)(2,1)}, f32[8,128]{1,0:T(8,128)}) custom-call(s32[1]{0:T(128)} %bitcast.core_ref, s32[8,128]{1,0:T(8,128)} %bitcast.28, bf16[4,128,128]{2,1,0:T(8,128)(2,1)} %get-tuple-element.55.sel_ref, bf16[2,128,128]{2,1,0:T(8,128)(2,1)} %get-tuple-element.56.wsel_ref, ...), custom_call_target="tpu_custom_call" | custom-call | flops 1500000000 | bytes 8500000 | tf_op jit(solution)/shard_map/last/pallas_call | solution.py:390
  (40 shorter events, 0.6 us)
Async XLA Ops:
  6.1 47.9 %all-to-all-start = ((bf16[64,8,2688]{2,1,0:T(8,128)(2,1)}), bf16[64,8,2688]{2,1,0:T(8,128)(2,1)S(1)}, u32[]{:S(2)}, u32[]{:S(2)}) async-start(bf16[64,8,2688]{2,1,0:T(8,128)(2,1)} %bitcast.25), calls=%async_computation | async-start | bytes 5505024 | tf_op jit(solution)/shard_map/all_to_all | solution.py:426
  17.6 4.2 %collective-permute-start = (bf16[896,1024]{1,0:T(8,128)(2,1)}, bf16[896,1024]{1,0:T(8,128)(2,1)}, u32[]{:S(2)}, u32[]{:S(2)}) collective-permute-start(bf16[896,1024]{1,0:T(8,128)(2,1)} %bitcast.19), channel_id=1, source_target_pairs={{0,1},{1,0},{2,3},{3,2},{4,5},{5,4},{6,7},{7,6},{8,9},{9,8},{10,11... | collective-permute-start | bytes 5505032 | tf_op jit(solution)/shard_map/ppermute | solution.py:419
  17.7 46.3 %collective-permute-start.8 = (bf16[896,1024]{1,0:T(8,128)(2,1)}, bf16[896,1024]{1,0:T(8,128)(2,1)}, u32[]{:S(2)}, u32[]{:S(2)}) collective-permute-start(bf16[896,1024]{1,0:T(8,128)(2,1)} %bitcast.22), channel_id=1, source_target_pairs={{0,1},{1,0},{2,3},{3,2},{4,5},{5,4},{6,7},{7,6},{8,9},{9,8},{10,11... | collective-permute-start | bytes 5505032 | tf_op jit(solution)/shard_map/ppermute | solution.py:419
  18.2 51.0 %collective-permute-start.1 = (bf16[1024,896]{1,0:T(8,128)(2,1)}, bf16[1024,896]{1,0:T(8,128)(2,1)}, u32[]{:S(2)}, u32[]{:S(2)}) collective-permute-start(bf16[1024,896]{1,0:T(8,128)(2,1)} %bitcast.16), channel_id=1, source_target_pairs={{0,1},{1,0},{2,3},{3,2},{4,5},{5,4},{6,7},{7,6},{8,9},{9,8},{10,11... | collective-permute-start | bytes 5505032 | tf_op jit(solution)/shard_map/ppermute | solution.py:419
  54.0 1.5 copy-start.1
  55.5 8.5 %copy-start.3 = (bf16[1,896,1024]{2,1,0:T(8,128)(2,1)S(1)}, bf16[1,896,1024]{2,1,0:T(8,128)(2,1)}, u32[]{:S(2)}) copy-start(bf16[1,896,1024]{2,1,0:T(8,128)(2,1)} %param.11) | copy-start | bytes 5505028
  59.9 7.8 %copy-start.5 = (bf16[384,896]{1,0:T(8,128)(2,1)}, bf16[384,896]{1,0:T(8,128)(2,1)S(1)}, u32[]{:S(2)}) copy-start(bf16[384,896]{1,0:T(8,128)(2,1)S(1)} %get-tuple-element.67.own_ref.am_ref) | copy-start | bytes 2064388
  59.9 9.3 %collective-permute-start.5 = (bf16[96,1024]{1,0:T(8,128)(2,1)S(1)}, bf16[96,1024]{1,0:T(8,128)(2,1)S(1)}, u32[]{:S(2)}, u32[]{:S(2)}) collective-permute-start(bf16[96,1024]{1,0:T(8,128)(2,1)S(1)} %get-tuple-element.64), channel_id=1, source_target_pairs={{0,4},{2,6},{4,0},{6,2},{1,5},{3,7},{5,1},{7,3},{8,12},{10,14},{12... | collective-permute-start | bytes 589832 | tf_op jit(solution)/shard_map/ppermute | solution.py:422
  60.8 16.0 %collective-permute-start.6 = (bf16[96,1024]{1,0:T(8,128)(2,1)S(1)}, bf16[96,1024]{1,0:T(8,128)(2,1)S(1)}, u32[]{:S(2)}, u32[]{:S(2)}) collective-permute-start(bf16[96,1024]{1,0:T(8,128)(2,1)S(1)} %get-tuple-element.65), channel_id=1, source_target_pairs={{0,2},{2,4},{4,6},{6,0},{1,3},{3,5},{5,7},{7,1},{8,10},{10,12},{12... | collective-permute-start | bytes 589832 | tf_op jit(solution)/shard_map/ppermute | solution.py:422
  62.1 15.6 %collective-permute-start.7 = (bf16[96,1024]{1,0:T(8,128)(2,1)S(1)}, bf16[96,1024]{1,0:T(8,128)(2,1)S(1)}, u32[]{:S(2)}, u32[]{:S(2)}) collective-permute-start(bf16[96,1024]{1,0:T(8,128)(2,1)S(1)} %get-tuple-element.66), channel_id=1, source_target_pairs={{0,6},{2,0},{4,2},{6,4},{1,7},{3,1},{5,3},{7,5},{8,14},{10,8},{12,... | collective-permute-start | bytes 589832 | tf_op jit(solution)/shard_map/ppermute | solution.py:422
  64.0 8.4 %copy-start = (bf16[1,1024,896]{2,1,0:T(8,128)(2,1)S(1)}, bf16[1,1024,896]{2,1,0:T(8,128)(2,1)}, u32[]{:S(2)}) copy-start(bf16[1,1024,896]{2,1,0:T(8,128)(2,1)} %param.12) | copy-start | bytes 5505028
  67.6 10.2 %collective-permute-start.9 = (bf16[96,1024]{1,0:T(8,128)(2,1)S(1)}, bf16[96,1024]{1,0:T(8,128)(2,1)S(1)}, u32[]{:S(2)}, u32[]{:S(2)}) collective-permute-start(bf16[96,1024]{1,0:T(8,128)(2,1)S(1)} %get-tuple-element.70), channel_id=1, source_target_pairs={{0,4},{2,6},{4,0},{6,2},{1,5},{3,7},{5,1},{7,3},{8,12},{10,14},{12... | collective-permute-start | bytes 589832 | tf_op jit(solution)/shard_map/ppermute | solution.py:422
  69.2 12.5 %collective-permute-start.10 = (bf16[96,1024]{1,0:T(8,128)(2,1)S(1)}, bf16[96,1024]{1,0:T(8,128)(2,1)S(1)}, u32[]{:S(2)}, u32[]{:S(2)}) collective-permute-start(bf16[96,1024]{1,0:T(8,128)(2,1)S(1)} %get-tuple-element.71), channel_id=1, source_target_pairs={{0,2},{2,4},{4,6},{6,0},{1,3},{3,5},{5,7},{7,1},{8,10},{10,12},{12... | collective-permute-start | bytes 589832 | tf_op jit(solution)/shard_map/ppermute | solution.py:422
  69.2 12.5 %collective-permute-start.11 = (bf16[96,1024]{1,0:T(8,128)(2,1)S(1)}, bf16[96,1024]{1,0:T(8,128)(2,1)S(1)}, u32[]{:S(2)}, u32[]{:S(2)}) collective-permute-start(bf16[96,1024]{1,0:T(8,128)(2,1)S(1)} %get-tuple-element.72), channel_id=1, source_target_pairs={{0,6},{2,0},{4,2},{6,4},{1,7},{3,1},{5,3},{7,5},{8,14},{10,8},{12,... | collective-permute-start | bytes 589832 | tf_op jit(solution)/shard_map/ppermute | solution.py:422
  76.8 13.4 %copy-start.7 = (bf16[384,896]{1,0:T(8,128)(2,1)}, bf16[384,896]{1,0:T(8,128)(2,1)S(1)}, u32[]{:S(2)}) copy-start(bf16[384,896]{1,0:T(8,128)(2,1)S(1)} %get-tuple-element.95.bm_ref) | copy-start | bytes 2064388
  76.8 21.5 %copy-start.4 = (bf16[384,896]{1,0:T(8,128)(2,1)}, bf16[384,896]{1,0:T(8,128)(2,1)S(1)}, u32[]{:S(2)}) copy-start(bf16[384,896]{1,0:T(8,128)(2,1)S(1)} %get-tuple-element.96) | copy-start | bytes 2064388
  76.8 9.4 %collective-permute-start.2 = (bf16[96,1024]{1,0:T(8,128)(2,1)S(1)}, bf16[96,1024]{1,0:T(8,128)(2,1)S(1)}, u32[]{:S(2)}, u32[]{:S(2)}) collective-permute-start(bf16[96,1024]{1,0:T(8,128)(2,1)S(1)} %get-tuple-element.60), channel_id=1, source_target_pairs={{0,4},{2,6},{4,0},{6,2},{1,5},{3,7},{5,1},{7,3},{8,12},{10,14},{12... | collective-permute-start | bytes 589832 | tf_op jit(solution)/shard_map/ppermute | solution.py:422
  77.7 12.2 %collective-permute-start.3 = (bf16[96,1024]{1,0:T(8,128)(2,1)S(1)}, bf16[96,1024]{1,0:T(8,128)(2,1)S(1)}, u32[]{:S(2)}, u32[]{:S(2)}) collective-permute-start(bf16[96,1024]{1,0:T(8,128)(2,1)S(1)} %get-tuple-element.61), channel_id=1, source_target_pairs={{0,2},{2,4},{4,6},{6,0},{1,3},{3,5},{5,7},{7,1},{8,10},{10,12},{12... | collective-permute-start | bytes 589832 | tf_op jit(solution)/shard_map/ppermute | solution.py:422
  77.8 12.3 %collective-permute-start.4 = (bf16[96,1024]{1,0:T(8,128)(2,1)S(1)}, bf16[96,1024]{1,0:T(8,128)(2,1)S(1)}, u32[]{:S(2)}, u32[]{:S(2)}) collective-permute-start(bf16[96,1024]{1,0:T(8,128)(2,1)S(1)} %get-tuple-element.62), channel_id=1, source_target_pairs={{0,6},{2,0},{4,2},{6,4},{1,7},{3,1},{5,3},{7,5},{8,14},{10,8},{12,... | collective-permute-start | bytes 589832 | tf_op jit(solution)/shard_map/ppermute | solution.py:422
  82.0 11.0 %collective-permute-start.14 = (bf16[96,1024]{1,0:T(8,128)(2,1)S(1)}, bf16[96,1024]{1,0:T(8,128)(2,1)S(1)}, u32[]{:S(2)}, u32[]{:S(2)}) collective-permute-start(bf16[96,1024]{1,0:T(8,128)(2,1)S(1)} %get-tuple-element.76.h0), channel_id=1, source_target_pairs={{0,2},{2,4},{4,6},{6,0},{1,3},{3,5},{5,7},{7,1},{8,10},{10,12},{12... | collective-permute-start | bytes 589832 | tf_op jit(solution)/shard_map/ppermute | solution.py:422
  83.7 11.5 %collective-permute-start.13 = (bf16[96,1024]{1,0:T(8,128)(2,1)S(1)}, bf16[96,1024]{1,0:T(8,128)(2,1)S(1)}, u32[]{:S(2)}, u32[]{:S(2)}) collective-permute-start(bf16[96,1024]{1,0:T(8,128)(2,1)S(1)} %get-tuple-element.76.h0), channel_id=1, source_target_pairs={{0,4},{2,6},{4,0},{6,2},{1,5},{3,7},{5,1},{7,3},{8,12},{10,14},{12... | collective-permute-start | bytes 589832 | tf_op jit(solution)/shard_map/ppermute | solution.py:422
  86.2 9.0 %collective-permute-start.12 = (bf16[96,1024]{1,0:T(8,128)(2,1)S(1)}, bf16[96,1024]{1,0:T(8,128)(2,1)S(1)}, u32[]{:S(2)}, u32[]{:S(2)}) collective-permute-start(bf16[96,1024]{1,0:T(8,128)(2,1)S(1)} %get-tuple-element.76.h0), channel_id=1, source_target_pairs={{0,6},{2,0},{4,2},{6,4},{1,7},{3,1},{5,3},{7,5},{8,14},{10,8},{12,... | collective-permute-start | bytes 589832 | tf_op jit(solution)/shard_map/ppermute | solution.py:422
  95.3 12.9 %copy-start.2 = (bf16[1,896,1024]{2,1,0:T(8,128)(2,1)S(1)}, bf16[1,896,1024]{2,1,0:T(8,128)(2,1)}, u32[]{:S(2)}) copy-start(bf16[1,896,1024]{2,1,0:T(8,128)(2,1)} %param.10) | copy-start | bytes 5505028
  95.3 10.3 %collective-permute-start.20 = (bf16[96,1024]{1,0:T(8,128)(2,1)S(1)}, bf16[96,1024]{1,0:T(8,128)(2,1)S(1)}, u32[]{:S(2)}, u32[]{:S(2)}) collective-permute-start(bf16[96,1024]{1,0:T(8,128)(2,1)S(1)} %get-tuple-element.107.g0), channel_id=1, source_target_pairs={{0,2},{2,4},{4,6},{6,0},{1,3},{3,5},{5,7},{7,1},{8,10},{10,12},{12... | collective-permute-start | bytes 589832 | tf_op jit(solution)/shard_map/ppermute | solution.py:422
  95.9 12.3 %collective-permute-start.19 = (bf16[96,1024]{1,0:T(8,128)(2,1)S(1)}, bf16[96,1024]{1,0:T(8,128)(2,1)S(1)}, u32[]{:S(2)}, u32[]{:S(2)}) collective-permute-start(bf16[96,1024]{1,0:T(8,128)(2,1)S(1)} %get-tuple-element.107.g0), channel_id=1, source_target_pairs={{0,4},{2,6},{4,0},{6,2},{1,5},{3,7},{5,1},{7,3},{8,12},{10,14},{12... | collective-permute-start | bytes 589832 | tf_op jit(solution)/shard_map/ppermute | solution.py:422
  98.3 9.9 %collective-permute-start.18 = (bf16[96,1024]{1,0:T(8,128)(2,1)S(1)}, bf16[96,1024]{1,0:T(8,128)(2,1)S(1)}, u32[]{:S(2)}, u32[]{:S(2)}) collective-permute-start(bf16[96,1024]{1,0:T(8,128)(2,1)S(1)} %get-tuple-element.107.g0), channel_id=1, source_target_pairs={{0,6},{2,0},{4,2},{6,4},{1,7},{3,1},{5,3},{7,5},{8,14},{10,8},{12,... | collective-permute-start | bytes 589832 | tf_op jit(solution)/shard_map/ppermute | solution.py:422
  103.1 10.8 %collective-permute-start.17 = (bf16[96,1024]{1,0:T(8,128)(2,1)S(1)}, bf16[96,1024]{1,0:T(8,128)(2,1)S(1)}, u32[]{:S(2)}, u32[]{:S(2)}) collective-permute-start(bf16[96,1024]{1,0:T(8,128)(2,1)S(1)} %get-tuple-element.81.g0), channel_id=1, source_target_pairs={{0,2},{2,4},{4,6},{6,0},{1,3},{3,5},{5,7},{7,1},{8,10},{10,12},{12... | collective-permute-start | bytes 589832 | tf_op jit(solution)/shard_map/ppermute | solution.py:422
  104.2 9.7 %collective-permute-start.16 = (bf16[96,1024]{1,0:T(8,128)(2,1)S(1)}, bf16[96,1024]{1,0:T(8,128)(2,1)S(1)}, u32[]{:S(2)}, u32[]{:S(2)}) collective-permute-start(bf16[96,1024]{1,0:T(8,128)(2,1)S(1)} %get-tuple-element.81.g0), channel_id=1, source_target_pairs={{0,4},{2,6},{4,0},{6,2},{1,5},{3,7},{5,1},{7,3},{8,12},{10,14},{12... | collective-permute-start | bytes 589832 | tf_op jit(solution)/shard_map/ppermute | solution.py:422
  105.6 8.3 %collective-permute-start.15 = (bf16[96,1024]{1,0:T(8,128)(2,1)S(1)}, bf16[96,1024]{1,0:T(8,128)(2,1)S(1)}, u32[]{:S(2)}, u32[]{:S(2)}) collective-permute-start(bf16[96,1024]{1,0:T(8,128)(2,1)S(1)} %get-tuple-element.81.g0), channel_id=1, source_target_pairs={{0,6},{2,0},{4,2},{6,4},{1,7},{3,1},{5,3},{7,5},{8,14},{10,8},{12,... | collective-permute-start | bytes 589832 | tf_op jit(solution)/shard_map/ppermute | solution.py:422
  120.1 46.0 %all-to-all-start.1 = ((bf16[64,8,2688]{2,1,0:T(8,128)(2,1)}), bf16[64,8,2688]{2,1,0:T(8,128)(2,1)}, u32[]{:S(2)}, u32[]{:S(2)}) async-start(bf16[64,8,2688]{2,1,0:T(8,128)(2,1)} %bitcast.9), calls=%async_computation.1 | async-start | bytes 5505024 | tf_op jit(solution)/shard_map/all_to_all | solution.py:426
  130.5 4.3 %collective-permute-start.22 = (bf16[384,1024]{1,0:T(8,128)(2,1)S(1)}, bf16[384,1024]{1,0:T(8,128)(2,1)S(1)}, u32[]{:S(2)}, u32[]{:S(2)}) collective-permute-start(bf16[384,1024]{1,0:T(8,128)(2,1)S(1)} %get-tuple-element.92.bm_ref), channel_id=1, source_target_pairs={{0,1},{1,0},{2,3},{3,2},{4,5},{5,4},{6,7},{7,6},{8,9},{9,8},{10,11... | collective-permute-start | bytes 2359304 | tf_op jit(solution)/shard_map/ppermute | solution.py:419
  130.5 4.2 %collective-permute-start.21 = (bf16[384,896]{1,0:T(8,128)(2,1)S(1)}, bf16[384,896]{1,0:T(8,128)(2,1)S(1)}, u32[]{:S(2)}, u32[]{:S(2)}) collective-permute-start(bf16[384,896]{1,0:T(8,128)(2,1)S(1)} %get-tuple-element.91.other_ref), channel_id=1, source_target_pairs={{0,1},{1,0},{2,3},{3,2},{4,5},{5,4},{6,7},{7,6},{8,9},{9,8},{10,11... | collective-permute-start | bytes 2064392 | tf_op jit(solution)/shard_map/ppermute | solution.py:419
  131.0 8.6 %collective-permute-start.23 = (bf16[384,1024]{1,0:T(8,128)(2,1)S(1)}, bf16[384,1024]{1,0:T(8,128)(2,1)S(1)}, u32[]{:S(2)}, u32[]{:S(2)}) collective-permute-start(bf16[384,1024]{1,0:T(8,128)(2,1)S(1)} %get-tuple-element.93.bm_ref), channel_id=1, source_target_pairs={{0,1},{1,0},{2,3},{3,2},{4,5},{5,4},{6,7},{7,6},{8,9},{9,8},{10,11... | collective-permute-start | bytes 2359304 | tf_op jit(solution)/shard_map/ppermute | solution.py:419
  131.1 12.3 %collective-permute-start.24 = (bf16[384,1024]{1,0:T(8,128)(2,1)S(1)}, bf16[384,1024]{1,0:T(8,128)(2,1)S(1)}, u32[]{:S(2)}, u32[]{:S(2)}) collective-permute-start(bf16[384,1024]{1,0:T(8,128)(2,1)S(1)} %get-tuple-element.94.am_ref), channel_id=1, source_target_pairs={{0,1},{1,0},{2,3},{3,2},{4,5},{5,4},{6,7},{7,6},{8,9},{9,8},{10,11... | collective-permute-start | bytes 2359304 | tf_op jit(solution)/shard_map/ppermute | solution.py:419
  131.6 11.8 %collective-permute-start.25 = (bf16[384,896]{1,0:T(8,128)(2,1)}, bf16[384,896]{1,0:T(8,128)(2,1)S(1)}, u32[]{:S(2)}, u32[]{:S(2)}) collective-permute-start(bf16[384,896]{1,0:T(8,128)(2,1)} %copy-done.4), channel_id=1, source_target_pairs={{0,1},{1,0},{2,3},{3,2},{4,5},{5,4},{6,7},{7,6},{8,9},{9,8},{10,11... | collective-permute-start | bytes 2064392 | tf_op jit(solution)/shard_map/ppermute | solution.py:419
  134.8 1.1 copy-start.6
  139.6 3.8 %copy-start.8 = (bf16[384,896]{1,0:T(8,128)(2,1)S(1)}, bf16[384,896]{1,0:T(8,128)(2,1)}, u32[]{:S(2)}) copy-start(bf16[384,896]{1,0:T(8,128)(2,1)} %copy-done.7) | copy-start | bytes 2064388

commit v4 on v3

--- a/solution.py
+++ b/solution.py
@@ -141,10 +141,10 @@
         out[...] = total_s[rows, :].astype(out.dtype)
 
 
-def gate_kernel(at_ref, recv_any, wo_ref, wx_ref, p0_ref, p1_ref, p2_ref, p3_ref, own_ref, other_ref, kept_any, total_s, recv_s, sems):
+def unpack_kernel(recv_any, wx_ref, own_ref, other_ref, total_ref, _, recv_s, sems):
     quarters, lanes, _ = recv_any.shape
-    half = wo_ref.shape[0]
-    slots = p0_ref.shape[0]
+    half = own_ref.shape[1]
+    slots = own_ref.shape[0] // quarters
     pairs = quarters // 2
     copies = start([(recv_any.at[pl.ds(2 * p, 2), :, pl.ds(0, 2 * half)], recv_s.at[p]) for p in range(pairs)], sems)
     main = slot_masks(2 * slots, 2 * lanes)[0]
@@ -154,7 +154,37 @@
         block = jnp.concatenate([recv_s[p, 0], recv_s[p, 1]], axis=0)
         own_ref[rows, :] = dot(main, block[:, :half]).astype(BF16)
         other_ref[rows, :] = dot(main, block[:, half:]).astype(BF16)
-    total_s[...] = dot(own_ref[...], wo_ref[...]) + dot(other_ref[...], wx_ref[...])
+    total_ref[...] = dot(other_ref[...], wx_ref[...])
+
+
+def unpack_x(recv, other_weight, slots):
+    quarters, lanes, _ = recv.shape
+    half, hidden = other_weight.shape
+    anywhere = pl.BlockSpec(memory_space=pl.ANY)
+    rows = jax.ShapeDtypeStruct((quarters * slots, half), BF16)
+    return pl.pallas_call(
+        unpack_kernel,
+        in_specs=[anywhere, whole()],
+        out_specs=[whole()] * 3 + [anywhere],
+        out_shape=[
+            rows,
+            rows,
+            jax.ShapeDtypeStruct((quarters * slots, hidden), F32),
+            jax.ShapeDtypeStruct(recv.shape, BF16),
+        ],
+        scratch_shapes=[
+            pltpu.VMEM((quarters // 2, 2, lanes, 2 * half), BF16),
+            pltpu.SemaphoreType.DMA((quarters // 2,)),
+        ],
+        input_output_aliases={0: 3},
+        compiler_params=pltpu.CompilerParams(vmem_limit_bytes=VMEM_LIMIT),
+        cost_estimate=pl.CostEstimate(flops=2_000_000_000, bytes_accessed=6_000_000, transcendentals=0),
+        name="unpack_x",
+    )(recv, other_weight)
+
+
+def gate_kernel(at_ref, own_ref, part_ref, wo_ref, p0_ref, p1_ref, p2_ref, p3_ref, total_s):
+    total_s[...] = part_ref[...] + dot(own_ref[...], wo_ref[...])
     share_out(at_ref, total_s, (p0_ref, p1_ref, p2_ref, p3_ref))
 
 
@@ -180,29 +210,14 @@
 def projection(kernel, name, at, rows, weights, over, slots, quarters):
     half, hidden = weights[0].shape[over], weights[0].shape[1 - over]
     outs = [jax.ShapeDtypeStruct((slots, hidden), F32 if j == 0 else BF16) for j in range(quarters)]
-    scratch = [pltpu.VMEM((quarters * slots, hidden), F32)]
     if len(rows) == 1:
         outs = outs + [jax.ShapeDtypeStruct((quarters * slots, half), BF16)] * 2
-    in_specs = [smem()] + [whole()] * (len(rows) + 2)
-    out_specs = [whole()] * len(outs)
-    aliases = {}
-    if kernel is gate_kernel:
-        anywhere = pl.BlockSpec(memory_space=pl.ANY)
-        in_specs[1] = anywhere
-        outs.append(jax.ShapeDtypeStruct(rows[0].shape, BF16))
-        out_specs.append(anywhere)
-        aliases = {1: len(outs) - 1}
-        scratch += [
-            pltpu.VMEM((quarters // 2, 2, rows[0].shape[1], 2 * half), BF16),
-            pltpu.SemaphoreType.DMA((quarters // 2,)),
-        ]
     return pl.pallas_call(
         kernel,
-        in_specs=in_specs,
-        out_specs=out_specs,
+        in_specs=[smem()] + [whole()] * (len(rows) + len(weights)),
+        out_specs=[whole()] * len(outs),
         out_shape=outs,
-        scratch_shapes=scratch,
-        input_output_aliases=aliases,
+        scratch_shapes=[pltpu.VMEM((quarters * slots, hidden), F32)],
         compiler_params=pltpu.CompilerParams(vmem_limit_bytes=VMEM_LIMIT),
         cost_estimate=pl.CostEstimate(flops=3_000_000_000, bytes_accessed=8_000_000, transcendentals=0),
         name=name,
@@ -293,12 +308,9 @@
             value = tails[2 * q * lanes : 2 * (q + 1) * lanes]
             if q == 2:
                 value = value + dot(masks[0], own[rows])
-            else:
-                mine = jnp.concatenate([main_ref[2 * p, :, columns], main_ref[2 * p + 1, :, columns]], axis=0)
-                value = value + mine.astype(F32)
-            value = value.astype(BF16)
-            out_ref[2 * p, :, columns] = value[:lanes]
-            out_ref[2 * p + 1, :, columns] = value[lanes:]
+            for i in range(2):
+                part = value[i * lanes : (i + 1) * lanes].astype(BF16)
+                out_ref[2 * p + i, :, columns] = part if q == 2 else part + main_ref[2 * p + i, :, columns]
     keep.wait()
 
 
@@ -432,7 +444,8 @@
         return total
 
     def from_y(value):
-        return [value] + [along(value, quarters - j) for j in range(1, quarters)]
+        got = {j: along(value, quarters - j) for j in (2, 1, 3)}
+        return [value, got[1], got[2], got[3]]
 
     gate_own, up_own, down_own = w_gate[0], w_up[0], w_down[0]
     gate_other, up_other, down_other = to_partner(gate_own), to_partner(up_own), to_partner(down_own)
@@ -441,8 +454,8 @@
     sent, sel, wsel = prep(core, routes, route_weight, tokens, grad_out, quarters, experts)
     recv = exchange(sent)
     down = (down_own, down_other)
-    *shares, x_own, x_other, recv = projection(gate_kernel, "gate", at, (recv,), (gate_own, gate_other), 0, slots, quarters)
-    gate = add_over_y(shares)
+    x_own, x_other, part, recv = unpack_x(recv, gate_other, slots)
+    gate = add_over_y(projection(gate_kernel, "gate", at, (x_own, part), (gate_own,), 0, slots, quarters))
     shares = projection(up_kernel, "up", at, (x_own, x_other), (up_own, up_other), 0, slots, quarters)
     up = add_over_y(shares)
     *shares, d_own, d_other = projection(back_kernel, "back", at, (recv,), down, 1, slots, quarters)

time: 173 us -> 172 us (level)
    pallas_call x3 -> x4, Pallas kernels: 12.2 us -> 12.4 us  [the longest x3 9.03 us: projection(): pl.pallas_call(kernel, in_specs=[smem()] + [whole()] * (len(rows) + len(w...]
where the time goes in v4:
time: 172 us
  waiting for transfers between devices  71.1 us (41%)
  Pallas kernels  48.9 us (28%)
  starting transfers between devices  48.9 us (28%)
    all_to_all x2, waiting for transfers between devices, exchange(): return lax.all_to_all(flat, everyone, 0, 0, tiled=True).reshape(value.shape)  51.4 us
    ppermute x18, starting transfers between devices, along(): lax.ppermute(value, 'y', [(i, (i + shift) % quarters) for i in range(quar...  25.1 us
    all_to_all x2, starting transfers between devices, exchange(): return lax.all_to_all(flat, everyone, 0, 0, tiled=True).reshape(value.shape)  21.9 us
    ppermute x18, waiting for transfers between devices, along(): lax.ppermute(value, 'y', [(i, (i + shift) % quarters) for i in range(quar...  13 us
    pallas_call x3, Pallas kernels, weight_grad(): pl.pallas_call(weight_kernel, grid=(columns // step,), in_specs=[a_spec,...  11 us
    pallas_call x3, Pallas kernels, projection(): pl.pallas_call(kernel, in_specs=[smem()] + [whole()] * (len(rows) + len(w...  9.03 us
    ppermute x8, waiting for transfers between devices, to_partner(): return lax.ppermute(value, 'k', [(0, 1), (1, 0)])  6.67 us
    pallas_call x1, Pallas kernels, last(): pl.pallas_call(last_kernel, grid=(quarters,), in_specs=[smem(), whole(),...  6.53 us
  transfers between devices with their start and end apart: 28, of which 11 were waited for; matrix products, arithmetic and copies ran while one was open for 0% of the time, Pallas kernels for 18%

profile of v4, /device:TPU:0, one launch (start us, length us, event | category | flops | bytes accessed | tf_op | source)
XLA Modules:
  0.0 171.5 jit_solution(6349390139720558873)
XLA Ops:
  0.6 5.5 %prep.1 = (bf16[4,128,2688]{2,1,0:T(8,128)(2,1)}, bf16[4,128,128]{2,1,0:T(8,128)(2,1)}, bf16[2,128,128]{2,1,0:T(8,128)(2,1)}) custom-call(s32[1]{0:T(128)} %bitcast.core_ref, s32[8,128]{1,0:T(8,128)} %bitcast.27, f32[8,128]{1,0:T(8,128)} %bitcast.26, bf16[128,7168]{1,0:T(8,128)(2,1)} %tok_ref.1, bf16[128,7168]{1,0:T(8,128)(2,1)} %go_ref.3), custom_call_target="tpu_custom_call" | custom-call | flops 800000000 | bytes 6500000 | tf_op jit(solution)/shard_map/prep/pallas_call | solution.py:98
  6.1 11.5 %all-to-all-start = ((bf16[64,8,2688]{2,1,0:T(8,128)(2,1)}), bf16[64,8,2688]{2,1,0:T(8,128)(2,1)S(1)}, u32[]{:S(2)}, u32[]{:S(2)}) async-start(bf16[64,8,2688]{2,1,0:T(8,128)(2,1)} %bitcast.25), calls=%async_computation | async-start | bytes 5505024 | tf_op jit(solution)/shard_map/all_to_all | solution.py:438
  17.7 0.5 collective-permute-start.8
  18.3 3.5 %collective-permute-done.wx_ref = bf16[896,1024]{1,0:T(8,128)(2,1)} collective-permute-done((bf16[896,1024]{1,0:T(8,128)(2,1)}, bf16[896,1024]{1,0:T(8,128)(2,1)}, u32[]{:S(2)}, u32[]{:S(2)}) %collective-permute-start) | collective-permute-done | bytes 1835040 | tf_op jit(solution)/shard_map/ppermute | solution.py:431
  21.8 32.2 %all-to-all-done = bf16[64,8,2688]{2,1,0:T(8,128)(2,1)S(1)} async-done(((bf16[64,8,2688]{2,1,0:T(8,128)(2,1)}), bf16[64,8,2688]{2,1,0:T(8,128)(2,1)S(1)}, u32[]{:S(2)}, u32[]{:S(2)}) %all-to-all-start) | async-done | bytes 2752544 | tf_op jit(solution)/shard_map/all_to_all | solution.py:438
  54.0 3.4 %unpack_x.1 = (bf16[384,896]{1,0:T(8,128)(2,1)S(1)}, bf16[384,896]{1,0:T(8,128)(2,1)S(1)}, f32[384,1024]{1,0:T(8,128)S(1)}, bf16[4,128,2688]{2,1,0:T(8,128)(2,1)S(1)}) custom-call(bf16[4,128,2688]{2,1,0:T(8,128)(2,1)S(1)} %bitcast.15, bf16[896,1024]{1,0:T(8,128)(2,1)} %collective-permute-done.wx_ref), custom_call_target="tpu_custom_call", output_to_operand_aliasing={{3}: (0, {})} | custom-call | flops 2000000000 | bytes 6000000 | tf_op jit(solution)/shard_map/unpack_x/pallas_call | solution.py:165
  57.4 1.2 gate.1
  58.6 0.9 collective-permute-start.5
  59.5 1.3 collective-permute-start.6
  60.8 1.9 %collective-permute-start.7 = (bf16[96,1024]{1,0:T(8,128)(2,1)S(1)}, bf16[96,1024]{1,0:T(8,128)(2,1)S(1)}, u32[]{:S(2)}, u32[]{:S(2)}) collective-permute-start(bf16[96,1024]{1,0:T(8,128)(2,1)S(1)} %get-tuple-element.69), channel_id=1, source_target_pairs={{0,6},{2,0},{4,2},{6,4},{1,7},{3,1},{5,3},{7,5},{8,14},{10,8},{12,... | collective-permute-start | bytes 589832 | tf_op jit(solution)/shard_map/ppermute | solution.py:434
  62.8 3.6 %up.1 = (f32[96,1024]{1,0:T(8,128)S(1)}, bf16[96,1024]{1,0:T(8,128)(2,1)S(1)}, bf16[96,1024]{1,0:T(8,128)(2,1)S(1)}, bf16[96,1024]{1,0:T(8,128)(2,1)S(1)}) custom-call(s32[1]{0:T(128)} %bitcast.3.at_ref, bf16[384,896]{1,0:T(8,128)(2,1)S(1)} %get-tuple-element.64.own_ref.am_ref, bf16[384,896]{1,0:T(8,128)(2,1)S(1)} %get-tuple-element.93.other_ref, ...), custom_call_target="tpu_custom_call" | custom-call | flops 3000000000 | bytes 8000000 | tf_op jit(solution)/shard_map/up/pallas_call | solution.py:215
  66.4 1.6 collective-permute-start.9
  67.9 3.2 %collective-permute-start.11 = (bf16[96,1024]{1,0:T(8,128)(2,1)S(1)}, bf16[96,1024]{1,0:T(8,128)(2,1)S(1)}, u32[]{:S(2)}, u32[]{:S(2)}) collective-permute-start(bf16[96,1024]{1,0:T(8,128)(2,1)S(1)} %get-tuple-element.74), channel_id=1, source_target_pairs={{0,6},{2,0},{4,2},{6,4},{1,7},{3,1},{5,3},{7,5},{8,14},{10,8},{12,... | collective-permute-start | bytes 589832 | tf_op jit(solution)/shard_map/ppermute | solution.py:434
  71.2 4.3 %back.1 = (f32[96,1024]{1,0:T(8,128)S(1)}, bf16[96,1024]{1,0:T(8,128)(2,1)S(1)}, bf16[96,1024]{1,0:T(8,128)(2,1)S(1)}, bf16[96,1024]{1,0:T(8,128)(2,1)S(1)}, bf1...) custom-call(s32[1]{0:T(128)} %bitcast.3.at_ref, bf16[4,128,2688]{2,1,0:T(8,128)(2,1)S(1)} %get-tuple-element.59.recv_ref, ...), custom_call_target="tpu_custom_call" | custom-call | flops 3000000000 | bytes 8000000 | tf_op jit(solution)/shard_map/back/pallas_call | solution.py:215
  75.5 0.9 collective-permute-start.2
  76.4 0.1 collective-permute-start.3
  76.6 3.1 %collective-permute-start.4 = (bf16[96,1024]{1,0:T(8,128)(2,1)S(1)}, bf16[96,1024]{1,0:T(8,128)(2,1)S(1)}, u32[]{:S(2)}, u32[]{:S(2)}) collective-permute-start(bf16[96,1024]{1,0:T(8,128)(2,1)S(1)} %get-tuple-element.63), channel_id=1, source_target_pairs={{0,6},{2,0},{4,2},{6,4},{1,7},{3,1},{5,3},{7,5},{8,14},{10,8},{12,... | collective-permute-start | bytes 589832 | tf_op jit(solution)/shard_map/ppermute | solution.py:434
  79.7 0.7 collective-permute-done.10
  80.4 0.3 multiply_convert_fusion.2
  80.7 1.7 %collective-permute-start.14 = (bf16[96,1024]{1,0:T(8,128)(2,1)S(1)}, bf16[96,1024]{1,0:T(8,128)(2,1)S(1)}, u32[]{:S(2)}, u32[]{:S(2)}) collective-permute-start(bf16[96,1024]{1,0:T(8,128)(2,1)S(1)} %get-tuple-element.78.h0), channel_id=1, source_target_pairs={{0,2},{2,4},{4,6},{6,0},{1,3},{3,5},{5,7},{7,1},{8,10},{10,12},{12... | collective-permute-start | bytes 589832 | tf_op jit(solution)/shard_map/ppermute | solution.py:434
  82.5 1.1 collective-permute-start.13
  83.5 1.4 collective-permute-done.2
  84.9 0.3 collective-permute-start.12
  85.2 3.4 %collective-permute-done.3 = bf16[96,1024]{1,0:T(8,128)(2,1)S(1)} collective-permute-done((bf16[96,1024]{1,0:T(8,128)(2,1)S(1)}, bf16[96,1024]{1,0:T(8,128)(2,1)S(1)}, u32[]{:S(2)}, u32[]{:S(2)}) %collective-permute-start.3) | collective-permute-done | bytes 196640 | tf_op jit(solution)/shard_map/ppermute | solution.py:434
  88.6 0.6 collective-permute-done.4
  89.2 0.1 convert_add_fusion.2
  89.3 2.5 %collective-permute-done.14.h3 = bf16[96,1024]{1,0:T(8,128)(2,1)S(1)} collective-permute-done((bf16[96,1024]{1,0:T(8,128)(2,1)S(1)}, bf16[96,1024]{1,0:T(8,128)(2,1)S(1)}, u32[]{:S(2)}, u32[]{:S(2)}) %collective-permute-start.14) | collective-permute-done | bytes 196640 | tf_op jit(solution)/shard_map/ppermute | solution.py:434
  91.8 2.2 %collective-permute-done.13.h2 = bf16[96,1024]{1,0:T(8,128)(2,1)S(1)} collective-permute-done((bf16[96,1024]{1,0:T(8,128)(2,1)S(1)}, bf16[96,1024]{1,0:T(8,128)(2,1)S(1)}, u32[]{:S(2)}, u32[]{:S(2)}) %collective-permute-start.13) | collective-permute-done | bytes 196640 | tf_op jit(solution)/shard_map/ppermute | solution.py:434
  94.0 0.5 collective-permute-start.20
  94.6 2.4 %collective-permute-start.19 = (bf16[96,1024]{1,0:T(8,128)(2,1)S(1)}, bf16[96,1024]{1,0:T(8,128)(2,1)S(1)}, u32[]{:S(2)}, u32[]{:S(2)}) collective-permute-start(bf16[96,1024]{1,0:T(8,128)(2,1)S(1)} %get-tuple-element.109.g0), channel_id=1, source_target_pairs={{0,4},{2,6},{4,0},{6,2},{1,5},{3,7},{5,1},{7,3},{8,12},{10,14},{12... | collective-permute-start | bytes 589832 | tf_op jit(solution)/shard_map/ppermute | solution.py:434
  97.0 0.9 collective-permute-start.18
  97.9 3.9 %out_rows.1 = (bf16[4,128,1792]{2,1,0:T(8,128)(2,1)S(1)}, bf16[384,1024]{1,0:T(8,128)(2,1)S(1)}) custom-call(s32[1]{0:T(128)} %bitcast.3.at_ref, bf16[96,1024]{1,0:T(8,128)(2,1)S(1)} %get-tuple-element.78.h0, bf16[96,1024]{1,0:T(8,128)(2,1)S(1)} %collective-permute-done.12.h1, bf16[96,1024]{1,0:T(8,128)(2,1)S(1)} %collective-permute-done.13.h2, ...), custom_call_target="tpu_custom_call" | custom-call | flops 2000000000 | bytes 7500000 | tf_op jit(solution)/shard_map/out_rows/pallas_call | solution.py:253
  101.8 1.2 collective-permute-start.17
  102.9 1.4 collective-permute-start.16
  104.3 2.5 %collective-permute-start.15 = (bf16[96,1024]{1,0:T(8,128)(2,1)S(1)}, bf16[96,1024]{1,0:T(8,128)(2,1)S(1)}, u32[]{:S(2)}, u32[]{:S(2)}) collective-permute-start(bf16[96,1024]{1,0:T(8,128)(2,1)S(1)} %get-tuple-element.83.g0), channel_id=1, source_target_pairs={{0,6},{2,0},{4,2},{6,4},{1,7},{3,1},{5,3},{7,5},{8,14},{10,8},{12,... | collective-permute-start | bytes 589832 | tf_op jit(solution)/shard_map/ppermute | solution.py:434
  106.9 3.4 %half_grad.1 = (f32[384,896]{1,0:T(8,128)S(1)}, f32[384,896]{1,0:T(8,128)S(1)}, bf16[384,1024]{1,0:T(8,128)(2,1)S(1)}) custom-call(s32[1]{0:T(128)} %bitcast.3.at_ref, bf16[96,1024]{1,0:T(8,128)(2,1)S(1)} %get-tuple-element.109.g0, bf16[96,1024]{1,0:T(8,128)(2,1)S(1)} %collective-permute-done.18.g1, bf16[96,1024]{1,0:T(8,128)(2,1)S(1)} %collective-permute-done.19.g2, ...), custom_call_target="tpu_custom_call" | custom-call | flops 1500000000 | bytes 8000000 | tf_op jit(solution)/shard_map/half_grad/pallas_call | solution.py:280
  110.3 2.2 %collective-permute-done.17.g3 = bf16[96,1024]{1,0:T(8,128)(2,1)S(1)} collective-permute-done((bf16[96,1024]{1,0:T(8,128)(2,1)S(1)}, bf16[96,1024]{1,0:T(8,128)(2,1)S(1)}, u32[]{:S(2)}, u32[]{:S(2)}) %collective-permute-start.17) | collective-permute-done | bytes 196640 | tf_op jit(solution)/shard_map/ppermute | solution.py:434
  112.5 6.2 %grad_rows.1 = (bf16[4,128,2688]{2,1,0:T(8,128)(2,1)}, bf16[384,1024]{1,0:T(8,128)(2,1)S(1)}) custom-call(s32[1]{0:T(128)} %bitcast.3.at_ref, bf16[96,1024]{1,0:T(8,128)(2,1)S(1)} %get-tuple-element.83.g0, bf16[96,1024]{1,0:T(8,128)(2,1)S(1)} %collective-permute-done.15.g1, bf16[96,1024]{1,0:T(8,128)(2,1)S(1)} %collective-permute-done.16.g2, ...), custom_call_target="tpu_custom_call" | custom-call | flops 2500000000 | bytes 14000000 | tf_op jit(solution)/shard_map/grad_rows/pallas_call | solution.py:320
  118.7 10.4 %all-to-all-start.1 = ((bf16[64,8,2688]{2,1,0:T(8,128)(2,1)}), bf16[64,8,2688]{2,1,0:T(8,128)(2,1)}, u32[]{:S(2)}, u32[]{:S(2)}) async-start(bf16[64,8,2688]{2,1,0:T(8,128)(2,1)} %bitcast.9), calls=%async_computation.1 | async-start | bytes 5505024 | tf_op jit(solution)/shard_map/all_to_all | solution.py:438
  129.2 0.5 collective-permute-start.21
  129.8 0.4 collective-permute-start.24
  130.3 3.1 %collective-permute-done.21.ap_ref = bf16[384,896]{1,0:T(8,128)(2,1)S(1)} collective-permute-done((bf16[384,896]{1,0:T(8,128)(2,1)S(1)}, bf16[384,896]{1,0:T(8,128)(2,1)S(1)}, u32[]{:S(2)}, u32[]{:S(2)}) %collective-permute-start.21) | collective-permute-done | bytes 688160 | tf_op jit(solution)/shard_map/ppermute | solution.py:431
  133.5 1.1 copy-done.5
  134.6 3.7 %weight_grad.3 = bf16[896,1024]{1,0:T(8,128)(2,1)} custom-call(bf16[384,896]{1,0:T(8,128)(2,1)S(1)} %copy-done.5, bf16[384,896]{1,0:T(8,128)(2,1)S(1)} %collective-permute-done.21.ap_ref, bf16[384,1024]{1,0:T(8,128)(2,1)S(1)} %get-tuple-element.94.bm_ref, bf16[384,1024]{1,0:T(8,128)(2,1)S(1)} %collective-permute-done.22.bp_ref), custom_call_target="tpu_custom_call" | custom-call | flops 1500000000 | bytes 5000000 | tf_op jit(solution)/shard_map/weight_grad/pallas_call | solution.py:344
  138.3 3.8 %weight_grad.4 = bf16[896,1024]{1,0:T(8,128)(2,1)} custom-call(bf16[384,896]{1,0:T(8,128)(2,1)S(1)} %copy-done.5, bf16[384,896]{1,0:T(8,128)(2,1)S(1)} %collective-permute-done.21.ap_ref, bf16[384,1024]{1,0:T(8,128)(2,1)S(1)} %get-tuple-element.95.bm_ref, bf16[384,1024]{1,0:T(8,128)(2,1)S(1)} %collective-permute-done.23.bp_ref), custom_call_target="tpu_custom_call" | custom-call | flops 1500000000 | bytes 5000000 | tf_op jit(solution)/shard_map/weight_grad/pallas_call | solution.py:344
  142.1 3.5 %weight_grad.5 = bf16[1024,896]{1,0:T(8,128)(2,1)} custom-call(bf16[384,1024]{1,0:T(8,128)(2,1)S(1)} %get-tuple-element.96.am_ref, bf16[384,1024]{1,0:T(8,128)(2,1)S(1)} %collective-permute-done.24.ap_ref, bf16[384,896]{1,0:T(8,128)(2,1)S(1)} %copy-done.7, bf16[384,896]{1,0:T(8,128)(2,1)S(1)} %collective-permute-done.25.bp_ref), custom_call_target="tpu_custom_call" | custom-call | flops 1500000000 | bytes 5000000 | tf_op jit(solution)/shard_map/weight_grad/pallas_call | solution.py:344
  145.6 19.2 %all-to-all-done.1 = bf16[64,8,2688]{2,1,0:T(8,128)(2,1)} async-done(((bf16[64,8,2688]{2,1,0:T(8,128)(2,1)}), bf16[64,8,2688]{2,1,0:T(8,128)(2,1)}, u32[]{:S(2)}, u32[]{:S(2)}) %all-to-all-start.1) | async-done | bytes 2752544 | tf_op jit(solution)/shard_map/all_to_all | solution.py:438
  164.8 6.5 %last.1 = (bf16[128,7168]{1,0:T(8,128)(2,1)}, bf16[128,7168]{1,0:T(8,128)(2,1)}, f32[8,128]{1,0:T(8,128)}) custom-call(s32[1]{0:T(128)} %bitcast.core_ref, s32[8,128]{1,0:T(8,128)} %bitcast.28, bf16[4,128,128]{2,1,0:T(8,128)(2,1)} %get-tuple-element.56.sel_ref, bf16[2,128,128]{2,1,0:T(8,128)(2,1)} %get-tuple-element.57.wsel_ref, ...), custom_call_target="tpu_custom_call" | custom-call | flops 1500000000 | bytes 8500000 | tf_op jit(solution)/shard_map/last/pallas_call | solution.py:402
  (39 shorter events, 0.6 us)
Async XLA Ops:
  6.1 47.9 %all-to-all-start = ((bf16[64,8,2688]{2,1,0:T(8,128)(2,1)}), bf16[64,8,2688]{2,1,0:T(8,128)(2,1)S(1)}, u32[]{:S(2)}, u32[]{:S(2)}) async-start(bf16[64,8,2688]{2,1,0:T(8,128)(2,1)} %bitcast.25), calls=%async_computation | async-start | bytes 5505024 | tf_op jit(solution)/shard_map/all_to_all | solution.py:438
  17.6 4.2 %collective-permute-start = (bf16[896,1024]{1,0:T(8,128)(2,1)}, bf16[896,1024]{1,0:T(8,128)(2,1)}, u32[]{:S(2)}, u32[]{:S(2)}) collective-permute-start(bf16[896,1024]{1,0:T(8,128)(2,1)} %bitcast.19), channel_id=1, source_target_pairs={{0,1},{1,0},{2,3},{3,2},{4,5},{5,4},{6,7},{7,6},{8,9},{9,8},{10,11... | collective-permute-start | bytes 5505032 | tf_op jit(solution)/shard_map/ppermute | solution.py:431
  17.7 45.1 %collective-permute-start.8 = (bf16[896,1024]{1,0:T(8,128)(2,1)}, bf16[896,1024]{1,0:T(8,128)(2,1)}, u32[]{:S(2)}, u32[]{:S(2)}) collective-permute-start(bf16[896,1024]{1,0:T(8,128)(2,1)} %bitcast.22), channel_id=1, source_target_pairs={{0,1},{1,0},{2,3},{3,2},{4,5},{5,4},{6,7},{7,6},{8,9},{9,8},{10,11... | collective-permute-start | bytes 5505032 | tf_op jit(solution)/shard_map/ppermute | solution.py:431
  18.2 49.7 %collective-permute-start.1 = (bf16[1024,896]{1,0:T(8,128)(2,1)}, bf16[1024,896]{1,0:T(8,128)(2,1)}, u32[]{:S(2)}, u32[]{:S(2)}) collective-permute-start(bf16[1024,896]{1,0:T(8,128)(2,1)} %bitcast.16), channel_id=1, source_target_pairs={{0,1},{1,0},{2,3},{3,2},{4,5},{5,4},{6,7},{7,6},{8,9},{9,8},{10,11... | collective-permute-start | bytes 5505032 | tf_op jit(solution)/shard_map/ppermute | solution.py:431
  54.0 3.4 %copy-start.1 = (bf16[1,896,1024]{2,1,0:T(8,128)(2,1)S(1)}, bf16[1,896,1024]{2,1,0:T(8,128)(2,1)}, u32[]{:S(2)}) copy-start(bf16[1,896,1024]{2,1,0:T(8,128)(2,1)} %param.10) | copy-start | bytes 5505028
  57.4 5.4 %copy-start.4 = (bf16[384,896]{1,0:T(8,128)(2,1)}, bf16[384,896]{1,0:T(8,128)(2,1)S(1)}, u32[]{:S(2)}) copy-start(bf16[384,896]{1,0:T(8,128)(2,1)S(1)} %get-tuple-element.64.own_ref.am_ref) | copy-start | bytes 2064388
  57.4 5.3 %copy-start.2 = (bf16[1,896,1024]{2,1,0:T(8,128)(2,1)S(1)}, bf16[1,896,1024]{2,1,0:T(8,128)(2,1)}, u32[]{:S(2)}) copy-start(bf16[1,896,1024]{2,1,0:T(8,128)(2,1)} %param.11) | copy-start | bytes 5505028
  58.6 9.3 %collective-permute-start.5 = (bf16[96,1024]{1,0:T(8,128)(2,1)S(1)}, bf16[96,1024]{1,0:T(8,128)(2,1)S(1)}, u32[]{:S(2)}, u32[]{:S(2)}) collective-permute-start(bf16[96,1024]{1,0:T(8,128)(2,1)S(1)} %get-tuple-element.67), channel_id=1, source_target_pairs={{0,4},{2,6},{4,0},{6,2},{1,5},{3,7},{5,1},{7,3},{8,12},{10,14},{12... | collective-permute-start | bytes 589832 | tf_op jit(solution)/shard_map/ppermute | solution.py:434
  59.5 16.0 %collective-permute-start.6 = (bf16[96,1024]{1,0:T(8,128)(2,1)S(1)}, bf16[96,1024]{1,0:T(8,128)(2,1)S(1)}, u32[]{:S(2)}, u32[]{:S(2)}) collective-permute-start(bf16[96,1024]{1,0:T(8,128)(2,1)S(1)} %get-tuple-element.68), channel_id=1, source_target_pairs={{0,2},{2,4},{4,6},{6,0},{1,3},{3,5},{5,7},{7,1},{8,10},{10,12},{12... | collective-permute-start | bytes 589832 | tf_op jit(solution)/shard_map/ppermute | solution.py:434
  60.8 15.6 %collective-permute-start.7 = (bf16[96,1024]{1,0:T(8,128)(2,1)S(1)}, bf16[96,1024]{1,0:T(8,128)(2,1)S(1)}, u32[]{:S(2)}, u32[]{:S(2)}) collective-permute-start(bf16[96,1024]{1,0:T(8,128)(2,1)S(1)} %get-tuple-element.69), channel_id=1, source_target_pairs={{0,6},{2,0},{4,2},{6,4},{1,7},{3,1},{5,3},{7,5},{8,14},{10,8},{12,... | collective-permute-start | bytes 589832 | tf_op jit(solution)/shard_map/ppermute | solution.py:434
  62.8 8.4 %copy-start = (bf16[1,1024,896]{2,1,0:T(8,128)(2,1)S(1)}, bf16[1,1024,896]{2,1,0:T(8,128)(2,1)}, u32[]{:S(2)}) copy-start(bf16[1,1024,896]{2,1,0:T(8,128)(2,1)} %param.12) | copy-start | bytes 5505028
  66.4 10.2 %collective-permute-start.9 = (bf16[96,1024]{1,0:T(8,128)(2,1)S(1)}, bf16[96,1024]{1,0:T(8,128)(2,1)S(1)}, u32[]{:S(2)}, u32[]{:S(2)}) collective-permute-start(bf16[96,1024]{1,0:T(8,128)(2,1)S(1)} %get-tuple-element.72), channel_id=1, source_target_pairs={{0,4},{2,6},{4,0},{6,2},{1,5},{3,7},{5,1},{7,3},{8,12},{10,14},{12... | collective-permute-start | bytes 589832 | tf_op jit(solution)/shard_map/ppermute | solution.py:434
  67.9 12.5 %collective-permute-start.10 = (bf16[96,1024]{1,0:T(8,128)(2,1)S(1)}, bf16[96,1024]{1,0:T(8,128)(2,1)S(1)}, u32[]{:S(2)}, u32[]{:S(2)}) collective-permute-start(bf16[96,1024]{1,0:T(8,128)(2,1)S(1)} %get-tuple-element.73), channel_id=1, source_target_pairs={{0,2},{2,4},{4,6},{6,0},{1,3},{3,5},{5,7},{7,1},{8,10},{10,12},{12... | collective-permute-start | bytes 589832 | tf_op jit(solution)/shard_map/ppermute | solution.py:434
  67.9 12.5 %collective-permute-start.11 = (bf16[96,1024]{1,0:T(8,128)(2,1)S(1)}, bf16[96,1024]{1,0:T(8,128)(2,1)S(1)}, u32[]{:S(2)}, u32[]{:S(2)}) collective-permute-start(bf16[96,1024]{1,0:T(8,128)(2,1)S(1)} %get-tuple-element.74), channel_id=1, source_target_pairs={{0,6},{2,0},{4,2},{6,4},{1,7},{3,1},{5,3},{7,5},{8,14},{10,8},{12,... | collective-permute-start | bytes 589832 | tf_op jit(solution)/shard_map/ppermute | solution.py:434
  75.5 13.8 %copy-start.6 = (bf16[384,896]{1,0:T(8,128)(2,1)}, bf16[384,896]{1,0:T(8,128)(2,1)S(1)}, u32[]{:S(2)}) copy-start(bf16[384,896]{1,0:T(8,128)(2,1)S(1)} %get-tuple-element.97.bm_ref) | copy-start | bytes 2064388
  75.5 21.5 %copy-start.3 = (bf16[384,896]{1,0:T(8,128)(2,1)}, bf16[384,896]{1,0:T(8,128)(2,1)S(1)}, u32[]{:S(2)}) copy-start(bf16[384,896]{1,0:T(8,128)(2,1)S(1)} %get-tuple-element.98) | copy-start | bytes 2064388
  75.5 9.4 %collective-permute-start.2 = (bf16[96,1024]{1,0:T(8,128)(2,1)S(1)}, bf16[96,1024]{1,0:T(8,128)(2,1)S(1)}, u32[]{:S(2)}, u32[]{:S(2)}) collective-permute-start(bf16[96,1024]{1,0:T(8,128)(2,1)S(1)} %get-tuple-element.61), channel_id=1, source_target_pairs={{0,4},{2,6},{4,0},{6,2},{1,5},{3,7},{5,1},{7,3},{8,12},{10,14},{12... | collective-permute-start | bytes 589832 | tf_op jit(solution)/shard_map/ppermute | solution.py:434
  76.4 12.2 %collective-permute-start.3 = (bf16[96,1024]{1,0:T(8,128)(2,1)S(1)}, bf16[96,1024]{1,0:T(8,128)(2,1)S(1)}, u32[]{:S(2)}, u32[]{:S(2)}) collective-permute-start(bf16[96,1024]{1,0:T(8,128)(2,1)S(1)} %get-tuple-element.62), channel_id=1, source_target_pairs={{0,2},{2,4},{4,6},{6,0},{1,3},{3,5},{5,7},{7,1},{8,10},{10,12},{12... | collective-permute-start | bytes 589832 | tf_op jit(solution)/shard_map/ppermute | solution.py:434
  76.6 12.6 %collective-permute-start.4 = (bf16[96,1024]{1,0:T(8,128)(2,1)S(1)}, bf16[96,1024]{1,0:T(8,128)(2,1)S(1)}, u32[]{:S(2)}, u32[]{:S(2)}) collective-permute-start(bf16[96,1024]{1,0:T(8,128)(2,1)S(1)} %get-tuple-element.63), channel_id=1, source_target_pairs={{0,6},{2,0},{4,2},{6,4},{1,7},{3,1},{5,3},{7,5},{8,14},{10,8},{12,... | collective-permute-start | bytes 589832 | tf_op jit(solution)/shard_map/ppermute | solution.py:434
  80.7 11.0 %collective-permute-start.14 = (bf16[96,1024]{1,0:T(8,128)(2,1)S(1)}, bf16[96,1024]{1,0:T(8,128)(2,1)S(1)}, u32[]{:S(2)}, u32[]{:S(2)}) collective-permute-start(bf16[96,1024]{1,0:T(8,128)(2,1)S(1)} %get-tuple-element.78.h0), channel_id=1, source_target_pairs={{0,2},{2,4},{4,6},{6,0},{1,3},{3,5},{5,7},{7,1},{8,10},{10,12},{12... | collective-permute-start | bytes 589832 | tf_op jit(solution)/shard_map/ppermute | solution.py:434
  82.5 11.5 %collective-permute-start.13 = (bf16[96,1024]{1,0:T(8,128)(2,1)S(1)}, bf16[96,1024]{1,0:T(8,128)(2,1)S(1)}, u32[]{:S(2)}, u32[]{:S(2)}) collective-permute-start(bf16[96,1024]{1,0:T(8,128)(2,1)S(1)} %get-tuple-element.78.h0), channel_id=1, source_target_pairs={{0,4},{2,6},{4,0},{6,2},{1,5},{3,7},{5,1},{7,3},{8,12},{10,14},{12... | collective-permute-start | bytes 589832 | tf_op jit(solution)/shard_map/ppermute | solution.py:434
  84.9 9.0 %collective-permute-start.12 = (bf16[96,1024]{1,0:T(8,128)(2,1)S(1)}, bf16[96,1024]{1,0:T(8,128)(2,1)S(1)}, u32[]{:S(2)}, u32[]{:S(2)}) collective-permute-start(bf16[96,1024]{1,0:T(8,128)(2,1)S(1)} %get-tuple-element.78.h0), channel_id=1, source_target_pairs={{0,6},{2,0},{4,2},{6,4},{1,7},{3,1},{5,3},{7,5},{8,14},{10,8},{12,... | collective-permute-start | bytes 589832 | tf_op jit(solution)/shard_map/ppermute | solution.py:434
  94.0 10.3 %collective-permute-start.20 = (bf16[96,1024]{1,0:T(8,128)(2,1)S(1)}, bf16[96,1024]{1,0:T(8,128)(2,1)S(1)}, u32[]{:S(2)}, u32[]{:S(2)}) collective-permute-start(bf16[96,1024]{1,0:T(8,128)(2,1)S(1)} %get-tuple-element.109.g0), channel_id=1, source_target_pairs={{0,2},{2,4},{4,6},{6,0},{1,3},{3,5},{5,7},{7,1},{8,10},{10,12},{12... | collective-permute-start | bytes 589832 | tf_op jit(solution)/shard_map/ppermute | solution.py:434
  94.6 12.3 %collective-permute-start.19 = (bf16[96,1024]{1,0:T(8,128)(2,1)S(1)}, bf16[96,1024]{1,0:T(8,128)(2,1)S(1)}, u32[]{:S(2)}, u32[]{:S(2)}) collective-permute-start(bf16[96,1024]{1,0:T(8,128)(2,1)S(1)} %get-tuple-element.109.g0), channel_id=1, source_target_pairs={{0,4},{2,6},{4,0},{6,2},{1,5},{3,7},{5,1},{7,3},{8,12},{10,14},{12... | collective-permute-start | bytes 589832 | tf_op jit(solution)/shard_map/ppermute | solution.py:434
  97.0 9.9 %collective-permute-start.18 = (bf16[96,1024]{1,0:T(8,128)(2,1)S(1)}, bf16[96,1024]{1,0:T(8,128)(2,1)S(1)}, u32[]{:S(2)}, u32[]{:S(2)}) collective-permute-start(bf16[96,1024]{1,0:T(8,128)(2,1)S(1)} %get-tuple-element.109.g0), channel_id=1, source_target_pairs={{0,6},{2,0},{4,2},{6,4},{1,7},{3,1},{5,3},{7,5},{8,14},{10,8},{12,... | collective-permute-start | bytes 589832 | tf_op jit(solution)/shard_map/ppermute | solution.py:434
  101.8 10.8 %collective-permute-start.17 = (bf16[96,1024]{1,0:T(8,128)(2,1)S(1)}, bf16[96,1024]{1,0:T(8,128)(2,1)S(1)}, u32[]{:S(2)}, u32[]{:S(2)}) collective-permute-start(bf16[96,1024]{1,0:T(8,128)(2,1)S(1)} %get-tuple-element.83.g0), channel_id=1, source_target_pairs={{0,2},{2,4},{4,6},{6,0},{1,3},{3,5},{5,7},{7,1},{8,10},{10,12},{12... | collective-permute-start | bytes 589832 | tf_op jit(solution)/shard_map/ppermute | solution.py:434
  102.9 9.6 %collective-permute-start.16 = (bf16[96,1024]{1,0:T(8,128)(2,1)S(1)}, bf16[96,1024]{1,0:T(8,128)(2,1)S(1)}, u32[]{:S(2)}, u32[]{:S(2)}) collective-permute-start(bf16[96,1024]{1,0:T(8,128)(2,1)S(1)} %get-tuple-element.83.g0), channel_id=1, source_target_pairs={{0,4},{2,6},{4,0},{6,2},{1,5},{3,7},{5,1},{7,3},{8,12},{10,14},{12... | collective-permute-start | bytes 589832 | tf_op jit(solution)/shard_map/ppermute | solution.py:434
  104.3 8.2 %collective-permute-start.15 = (bf16[96,1024]{1,0:T(8,128)(2,1)S(1)}, bf16[96,1024]{1,0:T(8,128)(2,1)S(1)}, u32[]{:S(2)}, u32[]{:S(2)}) collective-permute-start(bf16[96,1024]{1,0:T(8,128)(2,1)S(1)} %get-tuple-element.83.g0), channel_id=1, source_target_pairs={{0,6},{2,0},{4,2},{6,4},{1,7},{3,1},{5,3},{7,5},{8,14},{10,8},{12,... | collective-permute-start | bytes 589832 | tf_op jit(solution)/shard_map/ppermute | solution.py:434
  118.7 46.1 %all-to-all-start.1 = ((bf16[64,8,2688]{2,1,0:T(8,128)(2,1)}), bf16[64,8,2688]{2,1,0:T(8,128)(2,1)}, u32[]{:S(2)}, u32[]{:S(2)}) async-start(bf16[64,8,2688]{2,1,0:T(8,128)(2,1)} %bitcast.9), calls=%async_computation.1 | async-start | bytes 5505024 | tf_op jit(solution)/shard_map/all_to_all | solution.py:438
  129.1 4.3 %collective-permute-start.22 = (bf16[384,1024]{1,0:T(8,128)(2,1)S(1)}, bf16[384,1024]{1,0:T(8,128)(2,1)S(1)}, u32[]{:S(2)}, u32[]{:S(2)}) collective-permute-start(bf16[384,1024]{1,0:T(8,128)(2,1)S(1)} %get-tuple-element.94.bm_ref), channel_id=1, source_target_pairs={{0,1},{1,0},{2,3},{3,2},{4,5},{5,4},{6,7},{7,6},{8,9},{9,8},{10,11... | collective-permute-start | bytes 2359304 | tf_op jit(solution)/shard_map/ppermute | solution.py:431
  129.2 4.2 %collective-permute-start.21 = (bf16[384,896]{1,0:T(8,128)(2,1)S(1)}, bf16[384,896]{1,0:T(8,128)(2,1)S(1)}, u32[]{:S(2)}, u32[]{:S(2)}) collective-permute-start(bf16[384,896]{1,0:T(8,128)(2,1)S(1)} %get-tuple-element.93.other_ref), channel_id=1, source_target_pairs={{0,1},{1,0},{2,3},{3,2},{4,5},{5,4},{6,7},{7,6},{8,9},{9,8},{10,11... | collective-permute-start | bytes 2064392 | tf_op jit(solution)/shard_map/ppermute | solution.py:431
  129.7 8.6 %collective-permute-start.23 = (bf16[384,1024]{1,0:T(8,128)(2,1)S(1)}, bf16[384,1024]{1,0:T(8,128)(2,1)S(1)}, u32[]{:S(2)}, u32[]{:S(2)}) collective-permute-start(bf16[384,1024]{1,0:T(8,128)(2,1)S(1)} %get-tuple-element.95.bm_ref), channel_id=1, source_target_pairs={{0,1},{1,0},{2,3},{3,2},{4,5},{5,4},{6,7},{7,6},{8,9},{9,8},{10,11... | collective-permute-start | bytes 2359304 | tf_op jit(solution)/shard_map/ppermute | solution.py:431
  129.8 12.3 %collective-permute-start.24 = (bf16[384,1024]{1,0:T(8,128)(2,1)S(1)}, bf16[384,1024]{1,0:T(8,128)(2,1)S(1)}, u32[]{:S(2)}, u32[]{:S(2)}) collective-permute-start(bf16[384,1024]{1,0:T(8,128)(2,1)S(1)} %get-tuple-element.96.am_ref), channel_id=1, source_target_pairs={{0,1},{1,0},{2,3},{3,2},{4,5},{5,4},{6,7},{7,6},{8,9},{9,8},{10,11... | collective-permute-start | bytes 2359304 | tf_op jit(solution)/shard_map/ppermute | solution.py:431
  130.2 11.8 %collective-permute-start.25 = (bf16[384,896]{1,0:T(8,128)(2,1)}, bf16[384,896]{1,0:T(8,128)(2,1)S(1)}, u32[]{:S(2)}, u32[]{:S(2)}) collective-permute-start(bf16[384,896]{1,0:T(8,128)(2,1)} %copy-done.3), channel_id=1, source_target_pairs={{0,1},{1,0},{2,3},{3,2},{4,5},{5,4},{6,7},{7,6},{8,9},{9,8},{10,11... | collective-permute-start | bytes 2064392 | tf_op jit(solution)/shard_map/ppermute | solution.py:431
  133.5 1.1 copy-start.5
  138.3 3.8 %copy-start.7 = (bf16[384,896]{1,0:T(8,128)(2,1)S(1)}, bf16[384,896]{1,0:T(8,128)(2,1)}, u32[]{:S(2)}) copy-start(bf16[384,896]{1,0:T(8,128)(2,1)} %copy-done.6) | copy-start | bytes 2064388

commit v5 on v4

--- a/solution.py
+++ b/solution.py
@@ -289,7 +289,8 @@
     )(at, *parts, *weights)
 
 
-def grad_kernel(at_ref, g0, g1, g2, g3, main_ref, half_own_ref, half_other_ref, wo_ref, wx_ref, out_ref, keep_hbm, all_s, sem):
+def grad_kernel(at_ref, g0, g1, g2, g3, main_ref, half_own_ref, half_other_ref, wo_hbm, wx_hbm, out_ref, keep_hbm, all_s, w_s, sem, load_sems):
+    loads = start([(wx_hbm, w_s.at[0]), (wo_hbm, w_s.at[1])], load_sems)
     quarters, lanes, packed = out_ref.shape
     half = packed // 3
     slots = g0.shape[0]
@@ -298,8 +299,10 @@
     keep.start()
     masks = slot_masks(2 * slots, 2 * lanes, True)
     tail_masks = jnp.concatenate(masks[1:], axis=0)
-    other = (half_other_ref[...] + dot(all_s[...], wx_ref[...], 1, 1)).astype(BF16)
-    own = (half_own_ref[...] + dot(all_s[...], wo_ref[...], 1, 1)).astype(BF16)
+    loads[0].wait()
+    other = (half_other_ref[...] + dot(all_s[...], w_s[0], 1, 1)).astype(BF16)
+    loads[1].wait()
+    own = (half_own_ref[...] + dot(all_s[...], w_s[1], 1, 1)).astype(BF16)
     for p in range(quarters // 2):
         rows = slice(2 * p * slots, 2 * (p + 1) * slots)
         tails = dot(tail_masks, other[rows])
@@ -319,13 +322,18 @@
     slots, hidden = parts[0].shape
     return pl.pallas_call(
         grad_kernel,
-        in_specs=[smem()] + [whole()] * (quarters + 5),
+        in_specs=[smem()] + [whole()] * (quarters + 3) + [hbm()] * 2,
         out_specs=[whole(), hbm()],
         out_shape=[
             jax.ShapeDtypeStruct((quarters, lanes, width // 2 * 3), BF16),
             jax.ShapeDtypeStruct((quarters * slots, hidden), BF16),
         ],
-        scratch_shapes=[pltpu.VMEM((quarters * slots, hidden), BF16), pltpu.SemaphoreType.DMA],
+        scratch_shapes=[
+            pltpu.VMEM((quarters * slots, hidden), BF16),
+            pltpu.VMEM((2, *weights[0].shape), BF16),
+            pltpu.SemaphoreType.DMA,
+            pltpu.SemaphoreType.DMA((2,)),
+        ],
         compiler_params=pltpu.CompilerParams(vmem_limit_bytes=SMALL_LIMIT),
         cost_estimate=pl.CostEstimate(flops=2_500_000_000, bytes_accessed=14_000_000, transcendentals=0),
         name="grad_rows",

time: 172 us -> 172 us (level)
  no operation moved by 1% of the time
where the time goes in v5:
time: 172 us
  waiting for transfers between devices  71.1 us (41%)
  Pallas kernels  49 us (28%)
  starting transfers between devices  48.9 us (28%)
    all_to_all x2, waiting for transfers between devices, exchange(): return lax.all_to_all(flat, everyone, 0, 0, tiled=True).reshape(value.shape)  51.4 us
    ppermute x18, starting transfers between devices, along(): lax.ppermute(value, 'y', [(i, (i + shift) % quarters) for i in range(quar...  25.1 us
    all_to_all x2, starting transfers between devices, exchange(): return lax.all_to_all(flat, everyone, 0, 0, tiled=True).reshape(value.shape)  21.9 us
    ppermute x18, waiting for transfers between devices, along(): lax.ppermute(value, 'y', [(i, (i + shift) % quarters) for i in range(quar...  13 us
    pallas_call x3, Pallas kernels, weight_grad(): pl.pallas_call(weight_kernel, grid=(columns // step,), in_specs=[a_spec,...  11 us
    pallas_call x3, Pallas kernels, projection(): pl.pallas_call(kernel, in_specs=[smem()] + [whole()] * (len(rows) + len(w...  9.03 us
    ppermute x8, waiting for transfers between devices, to_partner(): return lax.ppermute(value, 'k', [(0, 1), (1, 0)])  6.67 us
    pallas_call x1, Pallas kernels, last(): pl.pallas_call(last_kernel, grid=(quarters,), in_specs=[smem(), whole(),...  6.53 us
  transfers between devices with their start and end apart: 28, of which 11 were waited for; matrix products, arithmetic and copies ran while one was open for 0% of the time, Pallas kernels for 18%

profile of v5, /device:TPU:0, one launch (start us, length us, event | category | flops | bytes accessed | tf_op | source)
XLA Modules:
  0.0 171.6 jit_solution(908511170482980499)
XLA Ops:
  0.6 5.5 %prep.1 = (bf16[4,128,2688]{2,1,0:T(8,128)(2,1)}, bf16[4,128,128]{2,1,0:T(8,128)(2,1)}, bf16[2,128,128]{2,1,0:T(8,128)(2,1)}) custom-call(s32[1]{0:T(128)} %bitcast.core_ref, s32[8,128]{1,0:T(8,128)} %bitcast.27, f32[8,128]{1,0:T(8,128)} %bitcast.26, bf16[128,7168]{1,0:T(8,128)(2,1)} %tok_ref.1, bf16[128,7168]{1,0:T(8,128)(2,1)} %go_ref.3), custom_call_target="tpu_custom_call" | custom-call | flops 800000000 | bytes 6500000 | tf_op jit(solution)/shard_map/prep/pallas_call | solution.py:98
  6.1 11.5 %all-to-all-start = ((bf16[64,8,2688]{2,1,0:T(8,128)(2,1)}), bf16[64,8,2688]{2,1,0:T(8,128)(2,1)S(1)}, u32[]{:S(2)}, u32[]{:S(2)}) async-start(bf16[64,8,2688]{2,1,0:T(8,128)(2,1)} %bitcast.25), calls=%async_computation | async-start | bytes 5505024 | tf_op jit(solution)/shard_map/all_to_all | solution.py:446
  17.7 0.5 collective-permute-start.8
  18.3 3.5 %collective-permute-done.wx_ref = bf16[896,1024]{1,0:T(8,128)(2,1)} collective-permute-done((bf16[896,1024]{1,0:T(8,128)(2,1)}, bf16[896,1024]{1,0:T(8,128)(2,1)}, u32[]{:S(2)}, u32[]{:S(2)}) %collective-permute-start) | collective-permute-done | bytes 1835040 | tf_op jit(solution)/shard_map/ppermute | solution.py:439
  21.8 32.2 %all-to-all-done = bf16[64,8,2688]{2,1,0:T(8,128)(2,1)S(1)} async-done(((bf16[64,8,2688]{2,1,0:T(8,128)(2,1)}), bf16[64,8,2688]{2,1,0:T(8,128)(2,1)S(1)}, u32[]{:S(2)}, u32[]{:S(2)}) %all-to-all-start) | async-done | bytes 2752544 | tf_op jit(solution)/shard_map/all_to_all | solution.py:446
  54.0 3.4 %unpack_x.1 = (bf16[384,896]{1,0:T(8,128)(2,1)S(1)}, bf16[384,896]{1,0:T(8,128)(2,1)S(1)}, f32[384,1024]{1,0:T(8,128)S(1)}, bf16[4,128,2688]{2,1,0:T(8,128)(2,1)S(1)}) custom-call(bf16[4,128,2688]{2,1,0:T(8,128)(2,1)S(1)} %bitcast.15, bf16[896,1024]{1,0:T(8,128)(2,1)} %collective-permute-done.wx_ref), custom_call_target="tpu_custom_call", output_to_operand_aliasing={{3}: (0, {})} | custom-call | flops 2000000000 | bytes 6000000 | tf_op jit(solution)/shard_map/unpack_x/pallas_call | solution.py:165
  57.4 1.2 gate.1
  58.6 0.9 collective-permute-start.5
  59.5 1.3 collective-permute-start.6
  60.8 1.9 %collective-permute-start.7 = (bf16[96,1024]{1,0:T(8,128)(2,1)S(1)}, bf16[96,1024]{1,0:T(8,128)(2,1)S(1)}, u32[]{:S(2)}, u32[]{:S(2)}) collective-permute-start(bf16[96,1024]{1,0:T(8,128)(2,1)S(1)} %get-tuple-element.69), channel_id=1, source_target_pairs={{0,6},{2,0},{4,2},{6,4},{1,7},{3,1},{5,3},{7,5},{8,14},{10,8},{12,... | collective-permute-start | bytes 589832 | tf_op jit(solution)/shard_map/ppermute | solution.py:442
  62.8 3.6 %up.1 = (f32[96,1024]{1,0:T(8,128)S(1)}, bf16[96,1024]{1,0:T(8,128)(2,1)S(1)}, bf16[96,1024]{1,0:T(8,128)(2,1)S(1)}, bf16[96,1024]{1,0:T(8,128)(2,1)S(1)}) custom-call(s32[1]{0:T(128)} %bitcast.3.at_ref, bf16[384,896]{1,0:T(8,128)(2,1)S(1)} %get-tuple-element.64.own_ref.am_ref, bf16[384,896]{1,0:T(8,128)(2,1)S(1)} %get-tuple-element.93.other_ref, ...), custom_call_target="tpu_custom_call" | custom-call | flops 3000000000 | bytes 8000000 | tf_op jit(solution)/shard_map/up/pallas_call | solution.py:215
  66.4 1.6 collective-permute-start.9
  67.9 3.2 %collective-permute-start.11 = (bf16[96,1024]{1,0:T(8,128)(2,1)S(1)}, bf16[96,1024]{1,0:T(8,128)(2,1)S(1)}, u32[]{:S(2)}, u32[]{:S(2)}) collective-permute-start(bf16[96,1024]{1,0:T(8,128)(2,1)S(1)} %get-tuple-element.74), channel_id=1, source_target_pairs={{0,6},{2,0},{4,2},{6,4},{1,7},{3,1},{5,3},{7,5},{8,14},{10,8},{12,... | collective-permute-start | bytes 589832 | tf_op jit(solution)/shard_map/ppermute | solution.py:442
  71.2 4.3 %back.1 = (f32[96,1024]{1,0:T(8,128)S(1)}, bf16[96,1024]{1,0:T(8,128)(2,1)S(1)}, bf16[96,1024]{1,0:T(8,128)(2,1)S(1)}, bf16[96,1024]{1,0:T(8,128)(2,1)S(1)}, bf1...) custom-call(s32[1]{0:T(128)} %bitcast.3.at_ref, bf16[4,128,2688]{2,1,0:T(8,128)(2,1)S(1)} %get-tuple-element.59.recv_ref, ...), custom_call_target="tpu_custom_call" | custom-call | flops 3000000000 | bytes 8000000 | tf_op jit(solution)/shard_map/back/pallas_call | solution.py:215
  75.5 0.9 collective-permute-start.2
  76.4 0.1 collective-permute-start.3
  76.6 3.1 %collective-permute-start.4 = (bf16[96,1024]{1,0:T(8,128)(2,1)S(1)}, bf16[96,1024]{1,0:T(8,128)(2,1)S(1)}, u32[]{:S(2)}, u32[]{:S(2)}) collective-permute-start(bf16[96,1024]{1,0:T(8,128)(2,1)S(1)} %get-tuple-element.63), channel_id=1, source_target_pairs={{0,6},{2,0},{4,2},{6,4},{1,7},{3,1},{5,3},{7,5},{8,14},{10,8},{12,... | collective-permute-start | bytes 589832 | tf_op jit(solution)/shard_map/ppermute | solution.py:442
  79.7 0.7 collective-permute-done.10
  80.4 0.3 multiply_convert_fusion.2
  80.7 1.7 %collective-permute-start.14 = (bf16[96,1024]{1,0:T(8,128)(2,1)S(1)}, bf16[96,1024]{1,0:T(8,128)(2,1)S(1)}, u32[]{:S(2)}, u32[]{:S(2)}) collective-permute-start(bf16[96,1024]{1,0:T(8,128)(2,1)S(1)} %get-tuple-element.78.h0), channel_id=1, source_target_pairs={{0,2},{2,4},{4,6},{6,0},{1,3},{3,5},{5,7},{7,1},{8,10},{10,12},{12... | collective-permute-start | bytes 589832 | tf_op jit(solution)/shard_map/ppermute | solution.py:442
  82.5 1.1 collective-permute-start.13
  83.5 1.4 collective-permute-done.2
  84.9 0.3 collective-permute-start.12
  85.2 3.4 %collective-permute-done.3 = bf16[96,1024]{1,0:T(8,128)(2,1)S(1)} collective-permute-done((bf16[96,1024]{1,0:T(8,128)(2,1)S(1)}, bf16[96,1024]{1,0:T(8,128)(2,1)S(1)}, u32[]{:S(2)}, u32[]{:S(2)}) %collective-permute-start.3) | collective-permute-done | bytes 196640 | tf_op jit(solution)/shard_map/ppermute | solution.py:442
  88.6 0.6 collective-permute-done.4
  89.2 0.1 convert_add_fusion.2
  89.3 2.5 %collective-permute-done.14.h3 = bf16[96,1024]{1,0:T(8,128)(2,1)S(1)} collective-permute-done((bf16[96,1024]{1,0:T(8,128)(2,1)S(1)}, bf16[96,1024]{1,0:T(8,128)(2,1)S(1)}, u32[]{:S(2)}, u32[]{:S(2)}) %collective-permute-start.14) | collective-permute-done | bytes 196640 | tf_op jit(solution)/shard_map/ppermute | solution.py:442
  91.8 2.2 %collective-permute-done.13.h2 = bf16[96,1024]{1,0:T(8,128)(2,1)S(1)} collective-permute-done((bf16[96,1024]{1,0:T(8,128)(2,1)S(1)}, bf16[96,1024]{1,0:T(8,128)(2,1)S(1)}, u32[]{:S(2)}, u32[]{:S(2)}) %collective-permute-start.13) | collective-permute-done | bytes 196640 | tf_op jit(solution)/shard_map/ppermute | solution.py:442
  94.0 0.5 collective-permute-start.20
  94.6 2.4 %collective-permute-start.19 = (bf16[96,1024]{1,0:T(8,128)(2,1)S(1)}, bf16[96,1024]{1,0:T(8,128)(2,1)S(1)}, u32[]{:S(2)}, u32[]{:S(2)}) collective-permute-start(bf16[96,1024]{1,0:T(8,128)(2,1)S(1)} %get-tuple-element.109.g0), channel_id=1, source_target_pairs={{0,4},{2,6},{4,0},{6,2},{1,5},{3,7},{5,1},{7,3},{8,12},{10,14},{12... | collective-permute-start | bytes 589832 | tf_op jit(solution)/shard_map/ppermute | solution.py:442
  97.0 0.9 collective-permute-start.18
  97.9 3.9 %out_rows.1 = (bf16[4,128,1792]{2,1,0:T(8,128)(2,1)S(1)}, bf16[384,1024]{1,0:T(8,128)(2,1)S(1)}) custom-call(s32[1]{0:T(128)} %bitcast.3.at_ref, bf16[96,1024]{1,0:T(8,128)(2,1)S(1)} %get-tuple-element.78.h0, bf16[96,1024]{1,0:T(8,128)(2,1)S(1)} %collective-permute-done.12.h1, bf16[96,1024]{1,0:T(8,128)(2,1)S(1)} %collective-permute-done.13.h2, ...), custom_call_target="tpu_custom_call" | custom-call | flops 2000000000 | bytes 7500000 | tf_op jit(solution)/shard_map/out_rows/pallas_call | solution.py:253
  101.8 1.2 collective-permute-start.17
  102.9 1.4 collective-permute-start.16
  104.3 2.5 %collective-permute-start.15 = (bf16[96,1024]{1,0:T(8,128)(2,1)S(1)}, bf16[96,1024]{1,0:T(8,128)(2,1)S(1)}, u32[]{:S(2)}, u32[]{:S(2)}) collective-permute-start(bf16[96,1024]{1,0:T(8,128)(2,1)S(1)} %get-tuple-element.83.g0), channel_id=1, source_target_pairs={{0,6},{2,0},{4,2},{6,4},{1,7},{3,1},{5,3},{7,5},{8,14},{10,8},{12,... | collective-permute-start | bytes 589832 | tf_op jit(solution)/shard_map/ppermute | solution.py:442
  106.9 3.4 %half_grad.1 = (f32[384,896]{1,0:T(8,128)S(1)}, f32[384,896]{1,0:T(8,128)S(1)}, bf16[384,1024]{1,0:T(8,128)(2,1)S(1)}) custom-call(s32[1]{0:T(128)} %bitcast.3.at_ref, bf16[96,1024]{1,0:T(8,128)(2,1)S(1)} %get-tuple-element.109.g0, bf16[96,1024]{1,0:T(8,128)(2,1)S(1)} %collective-permute-done.18.g1, bf16[96,1024]{1,0:T(8,128)(2,1)S(1)} %collective-permute-done.19.g2, ...), custom_call_target="tpu_custom_call" | custom-call | flops 1500000000 | bytes 8000000 | tf_op jit(solution)/shard_map/half_grad/pallas_call | solution.py:280
  110.3 2.2 %collective-permute-done.17.g3 = bf16[96,1024]{1,0:T(8,128)(2,1)S(1)} collective-permute-done((bf16[96,1024]{1,0:T(8,128)(2,1)S(1)}, bf16[96,1024]{1,0:T(8,128)(2,1)S(1)}, u32[]{:S(2)}, u32[]{:S(2)}) %collective-permute-start.17) | collective-permute-done | bytes 196640 | tf_op jit(solution)/shard_map/ppermute | solution.py:442
  112.5 6.2 %grad_rows.1 = (bf16[4,128,2688]{2,1,0:T(8,128)(2,1)}, bf16[384,1024]{1,0:T(8,128)(2,1)S(1)}) custom-call(s32[1]{0:T(128)} %bitcast.3.at_ref, bf16[96,1024]{1,0:T(8,128)(2,1)S(1)} %get-tuple-element.83.g0, bf16[96,1024]{1,0:T(8,128)(2,1)S(1)} %collective-permute-done.15.g1, bf16[96,1024]{1,0:T(8,128)(2,1)S(1)} %collective-permute-done.16.g2, ...), custom_call_target="tpu_custom_call" | custom-call | flops 2500000000 | bytes 14000000 | tf_op jit(solution)/shard_map/grad_rows/pallas_call | solution.py:323
  118.8 10.4 %all-to-all-start.1 = ((bf16[64,8,2688]{2,1,0:T(8,128)(2,1)}), bf16[64,8,2688]{2,1,0:T(8,128)(2,1)}, u32[]{:S(2)}, u32[]{:S(2)}) async-start(bf16[64,8,2688]{2,1,0:T(8,128)(2,1)} %bitcast.9), calls=%async_computation.1 | async-start | bytes 5505024 | tf_op jit(solution)/shard_map/all_to_all | solution.py:446
  129.3 0.5 collective-permute-start.21
  129.9 0.4 collective-permute-start.24
  130.4 3.1 %collective-permute-done.21.ap_ref = bf16[384,896]{1,0:T(8,128)(2,1)S(1)} collective-permute-done((bf16[384,896]{1,0:T(8,128)(2,1)S(1)}, bf16[384,896]{1,0:T(8,128)(2,1)S(1)}, u32[]{:S(2)}, u32[]{:S(2)}) %collective-permute-start.21) | collective-permute-done | bytes 688160 | tf_op jit(solution)/shard_map/ppermute | solution.py:439
  133.6 1.1 copy-done.5
  134.7 3.7 %weight_grad.3 = bf16[896,1024]{1,0:T(8,128)(2,1)} custom-call(bf16[384,896]{1,0:T(8,128)(2,1)S(1)} %copy-done.5, bf16[384,896]{1,0:T(8,128)(2,1)S(1)} %collective-permute-done.21.ap_ref, bf16[384,1024]{1,0:T(8,128)(2,1)S(1)} %get-tuple-element.94.bm_ref, bf16[384,1024]{1,0:T(8,128)(2,1)S(1)} %collective-permute-done.22.bp_ref), custom_call_target="tpu_custom_call" | custom-call | flops 1500000000 | bytes 5000000 | tf_op jit(solution)/shard_map/weight_grad/pallas_call | solution.py:352
  138.4 3.8 %weight_grad.4 = bf16[896,1024]{1,0:T(8,128)(2,1)} custom-call(bf16[384,896]{1,0:T(8,128)(2,1)S(1)} %copy-done.5, bf16[384,896]{1,0:T(8,128)(2,1)S(1)} %collective-permute-done.21.ap_ref, bf16[384,1024]{1,0:T(8,128)(2,1)S(1)} %get-tuple-element.95.bm_ref, bf16[384,1024]{1,0:T(8,128)(2,1)S(1)} %collective-permute-done.23.bp_ref), custom_call_target="tpu_custom_call" | custom-call | flops 1500000000 | bytes 5000000 | tf_op jit(solution)/shard_map/weight_grad/pallas_call | solution.py:352
  142.2 3.5 %weight_grad.5 = bf16[1024,896]{1,0:T(8,128)(2,1)} custom-call(bf16[384,1024]{1,0:T(8,128)(2,1)S(1)} %get-tuple-element.96.am_ref, bf16[384,1024]{1,0:T(8,128)(2,1)S(1)} %collective-permute-done.24.ap_ref, bf16[384,896]{1,0:T(8,128)(2,1)S(1)} %copy-done.7, bf16[384,896]{1,0:T(8,128)(2,1)S(1)} %collective-permute-done.25.bp_ref), custom_call_target="tpu_custom_call" | custom-call | flops 1500000000 | bytes 5000000 | tf_op jit(solution)/shard_map/weight_grad/pallas_call | solution.py:352
  145.7 19.2 %all-to-all-done.1 = bf16[64,8,2688]{2,1,0:T(8,128)(2,1)} async-done(((bf16[64,8,2688]{2,1,0:T(8,128)(2,1)}), bf16[64,8,2688]{2,1,0:T(8,128)(2,1)}, u32[]{:S(2)}, u32[]{:S(2)}) %all-to-all-start.1) | async-done | bytes 2752544 | tf_op jit(solution)/shard_map/all_to_all | solution.py:446
  164.9 6.5 %last.1 = (bf16[128,7168]{1,0:T(8,128)(2,1)}, bf16[128,7168]{1,0:T(8,128)(2,1)}, f32[8,128]{1,0:T(8,128)}) custom-call(s32[1]{0:T(128)} %bitcast.core_ref, s32[8,128]{1,0:T(8,128)} %bitcast.28, bf16[4,128,128]{2,1,0:T(8,128)(2,1)} %get-tuple-element.56.sel_ref, bf16[2,128,128]{2,1,0:T(8,128)(2,1)} %get-tuple-element.57.wsel_ref, ...), custom_call_target="tpu_custom_call" | custom-call | flops 1500000000 | bytes 8500000 | tf_op jit(solution)/shard_map/last/pallas_call | solution.py:410
  (39 shorter events, 0.6 us)
Async XLA Ops:
  6.1 47.9 %all-to-all-start = ((bf16[64,8,2688]{2,1,0:T(8,128)(2,1)}), bf16[64,8,2688]{2,1,0:T(8,128)(2,1)S(1)}, u32[]{:S(2)}, u32[]{:S(2)}) async-start(bf16[64,8,2688]{2,1,0:T(8,128)(2,1)} %bitcast.25), calls=%async_computation | async-start | bytes 5505024 | tf_op jit(solution)/shard_map/all_to_all | solution.py:446
  17.6 4.2 %collective-permute-start = (bf16[896,1024]{1,0:T(8,128)(2,1)}, bf16[896,1024]{1,0:T(8,128)(2,1)}, u32[]{:S(2)}, u32[]{:S(2)}) collective-permute-start(bf16[896,1024]{1,0:T(8,128)(2,1)} %bitcast.19), channel_id=1, source_target_pairs={{0,1},{1,0},{2,3},{3,2},{4,5},{5,4},{6,7},{7,6},{8,9},{9,8},{10,11... | collective-permute-start | bytes 5505032 | tf_op jit(solution)/shard_map/ppermute | solution.py:439
  17.7 45.1 %collective-permute-start.8 = (bf16[896,1024]{1,0:T(8,128)(2,1)}, bf16[896,1024]{1,0:T(8,128)(2,1)}, u32[]{:S(2)}, u32[]{:S(2)}) collective-permute-start(bf16[896,1024]{1,0:T(8,128)(2,1)} %bitcast.22), channel_id=1, source_target_pairs={{0,1},{1,0},{2,3},{3,2},{4,5},{5,4},{6,7},{7,6},{8,9},{9,8},{10,11... | collective-permute-start | bytes 5505032 | tf_op jit(solution)/shard_map/ppermute | solution.py:439
  18.2 49.7 %collective-permute-start.1 = (bf16[1024,896]{1,0:T(8,128)(2,1)}, bf16[1024,896]{1,0:T(8,128)(2,1)}, u32[]{:S(2)}, u32[]{:S(2)}) collective-permute-start(bf16[1024,896]{1,0:T(8,128)(2,1)} %bitcast.16), channel_id=1, source_target_pairs={{0,1},{1,0},{2,3},{3,2},{4,5},{5,4},{6,7},{7,6},{8,9},{9,8},{10,11... | collective-permute-start | bytes 5505032 | tf_op jit(solution)/shard_map/ppermute | solution.py:439
  54.0 3.4 %copy-start.1 = (bf16[1,896,1024]{2,1,0:T(8,128)(2,1)S(1)}, bf16[1,896,1024]{2,1,0:T(8,128)(2,1)}, u32[]{:S(2)}) copy-start(bf16[1,896,1024]{2,1,0:T(8,128)(2,1)} %param.10) | copy-start | bytes 5505028
  57.4 5.4 %copy-start.4 = (bf16[384,896]{1,0:T(8,128)(2,1)}, bf16[384,896]{1,0:T(8,128)(2,1)S(1)}, u32[]{:S(2)}) copy-start(bf16[384,896]{1,0:T(8,128)(2,1)S(1)} %get-tuple-element.64.own_ref.am_ref) | copy-start | bytes 2064388
  57.4 5.3 %copy-start.2 = (bf16[1,896,1024]{2,1,0:T(8,128)(2,1)S(1)}, bf16[1,896,1024]{2,1,0:T(8,128)(2,1)}, u32[]{:S(2)}) copy-start(bf16[1,896,1024]{2,1,0:T(8,128)(2,1)} %param.11) | copy-start | bytes 5505028
  58.6 9.3 %collective-permute-start.5 = (bf16[96,1024]{1,0:T(8,128)(2,1)S(1)}, bf16[96,1024]{1,0:T(8,128)(2,1)S(1)}, u32[]{:S(2)}, u32[]{:S(2)}) collective-permute-start(bf16[96,1024]{1,0:T(8,128)(2,1)S(1)} %get-tuple-element.67), channel_id=1, source_target_pairs={{0,4},{2,6},{4,0},{6,2},{1,5},{3,7},{5,1},{7,3},{8,12},{10,14},{12... | collective-permute-start | bytes 589832 | tf_op jit(solution)/shard_map/ppermute | solution.py:442
  59.5 16.0 %collective-permute-start.6 = (bf16[96,1024]{1,0:T(8,128)(2,1)S(1)}, bf16[96,1024]{1,0:T(8,128)(2,1)S(1)}, u32[]{:S(2)}, u32[]{:S(2)}) collective-permute-start(bf16[96,1024]{1,0:T(8,128)(2,1)S(1)} %get-tuple-element.68), channel_id=1, source_target_pairs={{0,2},{2,4},{4,6},{6,0},{1,3},{3,5},{5,7},{7,1},{8,10},{10,12},{12... | collective-permute-start | bytes 589832 | tf_op jit(solution)/shard_map/ppermute | solution.py:442
  60.8 15.6 %collective-permute-start.7 = (bf16[96,1024]{1,0:T(8,128)(2,1)S(1)}, bf16[96,1024]{1,0:T(8,128)(2,1)S(1)}, u32[]{:S(2)}, u32[]{:S(2)}) collective-permute-start(bf16[96,1024]{1,0:T(8,128)(2,1)S(1)} %get-tuple-element.69), channel_id=1, source_target_pairs={{0,6},{2,0},{4,2},{6,4},{1,7},{3,1},{5,3},{7,5},{8,14},{10,8},{12,... | collective-permute-start | bytes 589832 | tf_op jit(solution)/shard_map/ppermute | solution.py:442
  62.8 8.4 %copy-start = (bf16[1,1024,896]{2,1,0:T(8,128)(2,1)S(1)}, bf16[1,1024,896]{2,1,0:T(8,128)(2,1)}, u32[]{:S(2)}) copy-start(bf16[1,1024,896]{2,1,0:T(8,128)(2,1)} %param.12) | copy-start | bytes 5505028
  66.4 10.2 %collective-permute-start.9 = (bf16[96,1024]{1,0:T(8,128)(2,1)S(1)}, bf16[96,1024]{1,0:T(8,128)(2,1)S(1)}, u32[]{:S(2)}, u32[]{:S(2)}) collective-permute-start(bf16[96,1024]{1,0:T(8,128)(2,1)S(1)} %get-tuple-element.72), channel_id=1, source_target_pairs={{0,4},{2,6},{4,0},{6,2},{1,5},{3,7},{5,1},{7,3},{8,12},{10,14},{12... | collective-permute-start | bytes 589832 | tf_op jit(solution)/shard_map/ppermute | solution.py:442
  67.9 12.5 %collective-permute-start.10 = (bf16[96,1024]{1,0:T(8,128)(2,1)S(1)}, bf16[96,1024]{1,0:T(8,128)(2,1)S(1)}, u32[]{:S(2)}, u32[]{:S(2)}) collective-permute-start(bf16[96,1024]{1,0:T(8,128)(2,1)S(1)} %get-tuple-element.73), channel_id=1, source_target_pairs={{0,2},{2,4},{4,6},{6,0},{1,3},{3,5},{5,7},{7,1},{8,10},{10,12},{12... | collective-permute-start | bytes 589832 | tf_op jit(solution)/shard_map/ppermute | solution.py:442
  67.9 12.5 %collective-permute-start.11 = (bf16[96,1024]{1,0:T(8,128)(2,1)S(1)}, bf16[96,1024]{1,0:T(8,128)(2,1)S(1)}, u32[]{:S(2)}, u32[]{:S(2)}) collective-permute-start(bf16[96,1024]{1,0:T(8,128)(2,1)S(1)} %get-tuple-element.74), channel_id=1, source_target_pairs={{0,6},{2,0},{4,2},{6,4},{1,7},{3,1},{5,3},{7,5},{8,14},{10,8},{12,... | collective-permute-start | bytes 589832 | tf_op jit(solution)/shard_map/ppermute | solution.py:442
  75.5 13.8 %copy-start.6 = (bf16[384,896]{1,0:T(8,128)(2,1)}, bf16[384,896]{1,0:T(8,128)(2,1)S(1)}, u32[]{:S(2)}) copy-start(bf16[384,896]{1,0:T(8,128)(2,1)S(1)} %get-tuple-element.97.bm_ref) | copy-start | bytes 2064388
  75.5 21.5 %copy-start.3 = (bf16[384,896]{1,0:T(8,128)(2,1)}, bf16[384,896]{1,0:T(8,128)(2,1)S(1)}, u32[]{:S(2)}) copy-start(bf16[384,896]{1,0:T(8,128)(2,1)S(1)} %get-tuple-element.98) | copy-start | bytes 2064388
  75.5 9.4 %collective-permute-start.2 = (bf16[96,1024]{1,0:T(8,128)(2,1)S(1)}, bf16[96,1024]{1,0:T(8,128)(2,1)S(1)}, u32[]{:S(2)}, u32[]{:S(2)}) collective-permute-start(bf16[96,1024]{1,0:T(8,128)(2,1)S(1)} %get-tuple-element.61), channel_id=1, source_target_pairs={{0,4},{2,6},{4,0},{6,2},{1,5},{3,7},{5,1},{7,3},{8,12},{10,14},{12... | collective-permute-start | bytes 589832 | tf_op jit(solution)/shard_map/ppermute | solution.py:442
  76.4 12.2 %collective-permute-start.3 = (bf16[96,1024]{1,0:T(8,128)(2,1)S(1)}, bf16[96,1024]{1,0:T(8,128)(2,1)S(1)}, u32[]{:S(2)}, u32[]{:S(2)}) collective-permute-start(bf16[96,1024]{1,0:T(8,128)(2,1)S(1)} %get-tuple-element.62), channel_id=1, source_target_pairs={{0,2},{2,4},{4,6},{6,0},{1,3},{3,5},{5,7},{7,1},{8,10},{10,12},{12... | collective-permute-start | bytes 589832 | tf_op jit(solution)/shard_map/ppermute | solution.py:442
  76.6 12.6 %collective-permute-start.4 = (bf16[96,1024]{1,0:T(8,128)(2,1)S(1)}, bf16[96,1024]{1,0:T(8,128)(2,1)S(1)}, u32[]{:S(2)}, u32[]{:S(2)}) collective-permute-start(bf16[96,1024]{1,0:T(8,128)(2,1)S(1)} %get-tuple-element.63), channel_id=1, source_target_pairs={{0,6},{2,0},{4,2},{6,4},{1,7},{3,1},{5,3},{7,5},{8,14},{10,8},{12,... | collective-permute-start | bytes 589832 | tf_op jit(solution)/shard_map/ppermute | solution.py:442
  80.7 11.0 %collective-permute-start.14 = (bf16[96,1024]{1,0:T(8,128)(2,1)S(1)}, bf16[96,1024]{1,0:T(8,128)(2,1)S(1)}, u32[]{:S(2)}, u32[]{:S(2)}) collective-permute-start(bf16[96,1024]{1,0:T(8,128)(2,1)S(1)} %get-tuple-element.78.h0), channel_id=1, source_target_pairs={{0,2},{2,4},{4,6},{6,0},{1,3},{3,5},{5,7},{7,1},{8,10},{10,12},{12... | collective-permute-start | bytes 589832 | tf_op jit(solution)/shard_map/ppermute | solution.py:442
  82.5 11.5 %collective-permute-start.13 = (bf16[96,1024]{1,0:T(8,128)(2,1)S(1)}, bf16[96,1024]{1,0:T(8,128)(2,1)S(1)}, u32[]{:S(2)}, u32[]{:S(2)}) collective-permute-start(bf16[96,1024]{1,0:T(8,128)(2,1)S(1)} %get-tuple-element.78.h0), channel_id=1, source_target_pairs={{0,4},{2,6},{4,0},{6,2},{1,5},{3,7},{5,1},{7,3},{8,12},{10,14},{12... | collective-permute-start | bytes 589832 | tf_op jit(solution)/shard_map/ppermute | solution.py:442
  84.9 9.0 %collective-permute-start.12 = (bf16[96,1024]{1,0:T(8,128)(2,1)S(1)}, bf16[96,1024]{1,0:T(8,128)(2,1)S(1)}, u32[]{:S(2)}, u32[]{:S(2)}) collective-permute-start(bf16[96,1024]{1,0:T(8,128)(2,1)S(1)} %get-tuple-element.78.h0), channel_id=1, source_target_pairs={{0,6},{2,0},{4,2},{6,4},{1,7},{3,1},{5,3},{7,5},{8,14},{10,8},{12,... | collective-permute-start | bytes 589832 | tf_op jit(solution)/shard_map/ppermute | solution.py:442
  94.0 10.3 %collective-permute-start.20 = (bf16[96,1024]{1,0:T(8,128)(2,1)S(1)}, bf16[96,1024]{1,0:T(8,128)(2,1)S(1)}, u32[]{:S(2)}, u32[]{:S(2)}) collective-permute-start(bf16[96,1024]{1,0:T(8,128)(2,1)S(1)} %get-tuple-element.109.g0), channel_id=1, source_target_pairs={{0,2},{2,4},{4,6},{6,0},{1,3},{3,5},{5,7},{7,1},{8,10},{10,12},{12... | collective-permute-start | bytes 589832 | tf_op jit(solution)/shard_map/ppermute | solution.py:442
  94.6 12.3 %collective-permute-start.19 = (bf16[96,1024]{1,0:T(8,128)(2,1)S(1)}, bf16[96,1024]{1,0:T(8,128)(2,1)S(1)}, u32[]{:S(2)}, u32[]{:S(2)}) collective-permute-start(bf16[96,1024]{1,0:T(8,128)(2,1)S(1)} %get-tuple-element.109.g0), channel_id=1, source_target_pairs={{0,4},{2,6},{4,0},{6,2},{1,5},{3,7},{5,1},{7,3},{8,12},{10,14},{12... | collective-permute-start | bytes 589832 | tf_op jit(solution)/shard_map/ppermute | solution.py:442
  97.0 9.9 %collective-permute-start.18 = (bf16[96,1024]{1,0:T(8,128)(2,1)S(1)}, bf16[96,1024]{1,0:T(8,128)(2,1)S(1)}, u32[]{:S(2)}, u32[]{:S(2)}) collective-permute-start(bf16[96,1024]{1,0:T(8,128)(2,1)S(1)} %get-tuple-element.109.g0), channel_id=1, source_target_pairs={{0,6},{2,0},{4,2},{6,4},{1,7},{3,1},{5,3},{7,5},{8,14},{10,8},{12,... | collective-permute-start | bytes 589832 | tf_op jit(solution)/shard_map/ppermute | solution.py:442
  101.8 10.8 %collective-permute-start.17 = (bf16[96,1024]{1,0:T(8,128)(2,1)S(1)}, bf16[96,1024]{1,0:T(8,128)(2,1)S(1)}, u32[]{:S(2)}, u32[]{:S(2)}) collective-permute-start(bf16[96,1024]{1,0:T(8,128)(2,1)S(1)} %get-tuple-element.83.g0), channel_id=1, source_target_pairs={{0,2},{2,4},{4,6},{6,0},{1,3},{3,5},{5,7},{7,1},{8,10},{10,12},{12... | collective-permute-start | bytes 589832 | tf_op jit(solution)/shard_map/ppermute | solution.py:442
  102.9 9.6 %collective-permute-start.16 = (bf16[96,1024]{1,0:T(8,128)(2,1)S(1)}, bf16[96,1024]{1,0:T(8,128)(2,1)S(1)}, u32[]{:S(2)}, u32[]{:S(2)}) collective-permute-start(bf16[96,1024]{1,0:T(8,128)(2,1)S(1)} %get-tuple-element.83.g0), channel_id=1, source_target_pairs={{0,4},{2,6},{4,0},{6,2},{1,5},{3,7},{5,1},{7,3},{8,12},{10,14},{12... | collective-permute-start | bytes 589832 | tf_op jit(solution)/shard_map/ppermute | solution.py:442
  104.3 8.2 %collective-permute-start.15 = (bf16[96,1024]{1,0:T(8,128)(2,1)S(1)}, bf16[96,1024]{1,0:T(8,128)(2,1)S(1)}, u32[]{:S(2)}, u32[]{:S(2)}) collective-permute-start(bf16[96,1024]{1,0:T(8,128)(2,1)S(1)} %get-tuple-element.83.g0), channel_id=1, source_target_pairs={{0,6},{2,0},{4,2},{6,4},{1,7},{3,1},{5,3},{7,5},{8,14},{10,8},{12,... | collective-permute-start | bytes 589832 | tf_op jit(solution)/shard_map/ppermute | solution.py:442
  118.8 46.1 %all-to-all-start.1 = ((bf16[64,8,2688]{2,1,0:T(8,128)(2,1)}), bf16[64,8,2688]{2,1,0:T(8,128)(2,1)}, u32[]{:S(2)}, u32[]{:S(2)}) async-start(bf16[64,8,2688]{2,1,0:T(8,128)(2,1)} %bitcast.9), calls=%async_computation.1 | async-start | bytes 5505024 | tf_op jit(solution)/shard_map/all_to_all | solution.py:446
  129.2 4.3 %collective-permute-start.22 = (bf16[384,1024]{1,0:T(8,128)(2,1)S(1)}, bf16[384,1024]{1,0:T(8,128)(2,1)S(1)}, u32[]{:S(2)}, u32[]{:S(2)}) collective-permute-start(bf16[384,1024]{1,0:T(8,128)(2,1)S(1)} %get-tuple-element.94.bm_ref), channel_id=1, source_target_pairs={{0,1},{1,0},{2,3},{3,2},{4,5},{5,4},{6,7},{7,6},{8,9},{9,8},{10,11... | collective-permute-start | bytes 2359304 | tf_op jit(solution)/shard_map/ppermute | solution.py:439
  129.3 4.2 %collective-permute-start.21 = (bf16[384,896]{1,0:T(8,128)(2,1)S(1)}, bf16[384,896]{1,0:T(8,128)(2,1)S(1)}, u32[]{:S(2)}, u32[]{:S(2)}) collective-permute-start(bf16[384,896]{1,0:T(8,128)(2,1)S(1)} %get-tuple-element.93.other_ref), channel_id=1, source_target_pairs={{0,1},{1,0},{2,3},{3,2},{4,5},{5,4},{6,7},{7,6},{8,9},{9,8},{10,11... | collective-permute-start | bytes 2064392 | tf_op jit(solution)/shard_map/ppermute | solution.py:439
  129.8 8.6 %collective-permute-start.23 = (bf16[384,1024]{1,0:T(8,128)(2,1)S(1)}, bf16[384,1024]{1,0:T(8,128)(2,1)S(1)}, u32[]{:S(2)}, u32[]{:S(2)}) collective-permute-start(bf16[384,1024]{1,0:T(8,128)(2,1)S(1)} %get-tuple-element.95.bm_ref), channel_id=1, source_target_pairs={{0,1},{1,0},{2,3},{3,2},{4,5},{5,4},{6,7},{7,6},{8,9},{9,8},{10,11... | collective-permute-start | bytes 2359304 | tf_op jit(solution)/shard_map/ppermute | solution.py:439
  129.9 12.3 %collective-permute-start.24 = (bf16[384,1024]{1,0:T(8,128)(2,1)S(1)}, bf16[384,1024]{1,0:T(8,128)(2,1)S(1)}, u32[]{:S(2)}, u32[]{:S(2)}) collective-permute-start(bf16[384,1024]{1,0:T(8,128)(2,1)S(1)} %get-tuple-element.96.am_ref), channel_id=1, source_target_pairs={{0,1},{1,0},{2,3},{3,2},{4,5},{5,4},{6,7},{7,6},{8,9},{9,8},{10,11... | collective-permute-start | bytes 2359304 | tf_op jit(solution)/shard_map/ppermute | solution.py:439
  130.3 11.8 %collective-permute-start.25 = (bf16[384,896]{1,0:T(8,128)(2,1)}, bf16[384,896]{1,0:T(8,128)(2,1)S(1)}, u32[]{:S(2)}, u32[]{:S(2)}) collective-permute-start(bf16[384,896]{1,0:T(8,128)(2,1)} %copy-done.3), channel_id=1, source_target_pairs={{0,1},{1,0},{2,3},{3,2},{4,5},{5,4},{6,7},{7,6},{8,9},{9,8},{10,11... | collective-permute-start | bytes 2064392 | tf_op jit(solution)/shard_map/ppermute | solution.py:439
  133.6 1.1 copy-start.5
  138.4 3.8 %copy-start.7 = (bf16[384,896]{1,0:T(8,128)(2,1)S(1)}, bf16[384,896]{1,0:T(8,128)(2,1)}, u32[]{:S(2)}) copy-start(bf16[384,896]{1,0:T(8,128)(2,1)} %copy-done.6) | copy-start | bytes 2064388
